TPU v7x, 32 devices: a whole 2x2x4 slice. The times are simulated.
32 devices in a mesh: section: 2 (over core), fsdp: 2 (over x), tok: 8 (over z, y).
Axes of the slice: x: 2, y: 2, z: 4, core: 2. Of those that a mesh axis runs over, the one named last changes fastest.
Arguments:
- hidden: bfloat16 [4, 32, 3072], P(None, 'tok'), may hold values from -6 to 6
- lengths: int32 [4], replicated, may hold values from 1 to 32, 96 in all
- text_count: int32 [1], replicated, may hold values from 1 to 32
- timestep: int32 [1], replicated, may hold values from 0 to 49
- mod_table: bfloat16 [2, 50, 6, 3072], P('section'), may hold values from -3 to 3
- w_qkv: bfloat16 [2, 3072, 3, 1536], P('section', 'tok', None, 'fsdp'), may hold values from -0.109375 to 0.109375
- w_out: bfloat16 [2, 3072, 1536], P('section', 'tok', 'fsdp'), may hold values from -0.15625 to 0.15625
- qk_gain: float32 [2, 2, 64], P('section'), may hold values from 0.5 to 2
- stale_cache: bfloat16 [2, 2, 4, 32, 1536], P('section', None, None, None, 'fsdp'), may hold values from -6 to 6
Outputs:
- layer_out: bfloat16 [2, 4, 32, 3072], P('section', None, 'tok')
- new_cache: bfloat16 [2, 2, 4, 32, 1536], P('section', None, None, None, 'fsdp')
Inputs may be any that keep to these rules, and one draw needn't show every extreme that they name: The lengths sum to 96; one patch is full with exactly 32 live tokens.
All inputs are finite; a program needn't handle non-finite values.
Results may differ from a plain program's by a relative error of at most 0.012.
Values may be sent and summed in bfloat16 or wider, within the bound.
No kernel may reach another device: no remote copies, remote signals or barrier semaphores. Data moves between devices by JAX's collectives and lax.ppermute only.
A program may use at most 128 MiB of HBM per device.

v0:
```python
import jax
import jax.numpy as jnp
from jax import lax
from jax.sharding import PartitionSpec as P

HEAD_DIM = 64


def from_behind(block, axis, distance):
    devices = range(lax.axis_size(axis))
    route = [(i - distance, i) for i in devices if i - distance in devices]
    return lax.ppermute(block, axis, route)


def layer_norm(values, eps):
    mean = jnp.mean(values, axis=-1, keepdims=True)
    centred = values - mean
    spread = jnp.mean(centred * centred, axis=-1, keepdims=True)
    return centred * lax.rsqrt(spread + eps)


def modulate(inputs, positions, modulation, text_total):
    is_text = (positions < text_total)[:, None]
    shift = jnp.where(is_text, modulation[3], modulation[0])
    scale = jnp.where(is_text, modulation[4], modulation[1])
    gate = jnp.where(is_text, modulation[5], modulation[2])
    normed = layer_norm(inputs, 1e-05)
    return ((normed * (1.0 + scale) + shift).astype(jnp.bfloat16), gate)


def project_heads(mixed, gains):
    queries = (layer_norm(mixed[:, 0], 1e-06) * gains[0]).astype(jnp.bfloat16)
    keys_new = (layer_norm(mixed[:, 1], 1e-06) * gains[1]).astype(jnp.bfloat16)
    values_new = mixed[:, 2].astype(jnp.bfloat16)
    return (queries, keys_new, values_new)


def attend(queries, keys_all, values_all, key_live):
    scores = jnp.einsum(
        "qhd,khd->hqk", queries, keys_all, preferred_element_type=jnp.float32
    ) * HEAD_DIM ** (-0.5)
    scores = jnp.where(key_live[None, None, :], scores, -jnp.inf)
    top = jnp.max(scores, axis=-1, keepdims=True)
    expo = jnp.exp(scores - top)
    weights = (expo / jnp.sum(expo, axis=-1, keepdims=True)).astype(jnp.bfloat16)
    return jnp.einsum(
        "hqk,khd->qhd", weights, values_all, preferred_element_type=jnp.float32
    ).astype(jnp.bfloat16)


def local(hidden, lengths, text_count, timestep, mod_table, w_qkv, w_out, qk_gain, stale_cache):
    section_index = lax.axis_index("section")
    section_count = lax.axis_size("section")
    tok_index = lax.axis_index("tok")
    tok_count = lax.axis_size("tok")
    patches, cap_dev, width = hidden.shape
    cap_all = cap_dev * tok_count
    local_width = w_qkv.shape[3]
    heads_local = local_width // HEAD_DIM
    rows_local = jnp.arange(cap_dev, dtype=jnp.int32) + tok_index * cap_dev
    key_rows = jnp.arange(cap_all, dtype=jnp.int32)
    key_live = (key_rows[None, :] < lengths[:, None]).reshape(-1)
    offsets = jnp.cumsum(lengths) - lengths
    modulation = lax.dynamic_index_in_dim(mod_table[0], timestep[0], 0, keepdims=False).astype(
        jnp.float32
    )
    gains = qk_gain[0]
    shard_in = w_qkv[0].reshape(w_qkv.shape[1], 3 * local_width)
    out_local = w_out[0]
    weight_in, weight_out = (
        lax.all_gather(shard_in, "tok", axis=0, tiled=True),
        lax.all_gather(out_local, "tok", axis=0, tiled=True),
    )
    cache_keys = stale_cache[0, 0]
    cache_values = stale_cache[0, 1]
    out_states = jnp.zeros((patches, cap_dev, width), jnp.bfloat16)
    incoming = jnp.zeros((cap_dev, width), jnp.bfloat16)
    ticks = patches + section_count - 1
    for tick in range(ticks):
        patch = tick - section_index
        is_live = (patch >= 0) & (patch < patches)
        patch_slot = jnp.clip(patch, 0, patches - 1)
        own_states = hidden[min(tick, patches - 1)]
        inputs = jnp.where(section_index == 0, own_states, incoming).astype(jnp.float32)
        row_live = rows_local < lengths[patch_slot]
        modded, gate = modulate(inputs, offsets[patch_slot] + rows_local, modulation, text_count[0])
        mixed = jnp.dot(modded, weight_in, preferred_element_type=jnp.float32)
        mixed = mixed.reshape(cap_dev, 3, heads_local, HEAD_DIM)
        queries, keys_new, values_new = project_heads(mixed, gains)
        keys_new = jnp.where(row_live[:, None, None], keys_new, jnp.zeros_like(keys_new)).reshape(
            cap_dev, local_width
        )
        values_new = jnp.where(
            row_live[:, None, None], values_new, jnp.zeros_like(values_new)
        ).reshape(cap_dev, local_width)
        fresh_keys, fresh_values = (
            lax.all_gather(keys_new, "tok", axis=0, tiled=True),
            lax.all_gather(values_new, "tok", axis=0, tiled=True),
        )
        cache_keys = jnp.where(
            is_live,
            lax.dynamic_update_index_in_dim(cache_keys, fresh_keys, patch_slot, 0),
            cache_keys,
        )
        cache_values = jnp.where(
            is_live,
            lax.dynamic_update_index_in_dim(cache_values, fresh_values, patch_slot, 0),
            cache_values,
        )
        attended = attend(
            queries,
            cache_keys.reshape(-1, heads_local, HEAD_DIM),
            cache_values.reshape(-1, heads_local, HEAD_DIM),
            key_live,
        ).reshape(cap_dev, local_width)
        partial_out = lax.dot_general(
            attended, weight_out, (((1,), (1,)), ((), ())), preferred_element_type=jnp.float32
        )
        projected = lax.psum(partial_out.astype(jnp.bfloat16), "fsdp").astype(jnp.float32)
        result = jnp.where(row_live[:, None], inputs + gate * projected, 0.0).astype(jnp.bfloat16)
        out_states = jnp.where(
            is_live, lax.dynamic_update_index_in_dim(out_states, result, patch_slot, 0), out_states
        )
        if tick + 1 < ticks:
            incoming = from_behind(result, "section", 1)
    return (out_states[None], jnp.stack([cache_keys, cache_values])[None])


def solution(mesh):
    in_specs = (
        P(None, "tok", None),
        P(),
        P(),
        P(),
        P("section", None, None, None),
        P("section", "tok", None, "fsdp"),
        P("section", "tok", "fsdp"),
        P("section", None, None),
        P("section", None, None, None, "fsdp"),
    )
    out_specs = (P("section", None, "tok", None), P("section", None, None, None, "fsdp"))
    return jax.shard_map(local, mesh=mesh, in_specs=in_specs, out_specs=out_specs, check_vma=False)
```

profile of v0, /device:TPU:0, one launch (start us, length us, event | category | flops | bytes accessed | tf_op | source)
XLA Modules:
  0.0 660.5 jit_solution(15000618231810895690)
XLA Ops:
  7.3 3.9 copy.132
  20.3 189.7 %all-gather.14.cloned.1.call-done = bf16[3072,2304]{0,1:T(8,128)(2,1)} async-done(((bf16[384,2304]{0,1:T(8,128)(2,1)}), bf16[3072,2304]{0,1:T(8,128)(2,1)}) %all-gather.14.cloned.1.call-update) | async-done | bytes 14155792 | tf_op jit(solution)/shard_map/all_gather | solution.py:71
  210.0 8.8 %fusion.121 = f32[4,3,12,64]{3,0,2,1:T(4,128)S(1)} fusion(bf16[3,12,64,3072]{3,2,1,0:T(8,128)(2,1)} %bitcast.261, f32[3072]{0:T(1024)S(1)} %bitcast.266, f32[3072]{0:T(1024)S(1)} %bitcast.271, f32[3072]{0:T(1024)S(1)} %bitcast.276, f32[3072]{0:T(1024)S(1)} %bitcast.281, f32[4]{0:T(128)S(1)} %add_rsqrt_fusion.14, f32[4]{0:T(128)S(1)} %broadcast_multiply_fusion.14, ...), kind=kOutput, calls=%fused_computation.154 | convolution fusion | flops 56745984 | bytes 14267905 | tf_op jit(solution)/shard_map/dot_general | solution.py:87
  220.0 30.9 %all-gather.1 = bf16[8,4,768]{2,1,0:T(4,128)(2,1)S(1)} all-gather(bf16[1,4,768]{2,1,0:T(4,128)(2,1)S(1)} %get-tuple-element.70), channel_id=1, replica_groups=mesh['section'=2,'fsdp'=2,'tok'=8] {'tok'}, dimensions={0}, use_global_device_ids=true | all-gather | bytes 55296 | tf_op jit(solution)/shard_map/all_gather | solution.py:98
  250.9 31.1 %all-gather.2 = bf16[8,4,768]{2,1,0:T(4,128)(2,1)S(1)} all-gather(bf16[1,4,768]{2,1,0:T(4,128)(2,1)S(1)} %get-tuple-element.69), channel_id=1, replica_groups=mesh['section'=2,'fsdp'=2,'tok'=8] {'tok'}, dimensions={0}, use_global_device_ids=true | all-gather | bytes 55296 | tf_op jit(solution)/shard_map/all_gather | solution.py:97
  283.6 7.9 %all-gather.16.cloned.1.call-done = bf16[1,3072,768]{2,1,0:T(8,128)(2,1)} async-done(((bf16[1,384,768]{2,1,0:T(8,128)(2,1)}), bf16[1,3072,768]{2,1,0:T(8,128)(2,1)}) %all-gather.16.cloned.1.call-update) | async-done | bytes 4718608 | tf_op jit(solution)/shard_map/all_gather | solution.py:72
  291.5 3.6 fusion.15
  295.2 8.3 %psum.35 = bf16[4,3072]{1,0:T(4,128)(2,1)S(1)} all-reduce(bf16[4,3072]{1,0:T(4,128)(2,1)S(1)} %fusion.15), channel_id=1, replica_groups=mesh['section'=2,'fsdp'=2,'tok'=8] {'fsdp'}, use_global_device_ids=true, to_apply=%region_9.10 | all-reduce | flops 12288 | bytes 49152 | tf_op jit(solution)/shard_map/psum | solution.py:119
  303.6 1.3 collective-permute-start
  306.1 8.8 %fusion.110 = f32[4,2304]{1,0:T(4,128)S(1)} fusion(bf16[3072,2304]{0,1:T(8,128)(2,1)} %all-gather.14.cloned.1.call-done, bf16[4,3072]{1,0:T(4,128)(2,1)S(1)} %get-tuple-element.27, f32[3072]{0:T(1024)S(1)} %bitcast.267, f32[3072]{0:T(1024)S(1)} %bitcast.272, f32[3072]{0:T(1024)S(1)} %bitcast.277, f32[3072]{0:T(1024)S(1)} %bitcast.282, ...), kind=kOutput, calls=%fused_computation.147 | convolution fusion | flops 56733696 | bytes 14266404 | tf_op jit(solution)/shard_map/dot_general | solution.py:87
  316.1 30.7 %all-gather.4 = bf16[8,4,768]{2,1,0:T(4,128)(2,1)S(1)} all-gather(bf16[1,4,768]{2,1,0:T(4,128)(2,1)S(1)} %get-tuple-element.67), channel_id=1, replica_groups=mesh['section'=2,'fsdp'=2,'tok'=8] {'tok'}, dimensions={0}, use_global_device_ids=true | all-gather | bytes 55296 | tf_op jit(solution)/shard_map/all_gather | solution.py:97
  347.7 30.7 %all-gather.3 = bf16[8,4,768]{2,1,0:T(4,128)(2,1)S(1)} all-gather(bf16[1,4,768]{2,1,0:T(4,128)(2,1)S(1)} %get-tuple-element.68), channel_id=1, replica_groups=mesh['section'=2,'fsdp'=2,'tok'=8] {'tok'}, dimensions={0}, use_global_device_ids=true | all-gather | bytes 55296 | tf_op jit(solution)/shard_map/all_gather | solution.py:98
  379.1 3.7 fusion.18
  382.8 7.4 %psum.36 = bf16[4,3072]{1,0:T(4,128)(2,1)S(1)} all-reduce(bf16[4,3072]{1,0:T(4,128)(2,1)S(1)} %fusion.18), channel_id=1, replica_groups=mesh['section'=2,'fsdp'=2,'tok'=8] {'fsdp'}, use_global_device_ids=true, to_apply=%region_18.19 | all-reduce | flops 12288 | bytes 49152 | tf_op jit(solution)/shard_map/psum | solution.py:119
  390.3 1.5 collective-permute-start.1
  392.8 8.8 %fusion.112 = f32[4,2304]{1,0:T(4,128)S(1)} fusion(bf16[3072,2304]{0,1:T(8,128)(2,1)} %all-gather.14.cloned.1.call-done, bf16[4,3072]{1,0:T(4,128)(2,1)S(1)} %get-tuple-element.23, f32[4]{0:T(128)S(1)} %add_rsqrt_fusion.12, f32[4]{0:T(128)S(1)} %broadcast_multiply_fusion.12, f32[3072]{0:T(1024)S(1)} %bitcast.268, f32[3072]{0:T(1024)S(1)} %bitcast.273, ...), kind=kOutput, calls=%fused_computation.148 | convolution fusion | flops 56733696 | bytes 14266404 | tf_op jit(solution)/shard_map/dot_general | solution.py:87
  402.8 30.7 %all-gather.6 = bf16[8,4,768]{2,1,0:T(4,128)(2,1)S(1)} all-gather(bf16[1,4,768]{2,1,0:T(4,128)(2,1)S(1)} %get-tuple-element.65), channel_id=1, replica_groups=mesh['section'=2,'fsdp'=2,'tok'=8] {'tok'}, dimensions={0}, use_global_device_ids=true | all-gather | bytes 55296 | tf_op jit(solution)/shard_map/all_gather | solution.py:97
  434.4 30.7 %all-gather.5 = bf16[8,4,768]{2,1,0:T(4,128)(2,1)S(1)} all-gather(bf16[1,4,768]{2,1,0:T(4,128)(2,1)S(1)} %get-tuple-element.66), channel_id=1, replica_groups=mesh['section'=2,'fsdp'=2,'tok'=8] {'tok'}, dimensions={0}, use_global_device_ids=true | all-gather | bytes 55296 | tf_op jit(solution)/shard_map/all_gather | solution.py:98
  465.8 3.7 fusion.21
  469.5 8.3 %psum.37 = bf16[4,3072]{1,0:T(4,128)(2,1)S(1)} all-reduce(bf16[4,3072]{1,0:T(4,128)(2,1)S(1)} %fusion.21), channel_id=1, replica_groups=mesh['section'=2,'fsdp'=2,'tok'=8] {'fsdp'}, use_global_device_ids=true, to_apply=%region_27.28 | all-reduce | flops 12288 | bytes 49152 | tf_op jit(solution)/shard_map/psum | solution.py:119
  477.8 1.3 collective-permute-start.2
  480.3 8.8 %fusion.114 = f32[4,2304]{1,0:T(4,128)S(1)} fusion(bf16[3072,2304]{0,1:T(8,128)(2,1)} %all-gather.14.cloned.1.call-done, bf16[4,3072]{1,0:T(4,128)(2,1)S(1)} %get-tuple-element.19, f32[4]{0:T(128)S(1)} %add_rsqrt_fusion.11, f32[4]{0:T(128)S(1)} %broadcast_multiply_fusion.11, f32[3072]{0:T(1024)S(1)} %bitcast.269, f32[3072]{0:T(1024)S(1)} %bitcast.274, ...), kind=kOutput, calls=%fused_computation.149 | convolution fusion | flops 56733696 | bytes 14266404 | tf_op jit(solution)/shard_map/dot_general | solution.py:87
  490.4 30.7 %all-gather.8 = bf16[8,4,768]{2,1,0:T(4,128)(2,1)S(1)} all-gather(bf16[1,4,768]{2,1,0:T(4,128)(2,1)S(1)} %get-tuple-element.63), channel_id=1, replica_groups=mesh['section'=2,'fsdp'=2,'tok'=8] {'tok'}, dimensions={0}, use_global_device_ids=true | all-gather | bytes 55296 | tf_op jit(solution)/shard_map/all_gather | solution.py:97
  522.0 30.7 %all-gather.7 = bf16[8,4,768]{2,1,0:T(4,128)(2,1)S(1)} all-gather(bf16[1,4,768]{2,1,0:T(4,128)(2,1)S(1)} %get-tuple-element.64), channel_id=1, replica_groups=mesh['section'=2,'fsdp'=2,'tok'=8] {'tok'}, dimensions={0}, use_global_device_ids=true | all-gather | bytes 55296 | tf_op jit(solution)/shard_map/all_gather | solution.py:98
  553.4 3.7 fusion.24
  557.0 7.4 %psum.38 = bf16[4,3072]{1,0:T(4,128)(2,1)S(1)} all-reduce(bf16[4,3072]{1,0:T(4,128)(2,1)S(1)} %fusion.24), channel_id=1, replica_groups=mesh['section'=2,'fsdp'=2,'tok'=8] {'fsdp'}, use_global_device_ids=true, to_apply=%region_36.37 | all-reduce | flops 12288 | bytes 49152 | tf_op jit(solution)/shard_map/psum | solution.py:119
  564.5 1.5 collective-permute-start.3
  567.1 8.8 %fusion.116 = f32[4,2304]{1,0:T(4,128)S(1)} fusion(bf16[3072,2304]{0,1:T(8,128)(2,1)} %all-gather.14.cloned.1.call-done, bf16[4,3072]{1,0:T(4,128)(2,1)S(1)} %get-tuple-element.15, f32[4]{0:T(128)S(1)} %add_rsqrt_fusion.10, f32[4]{0:T(128)S(1)} %broadcast_multiply_fusion.10, f32[3072]{0:T(1024)S(1)} %bitcast.270, f32[3072]{0:T(1024)S(1)} %bitcast.275, ...), kind=kOutput, calls=%fused_computation.150 | convolution fusion | flops 56733696 | bytes 14266404 | tf_op jit(solution)/shard_map/dot_general | solution.py:87
  576.9 30.7 %all-gather.10 = bf16[8,4,768]{2,1,0:T(4,128)(2,1)S(1)} all-gather(bf16[1,4,768]{2,1,0:T(4,128)(2,1)S(1)} %get-tuple-element.51), channel_id=1, replica_groups=mesh['section'=2,'fsdp'=2,'tok'=8] {'tok'}, dimensions={0}, use_global_device_ids=true | all-gather | bytes 55296 | tf_op jit(solution)/shard_map/all_gather | solution.py:97
  607.6 30.7 %all-gather.9 = bf16[8,4,768]{2,1,0:T(4,128)(2,1)S(1)} all-gather(bf16[1,4,768]{2,1,0:T(4,128)(2,1)S(1)} %get-tuple-element.52), channel_id=1, replica_groups=mesh['section'=2,'fsdp'=2,'tok'=8] {'tok'}, dimensions={0}, use_global_device_ids=true | all-gather | bytes 55296 | tf_op jit(solution)/shard_map/all_gather | solution.py:98
  640.2 3.7 fusion.27
  643.8 8.3 %psum.39 = bf16[4,3072]{1,0:T(4,128)(2,1)S(1)} all-reduce(bf16[4,3072]{1,0:T(4,128)(2,1)S(1)} %fusion.27), channel_id=1, replica_groups=mesh['section'=2,'fsdp'=2,'tok'=8] {'fsdp'}, use_global_device_ids=true, to_apply=%region_45.46 | all-reduce | flops 12288 | bytes 49152 | tf_op jit(solution)/shard_map/psum | solution.py:119
  (209 shorter events, 28.4 us)
Async XLA Ops:
  7.2 4.8 copy-start.3
  7.2 6.3 copy-start.4
  7.2 11.7 %copy-start = (bf16[4,4,3072]{2,1,0:T(4,128)(2,1)S(1)}, bf16[4,4,3072]{2,1,0:T(4,128)(2,1)}, u32[]{:S(2)}) copy-start(bf16[4,4,3072]{2,1,0:T(4,128)(2,1)} %param.9) | copy-start | bytes 294916
  7.2 12.0 %copy-start.1 = (bf16[1,2,4,32,768]{4,3,2,1,0:T(8,128)(2,1)S(1)}, bf16[1,2,4,32,768]{4,3,2,1,0:T(8,128)(2,1)}, u32[]{:S(2)}) copy-start(bf16[1,2,4,32,768]{4,3,2,1,0:T(8,128)(2,1)} %param.17) | copy-start | bytes 1179652
  7.2 202.8 %all-gather.14.cloned.1.call-start = ((), (), s32[]{:S(2)}) async-start(), calls=%async_computation | async-start | bytes 15925248 | tf_op jit(solution)/shard_map/all_gather | solution.py:71
  11.2 280.3 %all-gather.16.cloned.1.call-start = ((), (), s32[]{:S(2)}) async-start(), calls=%async_computation.1 | async-start | bytes 5308416 | tf_op jit(solution)/shard_map/all_gather | solution.py:72
  303.6 2.1 collective-permute-start
  390.3 2.1 collective-permute-start.1
  477.8 2.1 collective-permute-start.2
  564.5 2.2 collective-permute-start.3
  653.0 0.6 copy-start.2
Sparse Core Ops, SparseCore 0:
  11.3 198.6 all-gather.13
  212.2 79.2 all-gather.15
where the time goes:
time: 661 us; the launch traced here: 660 us
  blocking collectives  347 us (52%)
  waiting for transfers between devices  199 us (30%)
  matrix products  65.3 us (10%)
  between operations  16 us (2%)
  other arithmetic  14.2 us (2%)
  local copies, waits for them, and re-layouts  13.6 us (2%)
    all_gather x1, waiting for transfers between devices, local(): lax.all_gather(shard_in, 'tok', axis=0, tiled=True)  190 us
    all_gather x5, blocking collectives, local(): lax.all_gather(keys_new, 'tok', axis=0, tiled=True)  154 us
    all_gather x5, blocking collectives, local(): lax.all_gather(values_new, 'tok', axis=0, tiled=True)  154 us
    dot_general x5, matrix products, local(): mixed = jnp.dot(modded, weight_in, preferred_element_type=jnp.float32)  43.9 us
    psum x5, blocking collectives, local(): lax.psum(partial_out.astype(jnp.bfloat16), 'fsdp').astype(jnp.float32)  39.6 us
    dot_general x5, matrix products, local(): lax.dot_general(attended, weight_out, (((1,), (1,)), ((), ())), preferred...  18.3 us
  transfers between devices with their start and end apart: 6, of which 4 were waited for; matrix products, arithmetic and copies ran while one was open for 3% of the time, Pallas kernels for 0%

commit v1 on v0

v1 whole, which is shorter than its diff:
```python
import collections
import functools
import math

import jax
import jax.numpy as jnp
from jax import lax
from jax.experimental import pallas as pl
from jax.experimental.pallas import tpu as pltpu
from jax.sharding import PartitionSpec as P

HEAD_DIM = 64
F32 = jnp.float32
BF16 = jnp.bfloat16
MOST_PEERS = 8


def swap(block, axis):
    size = lax.axis_size(axis)
    return lax.ppermute(block, axis, [(i, size - 1 - i) for i in range(size)])


def exchange(blocks):
    return lax.all_to_all(blocks, "tok", 0, 0, tiled=False)


def gather(block):
    count = lax.axis_size("tok")
    return exchange(jnp.broadcast_to(block[None], (count,) + block.shape))


def layer_norm(values, eps):
    mean = jnp.mean(values, axis=-1, keepdims=True)
    centred = values - mean
    spread = jnp.mean(centred * centred, axis=-1, keepdims=True)
    return centred * lax.rsqrt(spread + eps)


def three_terms(values):
    high = lax.reduce_precision(values, 8, 7)
    rest = values - high
    middle = lax.reduce_precision(rest, 8, 7)
    return jnp.concatenate([high, middle, rest - middle], axis=-1).astype(BF16)


def from_three(terms):
    terms = terms.astype(F32)
    count = terms.shape[-1] // 3
    return terms[..., :count] + terms[..., count : 2 * count] + terms[..., 2 * count :]


def by_all_to_all(hidden, lengths, text_count, timestep, mod_table, w_qkv, w_out, qk_gain, stale_cache):
    first = lax.axis_index("section") == 0
    own_half = lax.axis_index("section")
    tok_count = lax.axis_size("tok")
    tok_index = lax.axis_index("tok")
    patches, cap_dev, width = hidden.shape
    rows = patches * cap_dev
    total = rows * tok_count
    depth = w_qkv.shape[1]
    half = w_qkv.shape[3] // 2
    heads = half // HEAD_DIM

    def both_layers(own, other):
        return jnp.where(first, own, other), jnp.where(first, other, own)

    def halves(array):
        axis = array.ndim - 1
        keep = lax.dynamic_slice_in_dim(array, own_half * half, half, axis)
        send = lax.dynamic_slice_in_dim(array, (1 - own_half) * half, half, axis)
        return both_layers(keep, swap(send, "section"))

    offsets = jnp.cumsum(lengths) - lengths
    row = jnp.arange(total, dtype=jnp.int32)
    row_patch = (row // cap_dev) % patches
    row_slot = (row // rows) * cap_dev + row % cap_dev
    row_live = row_slot < lengths[row_patch]
    is_text = ((offsets[row_patch] + row_slot) < text_count[0])[:, None]
    own_patch = jnp.arange(rows, dtype=jnp.int32) // cap_dev
    own_live = (tok_index * cap_dev + jnp.arange(rows, dtype=jnp.int32) % cap_dev) < lengths[own_patch]
    cap_all = cap_dev * tok_count
    stale_patch = jnp.arange(patches * cap_all, dtype=jnp.int32) // cap_all
    stale_live = (jnp.arange(patches * cap_all, dtype=jnp.int32) % cap_all) < lengths[stale_patch]
    fresh_seen = row_live[None, :] & (row_patch[None, :] <= own_patch[:, None])
    stale_seen = stale_live[None, :] & (stale_patch[None, :] > own_patch[:, None])
    seen = jnp.concatenate([fresh_seen, stale_seen], axis=1)

    states = hidden.reshape(rows, width).astype(F32)
    mean = jnp.mean(states, axis=-1, keepdims=True)
    centred = states - mean
    inverse = lax.rsqrt(jnp.mean(centred * centred, axis=-1, keepdims=True) + 1e-05)
    stats = three_terms(jnp.concatenate([mean, inverse], axis=-1))
    stats = jnp.pad(stats, ((0, 0), (0, 128 - stats.shape[1])))
    blocks = hidden.reshape(rows, tok_count, depth).transpose(1, 0, 2)
    blocks = jnp.concatenate(
        [blocks, jnp.broadcast_to(stats[None], (tok_count,) + stats.shape)], axis=-1
    )
    arrived = exchange(blocks).reshape(total, depth + 128)
    slices = arrived[:, :depth].astype(F32)
    stats = from_three(arrived[:, depth : depth + 6])

    weight_in = halves(w_qkv[0].transpose(1, 0, 2))
    weight_out = halves(w_out[0])
    stale = halves(stale_cache[0].reshape(2, patches * cap_all, 2 * half))
    modulation = lax.dynamic_index_in_dim(mod_table[0], timestep[0], 0, keepdims=False)
    modulation = lax.dynamic_slice_in_dim(modulation, tok_index * depth, depth, 1)
    modulation = both_layers(modulation, swap(modulation, "section"))
    gains = both_layers(qk_gain[0], swap(qk_gain[0], "section"))

    outputs, caches = [], []
    for layer in range(2):
        if layer:
            part_mean = jnp.mean(slices, axis=-1, keepdims=True)
            off = slices - part_mean
            part = jnp.concatenate([part_mean, jnp.sum(off * off, axis=-1, keepdims=True)], axis=-1)
            parts = gather(part)
            mean = jnp.mean(parts[..., 0], axis=0)
            apart = parts[..., 0] - mean[None]
            spread = jnp.sum(parts[..., 1] + depth * apart * apart, axis=0) / (depth * tok_count)
            stats = jnp.stack([mean, lax.rsqrt(spread + 1e-05)], axis=-1)
        mod = modulation[layer].astype(F32)
        shift = jnp.where(is_text, mod[3], mod[0])
        scale = jnp.where(is_text, mod[4], mod[1])
        gate = jnp.where(is_text, mod[5], mod[2])
        normed = (slices - stats[:, :1]) * stats[:, 1:]
        modded = (normed * (1.0 + scale) + shift).astype(BF16)
        partial = jnp.concatenate(
            [
                jnp.dot(modded, weight_in[layer][i], preferred_element_type=F32).astype(BF16)
                for i in range(3)
            ],
            axis=-1,
        ).reshape(tok_count, rows, 3 * half)
        mixed = jnp.sum(exchange(partial).astype(F32), axis=0).reshape(rows, 3, heads, HEAD_DIM)
        gain = gains[layer]
        queries = (layer_norm(mixed[:, 0], 1e-06) * gain[0]).astype(BF16)
        keys_new = (layer_norm(mixed[:, 1], 1e-06) * gain[1]).astype(BF16)
        fresh = jnp.stack([keys_new, mixed[:, 2].astype(BF16)])
        fresh = jnp.where(own_live[None, :, None, None], fresh, jnp.zeros_like(fresh))
        fresh = gather(fresh.reshape(2, rows, half))
        caches.append(fresh)
        fresh = fresh.transpose(1, 0, 2, 3).reshape(2, total, half)
        keys_values = jnp.concatenate([fresh, stale[layer]], axis=1).reshape(
            2, total + patches * cap_all, heads, HEAD_DIM
        )
        scores = (
            jnp.einsum("qhd,khd->hqk", queries, keys_values[0], preferred_element_type=F32)
            * HEAD_DIM ** (-0.5)
        )
        scores = jnp.where(seen[None], scores, -jnp.inf)
        expo = jnp.exp(scores - jnp.max(scores, axis=-1, keepdims=True))
        weights = (expo / jnp.sum(expo, axis=-1, keepdims=True)).astype(BF16)
        attended = jnp.einsum("hqk,khd->qhd", weights, keys_values[1], preferred_element_type=F32)
        attended = gather(attended.astype(BF16).reshape(rows, half)).reshape(total, half)
        projected = lax.dot_general(
            attended, weight_out[layer], (((1,), (1,)), ((), ())), preferred_element_type=F32
        ).astype(BF16)
        projected = projected.astype(F32) + swap(projected, "section").astype(F32)
        projected = projected.astype(BF16)
        projected = projected.astype(F32) + swap(projected, "fsdp").astype(F32)
        result = jnp.where(row_live[:, None], slices + gate * projected, 0.0).astype(BF16)
        outputs.append(result)
        slices = result.astype(F32)

    final = jnp.where(first, outputs[0], outputs[1]).reshape(tok_count, rows, depth)
    final = exchange(final).transpose(1, 0, 2).reshape(1, patches, cap_dev, width)
    mine = jnp.where(first, caches[0], caches[1])
    theirs = swap(jnp.where(first, caches[1], caches[0]), "section")
    cache = jnp.concatenate(
        [jnp.where(first, mine, theirs), jnp.where(first, theirs, mine)], axis=-1
    ).reshape(tok_count, 2, patches, cap_dev, 2 * half)
    cache = cache.transpose(1, 2, 0, 3, 4).reshape(1, 2, patches, cap_all, 2 * half)
    return final, cache


def iota(shape, dim):
    return lax.broadcasted_iota(jnp.int32, shape, dim)


def total_of(parts):
    total = parts[0]
    for part in parts[1:]:
        total = total + part
    return total


def split_three(value):
    high = value.astype(BF16).astype(F32)
    middle = (value - high).astype(BF16).astype(F32)
    return [high, middle, value - high - middle]


def in_lanes(columns, lanes):
    rows = columns[0].shape[0]
    lane = iota((rows, lanes), 1)
    block = jnp.zeros((rows, lanes), F32)
    for i, column in enumerate(columns):
        block = jnp.where(lane == i, column, block)
    return block.astype(BF16)


def from_columns(block, at):
    return [
        sum(block[:, at + i : at + i + 1] for i in range(3 * j, 3 * j + 3)) for j in range(2)
    ]


def bounds(sizes, patches):
    ends = [sizes[0]]
    for p in range(1, patches):
        ends.append(ends[-1] + sizes[p])
    return ends


def positions(sizes, patch, slot, patches):
    ends = bounds(sizes, patches)
    position = jnp.full(slot.shape, -1, jnp.int32)
    for p in range(patches):
        own = (patch == p) & (slot < sizes[p])
        position = jnp.where(own, slot + (ends[p] - sizes[p]), position)
    return position


def slots_by_device(shape, dim, cap_dev, patches):
    index = iota(shape, dim)
    rows = cap_dev * patches
    return (index // cap_dev) % patches, (index // rows) * cap_dev + index % cap_dev


def slots_by_patch(shape, dim, cap_all):
    index = iota(shape, dim)
    return index // cap_all, index % cap_all


def begin(source, target, sem):
    copy = pltpu.make_async_copy(source, target, sem)
    copy.start()
    return copy


def finish(copies):
    for copy in copies:
        copy.wait()


def send_rows(dims, hidden, out, staged, sems):
    rows = dims.patches * dims.cap_dev
    given = hidden[...].astype(F32).reshape(rows, hidden.shape[2])
    mean = jnp.mean(given, axis=-1, keepdims=True)
    centred = given - mean
    inverse = lax.rsqrt(jnp.mean(centred * centred, axis=-1, keepdims=True) + 1e-05)
    stats = in_lanes(split_three(mean) + split_three(inverse), 128)
    given = given.astype(BF16)
    copies = []
    for i in range(dims.count):
        staged[i, :, : dims.depth] = given[:, i * dims.depth : (i + 1) * dims.depth]
        staged[i, :, dims.depth :] = stats
        copies.append(begin(staged.at[i], out.at[i], sems.at[i]))
    finish(copies)


def modulation_rows(dims, mod, sizes):
    is_text = iota((dims.live, 1), 0) < sizes[dims.patches]
    mod = mod[...].astype(F32)
    return [
        jnp.where(is_text, mod[i + 3 : i + 4, :], mod[i : i + 1, :]) for i in range(3)
    ]


def put_partials(dims, out, staged, sems, query, key, value, extra, stats):
    live, width, groups, turns = dims.live, dims.group_width, dims.groups, dims.turns
    share = live // turns
    fold = share // 2
    sides = query.shape[1] // (groups * width)
    copies = []
    for g in range(sides * groups):
        cut = slice(g * width, (g + 1) * width)
        pair = jnp.concatenate([key[:live, cut], value[:live, cut]], axis=1).astype(BF16)
        if extra:
            last = query[live : live + 4, cut]
            rest = [
                jnp.concatenate([key[live : live + 4, cut], value[live : live + 4, cut]], axis=1),
                jnp.concatenate([last, jnp.zeros_like(last)], axis=1),
            ]
        else:
            rest = []
        for h in range(turns):
            part = query[h * share : (h + 1) * share, cut]
            rows = [jnp.concatenate([part[:fold], part[fold:]], axis=1)] + rest
            at = (h * groups + g % groups) * sides + g // groups
            staged[at, :live, :] = pair
            rows = jnp.concatenate(rows, axis=0)
            staged[at, live : live + rows.shape[0], :] = rows.astype(BF16)
            if extra:
                staged[at, live + fold + 8 :, :] = stats
            copies.append(begin(staged.at[at], out.at[at], sems.at[at]))
    finish(copies)


def own_then_other(dims, wide):
    second = lax.axis_index("tok") % dims.pairs == 1
    left, right = wide[:, : dims.depth], wide[:, dims.depth :]
    return jnp.where(second, right, left), jnp.where(second, left, right)


def load(dims, side, weights, out, sems):
    columns = out.shape[2]
    start = pl.multiple_of(lax.axis_index("tok") % dims.pairs * columns, 128) if side else 0
    finish(
        [
            begin(weights.at[i, :, pl.ds(start, columns)], out.at[i], sems.at[i])
            for i in range(out.shape[0])
        ]
    )


def first_partials(
    dims, sizes, mod, weights, arrived, kept_states, out, staged, sems
):
    patch, slot = slots_by_device((1, dims.total), 1, dims.cap_dev, dims.patches)
    position = positions(sizes, patch, slot, dims.patches)
    pick = (iota((dims.live, dims.total), 0) == position).astype(F32).astype(BF16)
    rows = arrived[...].reshape(dims.total, dims.depth + 128)
    states = jnp.dot(pick, rows, preferred_element_type=F32)
    mean, inverse = from_columns(states, dims.depth)
    states = states[:, : dims.depth]
    own_mod = own_then_other(dims, mod[...].astype(F32))[0]
    shift, scale, gate = modulation_rows(dims, own_mod, sizes)
    modded = ((states - mean) * inverse * (1.0 + scale) + shift).astype(BF16)
    kept_states[...] = states.astype(BF16)
    mixed = [jnp.dot(modded, weights[i], preferred_element_type=F32) for i in range(3)]
    put_partials(dims, out, staged, sems, *mixed, False, None)


def head_means(values, blocks, terms):
    total = None
    for _ in range(terms):
        term = values.astype(BF16)
        part = jnp.dot(term, blocks, preferred_element_type=F32)
        total = part if total is None else total + part
        values = values - term.astype(F32)
    return total * (1.0 / HEAD_DIM)


def head_norm(values, gain, blocks):
    centred = values - head_means(values, blocks, 3)
    spread = head_means(centred * centred, blocks, 2)
    return (centred * lax.rsqrt(spread + 1e-06) * gain).astype(BF16)


def own_share(dims, turn, value, share):
    part = value[:share]
    for h in range(1, dims.turns):
        part = jnp.where(turn == h, value[h * share : (h + 1) * share], part)
    return part


def attention(
    dims, layer, sizes, gains, stale, arrived, attended, cache, block, fresh_rows, sems
):
    count = arrived.shape[0]
    turn = lax.axis_index("tok") // dims.pairs // dims.groups
    live, width = dims.live, dims.group_width
    share = live // dims.turns
    fold = share // 2
    pairs = total_of([arrived[i, :live, :].astype(F32) for i in range(count)])
    height = fold + 8 if layer else fold
    folded = [arrived[i, live : live + height, :].astype(F32) for i in range(count)]
    extras = [part[fold:] for part in folded]
    folded = total_of(folded)
    queries = jnp.concatenate([folded[:fold, :width], folded[:fold, width:]], axis=0)
    if layer:
        is_text = iota((live, 1), 0) < sizes[dims.patches]
        eye = (iota((live, live), 0) == iota((live, live), 1)).astype(F32).astype(BF16)
        means, spreads = [], []
        stats = jnp.concatenate(
            [arrived[i, live + fold + 8 :, :live].astype(F32) for i in range(count)], axis=0
        )
        columns = lax.dot_general(
            eye, stats.astype(BF16), (((1,), (1,)), ((), ())), preferred_element_type=F32
        )
        for i in range(count):
            mean, spread = from_columns(columns, 8 * i)
            means.append(mean)
            spreads.append(spread)
        mean = total_of(means) * (1.0 / count)
        apart = [part - mean for part in means]
        spread = total_of(spreads) + dims.count // count * dims.depth * total_of([part * part for part in apart])
        inverse = lax.rsqrt(spread * (1.0 / (dims.count * dims.depth)) + 1e-05)
        pairs = pairs + total_of(
            [a * jnp.where(is_text, e[0:1], e[1:2]) for a, e in zip(apart, extras)]
        )
        total = total_of(extras)
        pairs = pairs * inverse + jnp.where(is_text, total[2:3], total[3:4])
        mine = functools.partial(own_share, dims, turn, share=share)
        text_mine = (iota((share, 1), 0) + turn * share) < sizes[dims.patches]
        queries = queries + total_of(
            [
                mine(a) * jnp.where(text_mine, e[4:5, :width], e[5:6, :width])
                for a, e in zip(apart, extras)
            ]
        )
        queries = queries * mine(inverse) + jnp.where(text_mine, total[6:7, :width], total[7:8, :width])
    ends = bounds(sizes, dims.patches)
    query_at = iota((share, 1), 0) + turn * share
    query_patch = jnp.zeros((share, 1), jnp.int32)
    for end in ends[:-1]:
        query_patch = query_patch + (query_at >= end).astype(jnp.int32)
    query_end = jnp.zeros((share, 1), jnp.int32)
    for p, end in enumerate(ends):
        query_end = jnp.where(query_patch == p, end, query_end)
    stale_patch, stale_slot = slots_by_patch((1, dims.total), 1, dims.cap_all)
    stale_live = positions(sizes, stale_patch, stale_slot, dims.patches) >= 0
    fresh_seen = iota((share, live), 1) < query_end
    stale_seen = stale_live & (stale_patch > query_patch)
    heads = width // HEAD_DIM
    contract = (((1,), (1,)), ((), ()))
    same = iota((width, width), 0) // HEAD_DIM == iota((width, width), 1) // HEAD_DIM
    blocks = same.astype(F32).astype(BF16)
    gain = [jnp.concatenate([gains[i : i + 1, :]] * heads, axis=1) for i in range(2)]
    query = head_norm(queries, gain[0], blocks).astype(F32)
    key = head_norm(pairs[:, :width], gain[1], blocks)
    value = pairs[:, width:].astype(BF16)
    lanes = iota((heads * share, width), 1) // HEAD_DIM == iota((heads * share, width), 0) // share
    stacked = jnp.where(lanes, jnp.concatenate([query] * heads, axis=0), 0.0).astype(BF16)
    fresh = lax.dot_general(stacked, key, contract, preferred_element_type=F32)
    old = lax.dot_general(stacked, stale[0], contract, preferred_element_type=F32)
    repeated = lambda seen: jnp.concatenate([seen.astype(jnp.int32)] * heads, axis=0) > 0
    fresh = jnp.where(repeated(fresh_seen), fresh * HEAD_DIM ** (-0.5), -jnp.inf)
    old = jnp.where(repeated(stale_seen), old * HEAD_DIM ** (-0.5), -jnp.inf)
    top = jnp.maximum(jnp.max(fresh, axis=-1, keepdims=True), jnp.max(old, axis=-1, keepdims=True))
    fresh, old = jnp.exp(fresh - top), jnp.exp(old - top)
    norm = jnp.sum(fresh, axis=-1, keepdims=True) + jnp.sum(old, axis=-1, keepdims=True)
    fresh, old = (fresh / norm).astype(BF16), (old / norm).astype(BF16)
    outs = jnp.dot(fresh, value, preferred_element_type=F32)
    outs = outs + jnp.dot(old, stale[1], preferred_element_type=F32)
    outs = jnp.where(lanes, outs, 0.0)
    outs = total_of([outs[h * share : (h + 1) * share] for h in range(heads)])
    block[...] = jnp.concatenate([outs[:fold], outs[fold:]], axis=1).astype(BF16)
    copies = [begin(block, attended.at[i], sems.at[i]) for i in range(attended.shape[0])]
    new = jnp.concatenate([key.astype(F32), pairs[:, width:]], axis=1).astype(BF16)
    patch, slot = slots_by_patch((dims.total, 1), 0, dims.cap_all)
    position = positions(sizes, patch, slot, dims.patches)
    spread_out = (iota((dims.total, live), 1) == position).astype(F32).astype(BF16)
    fresh_rows[...] = jnp.dot(spread_out, new, preferred_element_type=F32).astype(BF16)
    copies.append(begin(fresh_rows, cache, sems.at[attended.shape[0]]))
    finish(copies)


def output_rows(dims, sizes, mod, near, states, arrived):
    width = dims.group_width
    rows = []
    for h in range(dims.turns):
        parts = [
            arrived[(h * dims.groups + g) * dims.pairs + y].astype(F32)
            for y in range(dims.pairs)
            for g in range(dims.groups)
        ]
        rows.append(jnp.concatenate([part[:, :width] for part in parts], axis=1))
        rows.append(jnp.concatenate([part[:, width:] for part in parts], axis=1))
    heads = jnp.concatenate(rows, axis=0).astype(BF16)
    projected = lax.dot_general(
        heads, near[...], (((1,), (1,)), ((), ())), preferred_element_type=F32
    )
    gate = own_then_other(dims, modulation_rows(dims, mod, sizes)[2])[0]
    return (from_first(dims, states) + gate * projected).astype(BF16)


def from_first(dims, states):
    half = jnp.zeros((dims.live, 1), jnp.int32) + lax.axis_index("fsdp")
    return jnp.where(half == 0, states.astype(F32), 0.0)


def layer_rows(dims, sizes, mod, near, states, arrived, out):
    out[...] = output_rows(dims, sizes, mod, near, states[...], arrived)


def both(first, second):
    return (first[...].astype(F32) + second[...].astype(F32)).astype(BF16)


def next_partials(
    dims, sizes, mod, weights, swapped, corner, others, across, given, out, staged, sems
):
    states = [both(given, across), both(others, corner)]
    states = jnp.concatenate([part.astype(F32) for part in states], axis=1)
    mean = jnp.mean(states, axis=-1, keepdims=True)
    centred = states - mean
    spread = jnp.sum(centred * centred, axis=-1, keepdims=True)
    stats = in_lanes(split_three(mean) + split_three(spread), 128)
    eye = (iota((dims.live, dims.live), 0) == iota((dims.live, dims.live), 1)).astype(F32).astype(BF16)
    stats = lax.dot_general(stats, eye, (((0,), (0,)), ((), ())), preferred_element_type=F32)[:8]
    lanes = 2 * dims.group_width
    stats = jnp.concatenate([stats, jnp.zeros((8, lanes - dims.live), F32)], axis=1).astype(BF16)
    rows = jnp.concatenate(own_then_other(dims, mod[...].astype(F32)), axis=1)
    is_text = iota((dims.live, 1), 0) < sizes[dims.patches]
    scaled = centred * (1.0 + jnp.where(is_text, rows[4:5], rows[1:2]))
    extra = jnp.concatenate(
        [1.0 + rows[4:5], 1.0 + rows[1:2], rows[3:4], rows[0:1], jnp.zeros_like(rows[:4])], axis=0
    )
    left = jnp.concatenate([scaled, extra], axis=0).astype(BF16)
    mixed = [
        jnp.dot(left[:, : dims.depth], weights[i], preferred_element_type=F32)
        + jnp.dot(left[:, dims.depth :], swapped[i], preferred_element_type=F32)
        for i in range(3)
    ]
    put_partials(dims, out, staged, sems, *mixed, True, stats)


def last_rows(
    dims, sizes, mod, near, made, back, given, across, first_cache, last_cache, first_side,
    last_side, arrived, out, pair, pieces, staged, sems, fetched, sent
):
    def spread(states):
        patch, slot = slots_by_device((dims.total, 1), 0, dims.cap_dev, dims.patches)
        position = positions(sizes, patch, slot, dims.patches)
        pick = (iota((dims.total, dims.live), 1) == position).astype(F32).astype(BF16)
        blocks = jnp.dot(pick, states, preferred_element_type=F32).astype(BF16)
        staged[...] = blocks.reshape(staged.shape)
        finish(
            [
                begin(staged, out.at[pl.ds(i * dims.count, dims.count)], sems.at[i])
                for i in range(out.shape[0] // dims.count)
            ]
        )

    def fetch(cache, side):
        copy = begin(cache, pieces.at[0], fetched)
        pieces[1] = side[...]
        return copy

    section = lax.axis_index("section")

    @pl.when(section == 0)
    def _():
        fetching = fetch(first_cache, first_side)
        states = from_first(dims, both(made, back)).astype(BF16)
        fetching.wait()
        copy = begin(pieces, pair, sent)
        spread(states)
        copy.wait()

    @pl.when(section != 0)
    def _():
        fetching = fetch(last_cache, last_side)
        states = output_rows(dims, sizes, mod, near, both(given, across), arrived)
        fetching.wait()
        copy = begin(pieces, pair, sent)
        spread(states)
        copy.wait()


def join(dims, arrived, pair, other, out, cache, pieces):
    for i in range(dims.count):
        block = arrived[i].astype(F32) + arrived[dims.count + i].astype(F32)
        block = block.reshape(dims.patches, dims.cap_dev, dims.depth)
        out[0, :, :, i * dims.depth : (i + 1) * dims.depth] = block.astype(BF16)
    groups, width, pairs = dims.groups, dims.group_width, dims.pairs
    own = lax.axis_index("tok")
    line, side = own // pairs, own % pairs
    for g, blocks in enumerate((pair, other)):
        for y in range(pairs):
            pieces[(side ^ y) * groups + (line % groups ^ g)] = blocks[y]
    for i in range(2):
        cut = slice(i * width, (i + 1) * width)
        cache[i] = jnp.concatenate([pieces[j][:, cut] for j in range(groups * pairs)], axis=1)


Dims = collections.namedtuple(
    "Dims",
    [
        "count",
        "pairs",
        "patches",
        "cap_dev",
        "cap_all",
        "total",
        "live",
        "depth",
        "groups",
        "turns",
        "group_width",
    ],
)


class Stays:
    def __init__(self, *shape):
        self.struct = pltpu.VMEM(shape, BF16)


class Leaves:
    def __init__(self, *shape):
        self.struct = pltpu.HBM(shape, BF16)


def only(section, body, *refs):
    @pl.when(lax.axis_index("section") == section)
    def _():
        body(*refs)


def stage(body, outs, smem, *arguments, left=(), scratch=(), grant=16, moved=0):
    spaces = [pltpu.SMEM] * smem + [pltpu.VMEM] * (len(arguments) - smem)
    place = lambda out: pltpu.HBM if isinstance(out, Leaves) else pltpu.VMEM
    out_specs = jax.tree.map(lambda out: pl.BlockSpec(memory_space=place(out)), outs)
    outs = jax.tree.map(lambda out: getattr(out, "struct", out), outs)
    arguments = list(arguments)
    for i in left:
        spaces[i] = pltpu.HBM
        arguments[i] = pltpu.with_memory_space_constraint(arguments[i], pltpu.HBM)
    return pl.pallas_call(
        body,
        out_shape=outs,
        in_specs=[pl.BlockSpec(memory_space=space) for space in spaces],
        out_specs=out_specs,
        scratch_shapes=scratch,
        cost_estimate=pl.CostEstimate(flops=0, bytes_accessed=moved, transcendentals=0) if moved else None,
        compiler_params=pltpu.CompilerParams(vmem_limit_bytes=grant * 1024 * 1024),
    )(*arguments)


def by_kernels(hidden, lengths, text_count, timestep, mod_table, w_qkv, w_out, qk_gain, stale_cache):
    count = lax.axis_size("tok")
    halves = lax.axis_size("fsdp")
    own = lax.axis_index("tok")
    patches, cap_dev, width = hidden.shape
    rows = patches * cap_dev
    total = rows * count
    live = total * 3 // 4
    depth, local_width = w_qkv.shape[1], w_qkv.shape[3]
    pairs = 2
    lines = count // pairs
    line, side = own // pairs, own % pairs
    half_width = local_width // pairs
    groups = math.gcd(half_width // HEAD_DIM, lines)
    turns = lines // groups
    group_width = half_width // groups
    cap_all = cap_dev * count
    dims = Dims(
        count, pairs, patches, cap_dev, cap_all, total, live, depth, groups, turns, group_width
    )
    share = live // turns
    fold = share // 2

    def struct(*shape):
        return jax.ShapeDtypeStruct(shape, BF16)

    kernel = lambda body, *rest: functools.partial(body, dims, *rest)
    working = lambda section, body, *rest: functools.partial(only, section, kernel(body, *rest))
    place = lambda s, f, t: (s * halves + f) * count + t

    def send(block, source, target, df=0, dt=0):
        ends = [
            (place(source, f, t), place(target, f ^ df, t ^ dt))
            for f in range(halves)
            for t in range(count)
        ]
        return lax.ppermute(block, ("section", "fsdp", "tok"), ends)

    def grouped(blocks, section, working, idle):
        sizes = {len(group) for group in working + idle}
        if len(sizes) > 1 or len(working) != len(idle):
            idle = working
        groups = [[place(section, *at) for at in group] for group in working]
        groups += [[place(1 - section, *at) for at in group] for group in idle]
        return lax.all_to_all(
            blocks, ("section", "fsdp", "tok"), 0, 0, axis_index_groups=groups, tiled=False
        )

    def over_tok(blocks, section):
        half = lines // 2
        working = [[(f, t) for t in range(count)] for f in range(halves)]
        idle = [
            [(f, t) for f in range(halves) for t in range(z * pairs, (z + half) * pairs)]
            for z in range(0, lines, half)
        ]
        return grouped(blocks, section, working, idle)

    def over_lines(blocks, section):
        working = [
            [(f, z * pairs + y) for z in range(lines)] for f in range(halves) for y in range(pairs)
        ]
        idle = [
            [(f, z * pairs + y) for f in range(halves) for y in range(pairs)] for z in range(lines)
        ]
        return grouped(blocks, section, working, idle)

    def all_devices(blocks):
        return lax.all_to_all(blocks, ("fsdp", "tok"), 0, 0, tiled=False)

    def after(done, *operands):
        return lax.optimization_barrier((done, *operands))

    height = live + fold
    attended_shape = (
        Leaves(count, fold, 2 * group_width),
        Leaves(total, 2 * group_width),
    )
    attended_scratch = [
        pltpu.VMEM((fold, 2 * group_width), BF16),
        pltpu.VMEM((total, 2 * group_width), BF16),
        pltpu.SemaphoreType.DMA((count + 1,)),
    ]
    weights = w_qkv[0].transpose(1, 0, 2)
    near = w_out[0]
    gains = qk_gain[0]
    stale = lax.dynamic_slice_in_dim(
        stale_cache[0].reshape(2, total, local_width),
        side * half_width + line % groups * group_width,
        group_width,
        2,
    )

    blocks = stage(
        kernel(send_rows),
        Leaves(count, rows, depth + 128),
        0,
        hidden,
        scratch=[pltpu.VMEM((count, rows, depth + 128), BF16), pltpu.SemaphoreType.DMA((count,))],
        grant=62,
    )
    blocks, step, lengths, text_count, weights_now = after(
        blocks, timestep, lengths, text_count, weights
    )
    sizes = jnp.concatenate([lengths, text_count])
    loaded_first = stage(
        working(0, load, False),
        Stays(3, depth, local_width),
        0,
        weights_now,
        left=(0,),
        scratch=[pltpu.SemaphoreType.DMA((3,))],
        moved=4 * weights.size,
    )
    arrived = over_tok(blocks, 0)
    mod = lax.dynamic_slice(
        mod_table[0].transpose(1, 0, 2), (0, step[0], line * pairs * depth), (6, 1, pairs * depth)
    )[:, 0]

    states, blocks = stage(
        working(0, first_partials),
        (struct(live, depth), Leaves(count, height, 2 * group_width)),
        1,
        sizes,
        mod,
        loaded_first,
        arrived,
        scratch=[
            pltpu.VMEM((count, height, 2 * group_width), BF16),
            pltpu.SemaphoreType.DMA((count,)),
        ],
    )
    blocks, weights_now = after(blocks, weights)
    arrived = over_tok(blocks, 0)
    loaded_last = stage(
        working(1, load, True),
        Stays(3, depth, half_width),
        0,
        weights_now,
        left=(0,),
        scratch=[pltpu.SemaphoreType.DMA((3,))],
        moved=4 * weights.size,
    )
    leaving = lax.dynamic_slice_in_dim(weights_now, (1 - side) * half_width, half_width, 2)

    attended, cache_first = stage(
        working(0, attention, 0),
        attended_shape,
        1,
        sizes,
        gains,
        stale,
        arrived,
        scratch=attended_scratch,
    )
    attended, leaving = after(attended, leaving)
    arrived = over_tok(attended, 0)
    swapped_last = send(leaving, 1, 1, dt=1)
    made = stage(
        working(0, layer_rows),
        struct(live, depth),
        1,
        sizes,
        mod,
        near,
        states,
        arrived,
    )
    given = send(made, 0, 1)
    across = send(made, 0, 1, df=1)
    others = send(made, 0, 1, dt=1)
    corner = send(made, 0, 1, df=1, dt=1)
    blocks = stage(
        working(1, next_partials),
        Leaves(lines, height + 16, 2 * group_width),
        1,
        sizes,
        mod,
        loaded_last,
        swapped_last,
        corner,
        others,
        across,
        given,
        scratch=[
            pltpu.VMEM((lines, height + 16, 2 * group_width), BF16),
            pltpu.SemaphoreType.DMA((lines,)),
        ],
    )
    blocks, made, cache_first = after(blocks, made, cache_first)
    arrived = over_lines(blocks, 1)
    back = send(made, 0, 0, df=1)
    side_first = send(cache_first, 0, 0, dt=1)
    arrived, back, side_first = after(arrived, back, side_first)

    attended, cache_last = stage(
        working(1, attention, 1),
        attended_shape,
        1,
        sizes,
        gains,
        stale,
        arrived,
        scratch=attended_scratch,
    )
    arrived = over_tok(attended, 1)
    side_last = send(cache_last, 1, 1, dt=1)
    arrived, side_last = after(arrived, side_last)
    blocks, pair, kept_pair = stage(
        kernel(last_rows),
        (
            Leaves(halves * count, rows, depth),
            Leaves(2, total, 2 * group_width),
            Stays(2, total, 2 * group_width),
        ),
        1,
        sizes,
        mod,
        near,
        made,
        back,
        given,
        across,
        cache_first,
        cache_last,
        side_first,
        side_last,
        arrived,
        left=(7, 8),
        scratch=[
            pltpu.VMEM((count, rows, depth), BF16),
            pltpu.SemaphoreType.DMA((halves,)),
            pltpu.SemaphoreType.DMA,
            pltpu.SemaphoreType.DMA,
        ],
    )
    arrived = all_devices(blocks)
    other = lax.ppermute(pair, "tok", [(t, t ^ pairs) for t in range(count)])
    final, new_cache = stage(
        kernel(join),
        (struct(1, patches, cap_dev, width), struct(2, total, local_width)),
        0,
        arrived,
        kept_pair,
        other,
        scratch=[pltpu.VMEM((groups * pairs, total, 2 * group_width), BF16)],
    )
    return final, new_cache.reshape(1, 2, patches, cap_all, local_width)


def solution(mesh):
    in_specs = (
        P(None, "tok", None),
        P(),
        P(),
        P(),
        P("section", None, None, None),
        P("section", "tok", None, "fsdp"),
        P("section", "tok", "fsdp"),
        P("section", None, None),
        P("section", None, None, None, "fsdp"),
    )
    out_specs = (P("section", None, "tok", None), P("section", None, None, None, "fsdp"))
    local = by_kernels if mesh.shape["tok"] <= MOST_PEERS else by_all_to_all
    return jax.shard_map(local, mesh=mesh, in_specs=in_specs, out_specs=out_specs, check_vma=False)
```

time: 661 us -> 102 us (0.15)
  the two profiles are of different devices: /device:TPU:0 before, /device:TPU:1 now
where the time goes in v1:
time: 102 us; the launch traced here: 101 us
  starting transfers between devices  33.6 us (33%)
  waiting for transfers between devices  32.9 us (32%)
  Pallas kernels  13.7 us (13%)
  blocking collectives  13.6 us (13%)
  local copies, waits for them, and re-layouts  5.1 us (5%)
  between operations  2.26 us (2%)
    all_to_all x4, starting transfers between devices, grouped(): lax.all_to_all(blocks, ('section', 'fsdp', 'tok'), 0, 0, axis_index_group...  15.7 us
    all_to_all x4, waiting for transfers between devices, grouped(): lax.all_to_all(blocks, ('section', 'fsdp', 'tok'), 0, 0, axis_index_group...  15.5 us
    pallas_call x10, Pallas kernels, stage(): pl.pallas_call(body, out_shape=outs, in_specs=[pl.BlockSpec(memory_space=...  13.7 us
    all_to_all x1, blocking collectives, grouped(): lax.all_to_all(blocks, ('section', 'fsdp', 'tok'), 0, 0, axis_index_group...  13.6 us
    ppermute x8, waiting for transfers between devices, send(): return lax.ppermute(block, ('section', 'fsdp', 'tok'), ends)  11.8 us
    ppermute x8, starting transfers between devices, send(): return lax.ppermute(block, ('section', 'fsdp', 'tok'), ends)  11.7 us
    ppermute x1, waiting for transfers between devices, by_kernels(): other = lax.ppermute(pair, 'tok', [(t, t ^ pairs) for t in range(count)])  4.84 us
    all_to_all x1, starting transfers between devices, all_devices(): return lax.all_to_all(blocks, ('fsdp', 'tok'), 0, 0, tiled=False)  4.81 us
  transfers between devices with their start and end apart: 14, of which 10 were waited for; matrix products, arithmetic and copies ran while one was open for 2% of the time, Pallas kernels for 2%

profile of v1, /device:TPU:1, one launch (start us, length us, event | category | flops | bytes accessed | tf_op | source)
XLA Modules:
  0.0 101.3 jit_solution(12830172724112445)
XLA Ops:
  0.6 1.9 %shard_map.104 = bf16[8,16,512]{2,1,0:T(8,128)(2,1)} custom-call(bf16[4,4,3072]{2,1,0:T(4,128)(2,1)} %hidden.1), custom_call_target="tpu_custom_call" | custom-call | tf_op jit(solution)/shard_map/pallas_call | solution.py:612
  2.5 5.3 %all-to-all-start = ((bf16[8,16,512]{2,1,0:T(8,128)(2,1)}), bf16[8,16,512]{2,1,0:T(8,128)(2,1)S(1)}, u32[]{:S(2)}, u32[]{:S(2)}) async-start(bf16[8,16,512]{2,1,0:T(8,128)(2,1)} %shard_map.104), calls=%async_computation | async-start | bytes 262144 | tf_op jit(solution)/shard_map/all_to_all | solution.py:667
  9.2 1.0 constant_dynamic-slice_fusion.2
  10.2 1.2 %copy-done.1 = bf16[3,384,768]{2,1,0:T(8,128)(2,1)} copy-done((bf16[3,384,768]{2,1,0:T(8,128)(2,1)}, bf16[3,384,768]{2,1,0:T(8,128)(2,1)S(1)}, u32[]{:S(2)}) %copy-start.1) | copy-done | bytes 1769496
  11.5 1.4 %all-to-all-done.refs_3_ = bf16[8,16,512]{2,1,0:T(8,128)(2,1)S(1)} async-done(((bf16[8,16,512]{2,1,0:T(8,128)(2,1)}), bf16[8,16,512]{2,1,0:T(8,128)(2,1)S(1)}, u32[]{:S(2)}, u32[]{:S(2)}) %all-to-all-start) | async-done | bytes 131104 | tf_op jit(solution)/shard_map/all_to_all | solution.py:667
  13.0 1.5 %copy-done.2 = bf16[3,384,768]{2,1,0:T(8,128)(2,1)S(1)} copy-done((bf16[3,384,768]{2,1,0:T(8,128)(2,1)S(1)}, bf16[3,384,768]{2,1,0:T(8,128)(2,1)}, u32[]{:S(2)}) %copy-start.2) | copy-done | bytes 1769496
  15.1 3.6 %all-to-all-start.1 = ((bf16[8,120,384]{2,1,0:T(8,128)(2,1)}), bf16[8,120,384]{2,1,0:T(8,128)(2,1)S(1)}, u32[]{:S(2)}, u32[]{:S(2)}) async-start(bf16[8,120,384]{2,1,0:T(8,128)(2,1)} %get-tuple-element.37), calls=%async_computation.1 | async-start | bytes 1474560 | tf_op jit(solution)/shard_map/all_to_all | solution.py:667
  18.8 1.3 %constant_dynamic-slice_fusion = bf16[3,384,384]{2,1,0:T(8,128)(2,1)S(1)} fusion(bf16[3,384,768]{2,1,0:T(8,128)(2,1)} %bitcast.24, s32[]{:T(128)S(6)} %select_n.33), kind=kLoop, calls=%fused_computation.1 | loop fusion | bytes 1769476 | tf_op jit(solution)/shard_map/dynamic_slice | solution.py:765
  20.1 6.9 %all-to-all-done.1.refs_3_ = bf16[8,120,384]{2,1,0:T(8,128)(2,1)S(1)} async-done(((bf16[8,120,384]{2,1,0:T(8,128)(2,1)}), bf16[8,120,384]{2,1,0:T(8,128)(2,1)S(1)}, u32[]{:S(2)}, u32[]{:S(2)}) %all-to-all-start.1) | async-done | bytes 737312 | tf_op jit(solution)/shard_map/all_to_all | solution.py:667
  27.6 1.9 %collective-permute-start = (bf16[3,384,384]{2,1,0:T(8,128)(2,1)S(1)}, bf16[3,384,384]{2,1,0:T(8,128)(2,1)S(1)}, u32[]{:S(2)}, u32[]{:S(2)}) collective-permute-start(bf16[3,384,384]{2,1,0:T(8,128)(2,1)S(1)} %constant_dynamic-slice_fusion), channel_id=1, source_target_pairs={{16,17},{17,16},{18,19},{19,18},{20,21},{21,20},{22,23},{23,22},{2... | collective-permute-start | bytes 2654216 | tf_op jit(solution)/shard_map/ppermute | solution.py:659
  29.6 13.6 %all_to_all.30.refs_4_ = bf16[8,24,384]{2,1,0:T(8,128)(2,1)S(1)} all-to-all(bf16[8,24,384]{2,1,0:T(8,128)(2,1)} %get-tuple-element.41), channel_id=1, replica_groups={{0,1,2,3,4,5,6,7},{8,9,10,11,12,13,14,15},{16,17,18,19,24,25,26,27},{20..., dimensions={0} | all-to-all | bytes 294912 | tf_op jit(solution)/shard_map/all_to_all | solution.py:667
  43.8 1.3 %collective-permute-start.1 = (bf16[96,384]{1,0:T(8,128)(2,1)S(1)}, bf16[96,384]{1,0:T(8,128)(2,1)S(1)}, u32[]{:S(2)}, u32[]{:S(2)}) collective-permute-start(bf16[96,384]{1,0:T(8,128)(2,1)S(1)} %shard_map.109.made), channel_id=1, source_target_pairs={{0,25},{1,24},{2,27},{3,26},{4,29},{5,28},{6,31},{7,30},{8,17},{9,... | collective-permute-start | bytes 221192 | tf_op jit(solution)/shard_map/ppermute | solution.py:659
  45.1 1.3 %collective-permute-start.2 = (bf16[96,384]{1,0:T(8,128)(2,1)S(1)}, bf16[96,384]{1,0:T(8,128)(2,1)S(1)}, u32[]{:S(2)}, u32[]{:S(2)}) collective-permute-start(bf16[96,384]{1,0:T(8,128)(2,1)S(1)} %shard_map.109.made), channel_id=1, source_target_pairs={{0,17},{1,16},{2,19},{3,18},{4,21},{5,20},{6,23},{7,22},{8,25},{9,... | collective-permute-start | bytes 221192 | tf_op jit(solution)/shard_map/ppermute | solution.py:659
  46.4 1.3 %collective-permute-start.3 = (bf16[96,384]{1,0:T(8,128)(2,1)S(1)}, bf16[96,384]{1,0:T(8,128)(2,1)S(1)}, u32[]{:S(2)}, u32[]{:S(2)}) collective-permute-start(bf16[96,384]{1,0:T(8,128)(2,1)S(1)} %shard_map.109.made), channel_id=1, source_target_pairs={{0,24},{1,25},{2,26},{3,27},{4,28},{5,29},{6,30},{7,31},{8,16},{9,... | collective-permute-start | bytes 221192 | tf_op jit(solution)/shard_map/ppermute | solution.py:659
  47.7 1.3 %collective-permute-start.4 = (bf16[96,384]{1,0:T(8,128)(2,1)S(1)}, bf16[96,384]{1,0:T(8,128)(2,1)S(1)}, u32[]{:S(2)}, u32[]{:S(2)}) collective-permute-start(bf16[96,384]{1,0:T(8,128)(2,1)S(1)} %shard_map.109.made), channel_id=1, source_target_pairs={{0,16},{1,17},{2,18},{3,19},{4,20},{5,21},{6,22},{7,23},{8,24},{9,... | collective-permute-start | bytes 221192 | tf_op jit(solution)/shard_map/ppermute | solution.py:659
  49.0 1.2 %shard_map.107.refs_2_ = bf16[3,384,384]{2,1,0:T(8,128)(2,1)S(1)} custom-call(bf16[3,384,768]{2,1,0:T(8,128)(2,1)} %bitcast.25), custom_call_target="tpu_custom_call" | custom-call | bytes 3538944 | tf_op jit(solution)/shard_map/pallas_call | solution.py:612
  50.2 6.5 %collective-permute-done.1.refs_4_ = bf16[96,384]{1,0:T(8,128)(2,1)S(1)} collective-permute-done((bf16[96,384]{1,0:T(8,128)(2,1)S(1)}, bf16[96,384]{1,0:T(8,128)(2,1)S(1)}, u32[]{:S(2)}, u32[]{:S(2)}) %collective-permute-start.1) | collective-permute-done | bytes 73760 | tf_op jit(solution)/shard_map/ppermute | solution.py:659
  56.7 0.7 collective-permute-done.2.refs_5_
  57.4 2.2 %collective-permute-done.3.refs_6_.across = bf16[96,384]{1,0:T(8,128)(2,1)S(1)} collective-permute-done((bf16[96,384]{1,0:T(8,128)(2,1)S(1)}, bf16[96,384]{1,0:T(8,128)(2,1)S(1)}, u32[]{:S(2)}, u32[]{:S(2)}) %collective-permute-start.3) | collective-permute-done | bytes 73760 | tf_op jit(solution)/shard_map/ppermute | solution.py:659
  59.6 2.2 %shard_map.110 = bf16[4,136,384]{2,1,0:T(8,128)(2,1)} custom-call(s32[5]{0:T(128)S(1)} %pad_add_fusion.refs_0_.sizes, bf16[6,768]{1,0:T(8,128)(2,1)S(1)} %bitcast.19, bf16[3,384,384]{2,1,0:T(8,128)(2,1)S(1)} %shard_map.107.refs_2_, bf16[3,384,384]{2,1,0:T(8,128)(2,1)S(1)} %collective-permute-done.refs_3_, ...), custom_call_target="tpu_custom_call" | custom-call | tf_op jit(solution)/shard_map/pallas_call | solution.py:612
  61.8 3.5 %all-to-all-start.3 = ((bf16[4,136,384]{2,1,0:T(8,128)(2,1)}), bf16[4,136,384]{2,1,0:T(8,128)(2,1)S(1)}, u32[]{:S(2)}, u32[]{:S(2)}) async-start(bf16[4,136,384]{2,1,0:T(8,128)(2,1)} %shard_map.110), calls=%async_computation.3 | async-start | bytes 835584 | tf_op jit(solution)/shard_map/all_to_all | solution.py:667
  66.7 6.6 %all-to-all-done.3.refs_3_ = bf16[4,136,384]{2,1,0:T(8,128)(2,1)S(1)} async-done(((bf16[4,136,384]{2,1,0:T(8,128)(2,1)}), bf16[4,136,384]{2,1,0:T(8,128)(2,1)S(1)}, u32[]{:S(2)}, u32[]{:S(2)}) %all-to-all-start.3) | async-done | bytes 417824 | tf_op jit(solution)/shard_map/all_to_all | solution.py:667
  73.3 3.1 %shard_map.111 = (bf16[8,24,384]{2,1,0:T(8,128)(2,1)}, bf16[128,384]{1,0:T(8,128)(2,1)}) custom-call(s32[5]{0:T(128)S(1)} %pad_add_fusion.refs_0_.sizes, f32[2,64]{1,0:T(2,128)S(1)} %bitcast.22, bf16[2,128,192]{2,1,0:T(8,128)(2,1)S(1)} %constant_dynamic-slice_fusion.1.refs_2_, bf16[4,136,384]{2,1,0:T(8,128)(2,1)S(1)} %all-to-all-done.3.refs_3_), custom_call_target="tpu_custom_call" | custom-call | tf_op jit(solution)/shard_map/pallas_call | solution.py:612
  76.4 3.4 %all-to-all-start.4 = ((bf16[8,24,384]{2,1,0:T(8,128)(2,1)}), bf16[8,24,384]{2,1,0:T(8,128)(2,1)S(1)}, u32[]{:S(2)}, u32[]{:S(2)}) async-start(bf16[8,24,384]{2,1,0:T(8,128)(2,1)} %get-tuple-element.50), calls=%async_computation.4 | async-start | bytes 294912 | tf_op jit(solution)/shard_map/all_to_all | solution.py:667
  79.8 3.3 %collective-permute-start.7 = (bf16[128,384]{1,0:T(8,128)(2,1)}, bf16[128,384]{1,0:T(8,128)(2,1)S(1)}, u32[]{:S(2)}, u32[]{:S(2)}) collective-permute-start(bf16[128,384]{1,0:T(8,128)(2,1)} %get-tuple-element.48.last_cache), channel_id=1, source_target_pairs={{16,17},{17,16},{18,19},{19,18},{20,21},{21,20},{22,23},{23,22},{2... | collective-permute-start | bytes 294920 | tf_op jit(solution)/shard_map/ppermute | solution.py:659
  83.1 2.3 %collective-permute-done.7.last_side = bf16[128,384]{1,0:T(8,128)(2,1)S(1)} collective-permute-done((bf16[128,384]{1,0:T(8,128)(2,1)}, bf16[128,384]{1,0:T(8,128)(2,1)S(1)}, u32[]{:S(2)}, u32[]{:S(2)}) %collective-permute-start.7) | collective-permute-done | bytes 98336 | tf_op jit(solution)/shard_map/ppermute | solution.py:659
  86.0 2.5 %shard_map.112 = (bf16[16,16,384]{2,1,0:T(8,128)(2,1)}, bf16[2,128,384]{2,1,0:T(8,128)(2,1)}, bf16[2,128,384]{2,1,0:T(8,128)(2,1)S(1)}) custom-call(s32[5]{0:T(128)S(1)} %pad_add_fusion.refs_0_.sizes, bf16[6,768]{1,0:T(8,128)(2,1)S(1)} %bitcast.20, bf16[384,768]{1,0:T(8,128)(2,1)S(1)} %bitcast.16, bf16[96,384]{1,0:T(8,128)(2,1)S(1)} %shard_map.109.made, ...), custom_call_target="tpu_custom_call" | custom-call | tf_op jit(solution)/shard_map/pallas_call | solution.py:612
  88.5 4.8 %all-to-all-start.5 = ((bf16[16,16,384]{2,1,0:T(8,128)(2,1)}), bf16[16,16,384]{2,1,0:T(8,128)(2,1)S(1)}, u32[]{:S(2)}, u32[]{:S(2)}) async-start(bf16[16,16,384]{2,1,0:T(8,128)(2,1)} %get-tuple-element.53), calls=%async_computation.5 | async-start | bytes 393216 | tf_op jit(solution)/shard_map/all_to_all | solution.py:690
  93.3 1.4 %collective-permute-start.8 = (bf16[2,128,384]{2,1,0:T(8,128)(2,1)}, bf16[2,128,384]{2,1,0:T(8,128)(2,1)S(1)}, u32[]{:S(2)}, u32[]{:S(2)}) collective-permute-start(bf16[2,128,384]{2,1,0:T(8,128)(2,1)} %get-tuple-element.55), channel_id=1, source_target_pairs={{0,2},{1,3},{2,0},{3,1},{4,6},{5,7},{6,4},{7,5},{8,10},{9,11},{10,... | collective-permute-start | bytes 589832 | tf_op jit(solution)/shard_map/ppermute | solution.py:859
  94.7 4.8 %collective-permute-done.8.other = bf16[2,128,384]{2,1,0:T(8,128)(2,1)S(1)} collective-permute-done((bf16[2,128,384]{2,1,0:T(8,128)(2,1)}, bf16[2,128,384]{2,1,0:T(8,128)(2,1)S(1)}, u32[]{:S(2)}, u32[]{:S(2)}) %collective-permute-start.8) | collective-permute-done | bytes 196640 | tf_op jit(solution)/shard_map/ppermute | solution.py:859
  99.6 0.7 all-to-all-done.5.arrived
  100.3 1.0 shard_map.113
  (26 shorter events, 4.1 us)
Async XLA Ops:
  0.6 18.1 %copy-start = (bf16[1,2,4,32,768]{4,3,2,1,0:T(8,128)(2,1)S(1)}, bf16[1,2,4,32,768]{4,3,2,1,0:T(8,128)(2,1)}, u32[]{:S(2)}) copy-start(bf16[1,2,4,32,768]{4,3,2,1,0:T(8,128)(2,1)} %param.17) | copy-start | bytes 1179652
  2.5 10.4 %all-to-all-start = ((bf16[8,16,512]{2,1,0:T(8,128)(2,1)}), bf16[8,16,512]{2,1,0:T(8,128)(2,1)S(1)}, u32[]{:S(2)}, u32[]{:S(2)}) async-start(bf16[8,16,512]{2,1,0:T(8,128)(2,1)} %shard_map.104), calls=%async_computation | async-start | bytes 262144 | tf_op jit(solution)/shard_map/all_to_all | solution.py:667
  10.2 1.3 %copy-start.6 = (s32[4]{0:T(128)S(1)}, s32[4]{0:T(128)}, u32[]{:S(2)}) copy-start(s32[4]{0:T(128)} %param.10) | copy-start | bytes 52
  10.2 1.2 %copy-start.1 = (bf16[3,384,768]{2,1,0:T(8,128)(2,1)}, bf16[3,384,768]{2,1,0:T(8,128)(2,1)S(1)}, u32[]{:S(2)}) copy-start(bf16[3,384,768]{2,1,0:T(8,128)(2,1)S(1)} %shard_map.105.refs_2_) | copy-start | bytes 5308420
  13.0 1.5 %copy-start.2 = (bf16[3,384,768]{2,1,0:T(8,128)(2,1)S(1)}, bf16[3,384,768]{2,1,0:T(8,128)(2,1)}, u32[]{:S(2)}) copy-start(bf16[3,384,768]{2,1,0:T(8,128)(2,1)} %copy-done.1) | copy-start | bytes 5308420
  15.1 11.9 %copy-start.4 = (f32[1,2,64]{2,1,0:T(2,128)S(1)}, f32[1,2,64]{2,1,0:T(2,128)}, u32[]{:S(2)}) copy-start(f32[1,2,64]{2,1,0:T(2,128)} %param.16) | copy-start | bytes 1540
  15.1 11.9 %all-to-all-start.1 = ((bf16[8,120,384]{2,1,0:T(8,128)(2,1)}), bf16[8,120,384]{2,1,0:T(8,128)(2,1)S(1)}, u32[]{:S(2)}, u32[]{:S(2)}) async-start(bf16[8,120,384]{2,1,0:T(8,128)(2,1)} %get-tuple-element.37), calls=%async_computation.1 | async-start | bytes 1474560 | tf_op jit(solution)/shard_map/all_to_all | solution.py:667
  18.7 24.5 %copy-start.3 = (bf16[1,384,768]{2,1,0:T(8,128)(2,1)S(1)}, bf16[1,384,768]{2,1,0:T(8,128)(2,1)}, u32[]{:S(2)}) copy-start(bf16[1,384,768]{2,1,0:T(8,128)(2,1)} %param.15) | copy-start | bytes 1769476
  27.6 32.0 %collective-permute-start = (bf16[3,384,384]{2,1,0:T(8,128)(2,1)S(1)}, bf16[3,384,384]{2,1,0:T(8,128)(2,1)S(1)}, u32[]{:S(2)}, u32[]{:S(2)}) collective-permute-start(bf16[3,384,384]{2,1,0:T(8,128)(2,1)S(1)} %constant_dynamic-slice_fusion), channel_id=1, source_target_pairs={{16,17},{17,16},{18,19},{19,18},{20,21},{21,20},{22,23},{23,22},{2... | collective-permute-start | bytes 2654216 | tf_op jit(solution)/shard_map/ppermute | solution.py:659
  43.8 12.9 %collective-permute-start.1 = (bf16[96,384]{1,0:T(8,128)(2,1)S(1)}, bf16[96,384]{1,0:T(8,128)(2,1)S(1)}, u32[]{:S(2)}, u32[]{:S(2)}) collective-permute-start(bf16[96,384]{1,0:T(8,128)(2,1)S(1)} %shard_map.109.made), channel_id=1, source_target_pairs={{0,25},{1,24},{2,27},{3,26},{4,29},{5,28},{6,31},{7,30},{8,17},{9,... | collective-permute-start | bytes 221192 | tf_op jit(solution)/shard_map/ppermute | solution.py:659
  45.1 12.3 %collective-permute-start.2 = (bf16[96,384]{1,0:T(8,128)(2,1)S(1)}, bf16[96,384]{1,0:T(8,128)(2,1)S(1)}, u32[]{:S(2)}, u32[]{:S(2)}) collective-permute-start(bf16[96,384]{1,0:T(8,128)(2,1)S(1)} %shard_map.109.made), channel_id=1, source_target_pairs={{0,17},{1,16},{2,19},{3,18},{4,21},{5,20},{6,23},{7,22},{8,25},{9,... | collective-permute-start | bytes 221192 | tf_op jit(solution)/shard_map/ppermute | solution.py:659
  46.4 13.3 %collective-permute-start.3 = (bf16[96,384]{1,0:T(8,128)(2,1)S(1)}, bf16[96,384]{1,0:T(8,128)(2,1)S(1)}, u32[]{:S(2)}, u32[]{:S(2)}) collective-permute-start(bf16[96,384]{1,0:T(8,128)(2,1)S(1)} %shard_map.109.made), channel_id=1, source_target_pairs={{0,24},{1,25},{2,26},{3,27},{4,28},{5,29},{6,30},{7,31},{8,16},{9,... | collective-permute-start | bytes 221192 | tf_op jit(solution)/shard_map/ppermute | solution.py:659
  47.7 12.0 %collective-permute-start.4 = (bf16[96,384]{1,0:T(8,128)(2,1)S(1)}, bf16[96,384]{1,0:T(8,128)(2,1)S(1)}, u32[]{:S(2)}, u32[]{:S(2)}) collective-permute-start(bf16[96,384]{1,0:T(8,128)(2,1)S(1)} %shard_map.109.made), channel_id=1, source_target_pairs={{0,16},{1,17},{2,18},{3,19},{4,20},{5,21},{6,22},{7,23},{8,24},{9,... | collective-permute-start | bytes 221192 | tf_op jit(solution)/shard_map/ppermute | solution.py:659
  50.1 15.2 %copy-start.5 = (bf16[128,384]{1,0:T(8,128)(2,1)S(1)}, bf16[128,384]{1,0:T(8,128)(2,1)}, u32[]{:S(2)}) copy-start(bf16[128,384]{1,0:T(8,128)(2,1)} %get-tuple-element.45.first_cache) | copy-start | bytes 294916
  61.8 11.4 %all-to-all-start.3 = ((bf16[4,136,384]{2,1,0:T(8,128)(2,1)}), bf16[4,136,384]{2,1,0:T(8,128)(2,1)S(1)}, u32[]{:S(2)}, u32[]{:S(2)}) async-start(bf16[4,136,384]{2,1,0:T(8,128)(2,1)} %shard_map.110), calls=%async_computation.3 | async-start | bytes 835584 | tf_op jit(solution)/shard_map/all_to_all | solution.py:667
  65.3 1.4 %collective-permute-start.6 = (bf16[128,384]{1,0:T(8,128)(2,1)S(1)}, bf16[128,384]{1,0:T(8,128)(2,1)S(1)}, u32[]{:S(2)}, u32[]{:S(2)}) collective-permute-start(bf16[128,384]{1,0:T(8,128)(2,1)S(1)} %copy-done.5), channel_id=1, source_target_pairs={{0,1},{1,0},{2,3},{3,2},{4,5},{5,4},{6,7},{7,6},{8,9},{9,8},{10,11... | collective-permute-start | bytes 294920 | tf_op jit(solution)/shard_map/ppermute | solution.py:659
  66.0 0.7 collective-permute-start.5
  76.4 9.6 %all-to-all-start.4 = ((bf16[8,24,384]{2,1,0:T(8,128)(2,1)}), bf16[8,24,384]{2,1,0:T(8,128)(2,1)S(1)}, u32[]{:S(2)}, u32[]{:S(2)}) async-start(bf16[8,24,384]{2,1,0:T(8,128)(2,1)} %get-tuple-element.50), calls=%async_computation.4 | async-start | bytes 294912 | tf_op jit(solution)/shard_map/all_to_all | solution.py:667
  79.8 5.6 %collective-permute-start.7 = (bf16[128,384]{1,0:T(8,128)(2,1)}, bf16[128,384]{1,0:T(8,128)(2,1)S(1)}, u32[]{:S(2)}, u32[]{:S(2)}) collective-permute-start(bf16[128,384]{1,0:T(8,128)(2,1)} %get-tuple-element.48.last_cache), channel_id=1, source_target_pairs={{16,17},{17,16},{18,19},{19,18},{20,21},{21,20},{22,23},{23,22},{2... | collective-permute-start | bytes 294920 | tf_op jit(solution)/shard_map/ppermute | solution.py:659
  88.5 11.8 %all-to-all-start.5 = ((bf16[16,16,384]{2,1,0:T(8,128)(2,1)}), bf16[16,16,384]{2,1,0:T(8,128)(2,1)S(1)}, u32[]{:S(2)}, u32[]{:S(2)}) async-start(bf16[16,16,384]{2,1,0:T(8,128)(2,1)} %get-tuple-element.53), calls=%async_computation.5 | async-start | bytes 393216 | tf_op jit(solution)/shard_map/all_to_all | solution.py:690
  93.3 6.2 %collective-permute-start.8 = (bf16[2,128,384]{2,1,0:T(8,128)(2,1)}, bf16[2,128,384]{2,1,0:T(8,128)(2,1)S(1)}, u32[]{:S(2)}, u32[]{:S(2)}) collective-permute-start(bf16[2,128,384]{2,1,0:T(8,128)(2,1)} %get-tuple-element.55), channel_id=1, source_target_pairs={{0,2},{1,3},{2,0},{3,1},{4,6},{5,7},{6,4},{7,5},{8,10},{9,11},{10,... | collective-permute-start | bytes 589832 | tf_op jit(solution)/shard_map/ppermute | solution.py:859

commit v2 on v1

--- a/solution.py
+++ b/solution.py
@@ -315,8 +315,9 @@
 
 
 def first_partials(
-    dims, sizes, mod, weights, arrived, kept_states, out, staged, sems
+    dims, sizes, mod, weights, values, arrived, kept_states, out, held, sem, staged, sems
 ):
+    copy = begin(values.at[2], held, sem)
     patch, slot = slots_by_device((1, dims.total), 1, dims.cap_dev, dims.patches)
     position = positions(sizes, patch, slot, dims.patches)
     pick = (iota((dims.live, dims.total), 0) == position).astype(F32).astype(BF16)
@@ -328,7 +329,9 @@
     shift, scale, gate = modulation_rows(dims, own_mod, sizes)
     modded = ((states - mean) * inverse * (1.0 + scale) + shift).astype(BF16)
     kept_states[...] = states.astype(BF16)
-    mixed = [jnp.dot(modded, weights[i], preferred_element_type=F32) for i in range(3)]
+    mixed = [jnp.dot(modded, weights[i], preferred_element_type=F32) for i in range(2)]
+    copy.wait()
+    mixed.append(jnp.dot(modded, held[...], preferred_element_type=F32))
     put_partials(dims, out, staged, sems, *mixed, False, None)
 
 
@@ -356,7 +359,7 @@
 
 
 def attention(
-    dims, layer, sizes, gains, stale, arrived, attended, cache, block, fresh_rows, sems
+    dims, layer, sizes, gains, stale, arrived, attended, cache, fresh_rows, block, sems
 ):
     count = arrived.shape[0]
     turn = lax.axis_index("tok") // dims.pairs // dims.groups
@@ -524,28 +527,24 @@
             ]
         )
 
-    def fetch(cache, side):
-        copy = begin(cache, pieces.at[0], fetched)
-        pieces[1] = side[...]
-        return copy
-
     section = lax.axis_index("section")
 
     @pl.when(section == 0)
     def _():
-        fetching = fetch(first_cache, first_side)
+        copy = begin(first_cache, pieces.at[0], fetched)
+        pieces[1] = first_side[...]
+        copy.wait()
+        copy = begin(pieces, pair, sent)
         states = from_first(dims, both(made, back)).astype(BF16)
-        fetching.wait()
-        copy = begin(pieces, pair, sent)
         spread(states)
         copy.wait()
 
     @pl.when(section != 0)
     def _():
-        fetching = fetch(last_cache, last_side)
+        pieces[0] = last_cache[...]
+        pieces[1] = last_side[...]
+        copy = begin(pieces, pair, sent)
         states = output_rows(dims, sizes, mod, near, both(given, across), arrived)
-        fetching.wait()
-        copy = begin(pieces, pair, sent)
         spread(states)
         copy.wait()
 
@@ -696,10 +695,10 @@
     attended_shape = (
         Leaves(count, fold, 2 * group_width),
         Leaves(total, 2 * group_width),
+        Stays(total, 2 * group_width),
     )
     attended_scratch = [
         pltpu.VMEM((fold, 2 * group_width), BF16),
-        pltpu.VMEM((total, 2 * group_width), BF16),
         pltpu.SemaphoreType.DMA((count + 1,)),
     ]
     weights = w_qkv[0].transpose(1, 0, 2)
@@ -726,11 +725,11 @@
     sizes = jnp.concatenate([lengths, text_count])
     loaded_first = stage(
         working(0, load, False),
-        Stays(3, depth, local_width),
+        Stays(2, depth, local_width),
         0,
         weights_now,
         left=(0,),
-        scratch=[pltpu.SemaphoreType.DMA((3,))],
+        scratch=[pltpu.SemaphoreType.DMA((2,))],
         moved=4 * weights.size,
     )
     arrived = over_tok(blocks, 0)
@@ -745,8 +744,12 @@
         sizes,
         mod,
         loaded_first,
+        weights,
         arrived,
+        left=(3,),
         scratch=[
+            pltpu.VMEM((depth, local_width), BF16),
+            pltpu.SemaphoreType.DMA,
             pltpu.VMEM((count, height, 2 * group_width), BF16),
             pltpu.SemaphoreType.DMA((count,)),
         ],
@@ -763,8 +766,10 @@
         moved=4 * weights.size,
     )
     leaving = lax.dynamic_slice_in_dim(weights_now, (1 - side) * half_width, half_width, 2)
-
-    attended, cache_first = stage(
+    swapped_last = send(leaving, 1, 1, dt=1)
+    arrived, swapped_last = after(arrived, swapped_last)
+
+    attended, cache_first, _ = stage(
         working(0, attention, 0),
         attended_shape,
         1,
@@ -774,9 +779,7 @@
         arrived,
         scratch=attended_scratch,
     )
-    attended, leaving = after(attended, leaving)
     arrived = over_tok(attended, 0)
-    swapped_last = send(leaving, 1, 1, dt=1)
     made = stage(
         working(0, layer_rows),
         struct(live, depth),
@@ -814,7 +817,7 @@
     side_first = send(cache_first, 0, 0, dt=1)
     arrived, back, side_first = after(arrived, back, side_first)
 
-    attended, cache_last = stage(
+    attended, cache_last, kept_last = stage(
         working(1, attention, 1),
         attended_shape,
         1,
@@ -843,11 +846,11 @@
         given,
         across,
         cache_first,
-        cache_last,
+        kept_last,
         side_first,
         side_last,
         arrived,
-        left=(7, 8),
+        left=(7,),
         scratch=[
             pltpu.VMEM((count, rows, depth), BF16),
             pltpu.SemaphoreType.DMA((halves,)),

time: 102 us -> 102 us (level)
  waiting for transfers between devices: 32.9 us -> 38.1 us
  blocking collectives: 13.6 us -> 8.68 us
  local copies, waits for them, and re-layouts: 5.1 us -> 3.38 us
  starting transfers between devices: 33.6 us -> 34.9 us
    ppermute x8, waiting for transfers between devices: 11.8 us -> 21.8 us  [send(): return lax.ppermute(block, ('section', 'fsdp', 'tok'), ends)]
    all_to_all x4, waiting for transfers between devices: 15.5 us -> 9.91 us  [grouped(): lax.all_to_all(blocks, ('section', 'fsdp', 'tok'), 0, 0, axis_index_group...]
    all_to_all x1, blocking collectives: 13.6 us -> 8.68 us  [grouped(): lax.all_to_all(blocks, ('section', 'fsdp', 'tok'), 0, 0, axis_index_group...]
    unnamed x15 -> x11, local copies, waits for them, and re-layouts: 2.75 us -> 0.04 us
    ppermute x8, starting transfers between devices: 11.7 us -> 13 us  [send(): return lax.ppermute(block, ('section', 'fsdp', 'tok'), ends)]
  transfers between devices with their start and end apart: 14 -> 14, of which waited for: 10 -> 10; matrix products, arithmetic and copies ran while one was open for 2% -> 3% of each run, Pallas kernels for 2% -> 1%
where the time goes in v2:
time: 102 us; the launch traced here: 101 us
  waiting for transfers between devices  38.1 us (37%)
  starting transfers between devices  34.9 us (34%)
  Pallas kernels  13.7 us (13%)
  blocking collectives  8.68 us (9%)
  local copies, waits for them, and re-layouts  3.38 us (3%)
  between operations  2.26 us (2%)
    ppermute x8, waiting for transfers between devices, send(): return lax.ppermute(block, ('section', 'fsdp', 'tok'), ends)  21.8 us
    all_to_all x4, starting transfers between devices, grouped(): lax.all_to_all(blocks, ('section', 'fsdp', 'tok'), 0, 0, axis_index_group...  15.7 us
    pallas_call x10, Pallas kernels, stage(): pl.pallas_call(body, out_shape=outs, in_specs=[pl.BlockSpec(memory_space=...  13.7 us
    ppermute x8, starting transfers between devices, send(): return lax.ppermute(block, ('section', 'fsdp', 'tok'), ends)  13 us
    all_to_all x4, waiting for transfers between devices, grouped(): lax.all_to_all(blocks, ('section', 'fsdp', 'tok'), 0, 0, axis_index_group...  9.91 us
    all_to_all x1, blocking collectives, grouped(): lax.all_to_all(blocks, ('section', 'fsdp', 'tok'), 0, 0, axis_index_group...  8.68 us
    ppermute x1, waiting for transfers between devices, by_kernels(): other = lax.ppermute(pair, 'tok', [(t, t ^ pairs) for t in range(count)])  5.46 us
    all_to_all x1, starting transfers between devices, all_devices(): return lax.all_to_all(blocks, ('fsdp', 'tok'), 0, 0, tiled=False)  4.81 us
  transfers between devices with their start and end apart: 14, of which 10 were waited for; matrix products, arithmetic and copies ran while one was open for 3% of the time, Pallas kernels for 1%

profile of v2, /device:TPU:1, one launch (start us, length us, event | category | flops | bytes accessed | tf_op | source)
XLA Modules:
  0.0 101.1 jit_solution(5305072326482036187)
XLA Ops:
  0.7 1.9 %shard_map.104 = bf16[8,16,512]{2,1,0:T(8,128)(2,1)} custom-call(bf16[4,4,3072]{2,1,0:T(4,128)(2,1)} %hidden.1), custom_call_target="tpu_custom_call" | custom-call | tf_op jit(solution)/shard_map/pallas_call | solution.py:611
  2.6 5.3 %all-to-all-start = ((bf16[8,16,512]{2,1,0:T(8,128)(2,1)}), bf16[8,16,512]{2,1,0:T(8,128)(2,1)S(1)}, u32[]{:S(2)}, u32[]{:S(2)}) async-start(bf16[8,16,512]{2,1,0:T(8,128)(2,1)} %shard_map.104), calls=%async_computation | async-start | bytes 262144 | tf_op jit(solution)/shard_map/all_to_all | solution.py:666
  9.2 1.0 constant_dynamic-slice_fusion.2
  10.3 2.7 %all-to-all-done.refs_4_ = bf16[8,16,512]{2,1,0:T(8,128)(2,1)S(1)} async-done(((bf16[8,16,512]{2,1,0:T(8,128)(2,1)}), bf16[8,16,512]{2,1,0:T(8,128)(2,1)S(1)}, u32[]{:S(2)}, u32[]{:S(2)}) %all-to-all-start) | async-done | bytes 131104 | tf_op jit(solution)/shard_map/all_to_all | solution.py:666
  13.6 3.6 %all-to-all-start.1 = ((bf16[8,120,384]{2,1,0:T(8,128)(2,1)}), bf16[8,120,384]{2,1,0:T(8,128)(2,1)S(1)}, u32[]{:S(2)}, u32[]{:S(2)}) async-start(bf16[8,120,384]{2,1,0:T(8,128)(2,1)} %get-tuple-element.38), calls=%async_computation.1 | async-start | bytes 1474560 | tf_op jit(solution)/shard_map/all_to_all | solution.py:666
  17.2 2.3 %constant_dynamic-slice_fusion.1 = bf16[3,384,384]{2,1,0:T(8,128)(2,1)} fusion(bf16[3,384,768]{2,1,0:T(8,128)(2,1)} %bitcast.25, s32[]{:T(128)S(6)} %select_n.31), kind=kLoop, calls=%fused_computation.2 | loop fusion | bytes 1769476 | tf_op jit(solution)/shard_map/dynamic_slice | solution.py:768
  19.5 3.2 %collective-permute-start = (bf16[3,384,384]{2,1,0:T(8,128)(2,1)}, bf16[3,384,384]{2,1,0:T(8,128)(2,1)S(1)}, u32[]{:S(2)}, u32[]{:S(2)}) collective-permute-start(bf16[3,384,384]{2,1,0:T(8,128)(2,1)} %constant_dynamic-slice_fusion.1), channel_id=1, source_target_pairs={{16,17},{17,16},{18,19},{19,18},{20,21},{21,20},{22,23},{23,22},{2... | collective-permute-start | bytes 2654216 | tf_op jit(solution)/shard_map/ppermute | solution.py:658
  22.9 15.5 %collective-permute-done.refs_3_ = bf16[3,384,384]{2,1,0:T(8,128)(2,1)S(1)} collective-permute-done((bf16[3,384,384]{2,1,0:T(8,128)(2,1)}, bf16[3,384,384]{2,1,0:T(8,128)(2,1)S(1)}, u32[]{:S(2)}, u32[]{:S(2)}) %collective-permute-start) | collective-permute-done | bytes 884768 | tf_op jit(solution)/shard_map/ppermute | solution.py:658
  38.4 1.3 %shard_map.108 = (bf16[8,24,384]{2,1,0:T(8,128)(2,1)}, bf16[128,384]{1,0:T(8,128)(2,1)}, bf16[128,384]{1,0:T(8,128)(2,1)}) custom-call(s32[5]{0:T(128)S(1)} %pad_add_fusion.refs_0_.sizes, f32[2,64]{1,0:T(2,128)S(1)} %bitcast.21, bf16[2,128,192]{2,1,0:T(8,128)(2,1)S(1)} %constant_dynamic-slice_fusion.refs_2_, bf16[8,120,384]{2,1,0:T(8,128)(2,1)S(1)} %all-to-all-done.1.refs_3_), custom_call_target="tpu_custom_call" | custom-call | tf_op jit(solution)/shard_map/pallas_call | solution.py:611
  39.7 8.7 %all_to_all.30.refs_4_ = bf16[8,24,384]{2,1,0:T(8,128)(2,1)S(1)} all-to-all(bf16[8,24,384]{2,1,0:T(8,128)(2,1)} %get-tuple-element.42), channel_id=1, replica_groups={{0,1,2,3,4,5,6,7},{8,9,10,11,12,13,14,15},{16,17,18,19,24,25,26,27},{20..., dimensions={0} | all-to-all | bytes 294912 | tf_op jit(solution)/shard_map/all_to_all | solution.py:666
  48.9 1.3 %collective-permute-start.1 = (bf16[96,384]{1,0:T(8,128)(2,1)S(1)}, bf16[96,384]{1,0:T(8,128)(2,1)S(1)}, u32[]{:S(2)}, u32[]{:S(2)}) collective-permute-start(bf16[96,384]{1,0:T(8,128)(2,1)S(1)} %shard_map.109.made), channel_id=1, source_target_pairs={{0,25},{1,24},{2,27},{3,26},{4,29},{5,28},{6,31},{7,30},{8,17},{9,... | collective-permute-start | bytes 221192 | tf_op jit(solution)/shard_map/ppermute | solution.py:658
  50.2 1.3 %collective-permute-start.2 = (bf16[96,384]{1,0:T(8,128)(2,1)S(1)}, bf16[96,384]{1,0:T(8,128)(2,1)S(1)}, u32[]{:S(2)}, u32[]{:S(2)}) collective-permute-start(bf16[96,384]{1,0:T(8,128)(2,1)S(1)} %shard_map.109.made), channel_id=1, source_target_pairs={{0,17},{1,16},{2,19},{3,18},{4,21},{5,20},{6,23},{7,22},{8,25},{9,... | collective-permute-start | bytes 221192 | tf_op jit(solution)/shard_map/ppermute | solution.py:658
  51.5 1.3 %collective-permute-start.3 = (bf16[96,384]{1,0:T(8,128)(2,1)S(1)}, bf16[96,384]{1,0:T(8,128)(2,1)S(1)}, u32[]{:S(2)}, u32[]{:S(2)}) collective-permute-start(bf16[96,384]{1,0:T(8,128)(2,1)S(1)} %shard_map.109.made), channel_id=1, source_target_pairs={{0,24},{1,25},{2,26},{3,27},{4,28},{5,29},{6,30},{7,31},{8,16},{9,... | collective-permute-start | bytes 221192 | tf_op jit(solution)/shard_map/ppermute | solution.py:658
  52.8 1.3 %collective-permute-start.4 = (bf16[96,384]{1,0:T(8,128)(2,1)S(1)}, bf16[96,384]{1,0:T(8,128)(2,1)S(1)}, u32[]{:S(2)}, u32[]{:S(2)}) collective-permute-start(bf16[96,384]{1,0:T(8,128)(2,1)S(1)} %shard_map.109.made), channel_id=1, source_target_pairs={{0,16},{1,17},{2,18},{3,19},{4,20},{5,21},{6,22},{7,23},{8,24},{9,... | collective-permute-start | bytes 221192 | tf_op jit(solution)/shard_map/ppermute | solution.py:658
  54.1 1.2 %shard_map.107.refs_2_ = bf16[3,384,384]{2,1,0:T(8,128)(2,1)S(1)} custom-call(bf16[3,384,768]{2,1,0:T(8,128)(2,1)} %bitcast.26), custom_call_target="tpu_custom_call" | custom-call | bytes 3538944 | tf_op jit(solution)/shard_map/pallas_call | solution.py:611
  55.3 1.0 collective-permute-done.1.refs_4_
  56.3 0.8 collective-permute-done.2.refs_5_
  57.1 2.2 %collective-permute-done.3.refs_6_.across = bf16[96,384]{1,0:T(8,128)(2,1)S(1)} collective-permute-done((bf16[96,384]{1,0:T(8,128)(2,1)S(1)}, bf16[96,384]{1,0:T(8,128)(2,1)S(1)}, u32[]{:S(2)}, u32[]{:S(2)}) %collective-permute-start.3) | collective-permute-done | bytes 73760 | tf_op jit(solution)/shard_map/ppermute | solution.py:658
  59.3 2.2 %shard_map.110 = bf16[4,136,384]{2,1,0:T(8,128)(2,1)} custom-call(s32[5]{0:T(128)S(1)} %pad_add_fusion.refs_0_.sizes, bf16[6,768]{1,0:T(8,128)(2,1)S(1)} %bitcast.19, bf16[3,384,384]{2,1,0:T(8,128)(2,1)S(1)} %shard_map.107.refs_2_, bf16[3,384,384]{2,1,0:T(8,128)(2,1)S(1)} %collective-permute-done.refs_3_, ...), custom_call_target="tpu_custom_call" | custom-call | tf_op jit(solution)/shard_map/pallas_call | solution.py:611
  61.5 3.5 %all-to-all-start.3 = ((bf16[4,136,384]{2,1,0:T(8,128)(2,1)}), bf16[4,136,384]{2,1,0:T(8,128)(2,1)S(1)}, u32[]{:S(2)}, u32[]{:S(2)}) async-start(bf16[4,136,384]{2,1,0:T(8,128)(2,1)} %shard_map.110), calls=%async_computation.3 | async-start | bytes 835584 | tf_op jit(solution)/shard_map/all_to_all | solution.py:666
  65.0 0.7 collective-permute-start.6
  66.4 6.6 %all-to-all-done.3.refs_3_ = bf16[4,136,384]{2,1,0:T(8,128)(2,1)S(1)} async-done(((bf16[4,136,384]{2,1,0:T(8,128)(2,1)}), bf16[4,136,384]{2,1,0:T(8,128)(2,1)S(1)}, u32[]{:S(2)}, u32[]{:S(2)}) %all-to-all-start.3) | async-done | bytes 417824 | tf_op jit(solution)/shard_map/all_to_all | solution.py:666
  73.0 3.1 %shard_map.111 = (bf16[8,24,384]{2,1,0:T(8,128)(2,1)}, bf16[128,384]{1,0:T(8,128)(2,1)}, bf16[128,384]{1,0:T(8,128)(2,1)S(1)}) custom-call(s32[5]{0:T(128)S(1)} %pad_add_fusion.refs_0_.sizes, f32[2,64]{1,0:T(2,128)S(1)} %bitcast.22, bf16[2,128,192]{2,1,0:T(8,128)(2,1)S(1)} %constant_dynamic-slice_fusion.refs_2_, bf16[4,136,384]{2,1,0:T(8,128)(2,1)S(1)} %all-to-all-done.3.refs_3_), custom_call_target="tpu_custom_call" | custom-call | tf_op jit(solution)/shard_map/pallas_call | solution.py:611
  76.1 3.4 %all-to-all-start.4 = ((bf16[8,24,384]{2,1,0:T(8,128)(2,1)}), bf16[8,24,384]{2,1,0:T(8,128)(2,1)S(1)}, u32[]{:S(2)}, u32[]{:S(2)}) async-start(bf16[8,24,384]{2,1,0:T(8,128)(2,1)} %get-tuple-element.51), calls=%async_computation.4 | async-start | bytes 294912 | tf_op jit(solution)/shard_map/all_to_all | solution.py:666
  79.5 3.3 %collective-permute-start.7 = (bf16[128,384]{1,0:T(8,128)(2,1)}, bf16[128,384]{1,0:T(8,128)(2,1)S(1)}, u32[]{:S(2)}, u32[]{:S(2)}) collective-permute-start(bf16[128,384]{1,0:T(8,128)(2,1)} %get-tuple-element.52), channel_id=1, source_target_pairs={{16,17},{17,16},{18,19},{19,18},{20,21},{21,20},{22,23},{23,22},{2... | collective-permute-start | bytes 294920 | tf_op jit(solution)/shard_map/ppermute | solution.py:658
  82.8 2.3 %collective-permute-done.7.last_side = bf16[128,384]{1,0:T(8,128)(2,1)S(1)} collective-permute-done((bf16[128,384]{1,0:T(8,128)(2,1)}, bf16[128,384]{1,0:T(8,128)(2,1)S(1)}, u32[]{:S(2)}, u32[]{:S(2)}) %collective-permute-start.7) | collective-permute-done | bytes 98336 | tf_op jit(solution)/shard_map/ppermute | solution.py:658
  85.7 1.8 %shard_map.112 = (bf16[16,16,384]{2,1,0:T(8,128)(2,1)}, bf16[2,128,384]{2,1,0:T(8,128)(2,1)}, bf16[2,128,384]{2,1,0:T(8,128)(2,1)S(1)}) custom-call(s32[5]{0:T(128)S(1)} %pad_add_fusion.refs_0_.sizes, bf16[6,768]{1,0:T(8,128)(2,1)S(1)} %bitcast.20, bf16[384,768]{1,0:T(8,128)(2,1)S(1)} %bitcast.16, bf16[96,384]{1,0:T(8,128)(2,1)S(1)} %shard_map.109.made, ...), custom_call_target="tpu_custom_call" | custom-call | tf_op jit(solution)/shard_map/pallas_call | solution.py:611
  87.5 4.8 %all-to-all-start.5 = ((bf16[16,16,384]{2,1,0:T(8,128)(2,1)}), bf16[16,16,384]{2,1,0:T(8,128)(2,1)S(1)}, u32[]{:S(2)}, u32[]{:S(2)}) async-start(bf16[16,16,384]{2,1,0:T(8,128)(2,1)} %get-tuple-element.55), calls=%async_computation.5 | async-start | bytes 393216 | tf_op jit(solution)/shard_map/all_to_all | solution.py:689
  92.4 1.4 %collective-permute-start.8 = (bf16[2,128,384]{2,1,0:T(8,128)(2,1)}, bf16[2,128,384]{2,1,0:T(8,128)(2,1)S(1)}, u32[]{:S(2)}, u32[]{:S(2)}) collective-permute-start(bf16[2,128,384]{2,1,0:T(8,128)(2,1)} %get-tuple-element.57), channel_id=1, source_target_pairs={{0,2},{1,3},{2,0},{3,1},{4,6},{5,7},{6,4},{7,5},{8,10},{9,11},{10,... | collective-permute-start | bytes 589832 | tf_op jit(solution)/shard_map/ppermute | solution.py:862
  93.7 5.5 %collective-permute-done.8.other = bf16[2,128,384]{2,1,0:T(8,128)(2,1)S(1)} collective-permute-done((bf16[2,128,384]{2,1,0:T(8,128)(2,1)}, bf16[2,128,384]{2,1,0:T(8,128)(2,1)S(1)}, u32[]{:S(2)}, u32[]{:S(2)}) %collective-permute-start.8) | collective-permute-done | bytes 196640 | tf_op jit(solution)/shard_map/ppermute | solution.py:862
  99.2 0.9 all-to-all-done.5.arrived
  100.1 1.0 shard_map.113
  (22 shorter events, 2.8 us)
Async XLA Ops:
  0.6 22.1 %copy-start = (bf16[1,2,4,32,768]{4,3,2,1,0:T(8,128)(2,1)S(1)}, bf16[1,2,4,32,768]{4,3,2,1,0:T(8,128)(2,1)}, u32[]{:S(2)}) copy-start(bf16[1,2,4,32,768]{4,3,2,1,0:T(8,128)(2,1)} %param.17) | copy-start | bytes 1179652
  0.6 9.6 %copy-start.4 = (s32[4]{0:T(128)S(1)}, s32[4]{0:T(128)}, u32[]{:S(2)}) copy-start(s32[4]{0:T(128)} %param.10) | copy-start | bytes 52
  2.6 10.4 %all-to-all-start = ((bf16[8,16,512]{2,1,0:T(8,128)(2,1)}), bf16[8,16,512]{2,1,0:T(8,128)(2,1)S(1)}, u32[]{:S(2)}, u32[]{:S(2)}) async-start(bf16[8,16,512]{2,1,0:T(8,128)(2,1)} %shard_map.104), calls=%async_computation | async-start | bytes 262144 | tf_op jit(solution)/shard_map/all_to_all | solution.py:666
  13.6 24.8 %copy-start.2 = (f32[1,2,64]{2,1,0:T(2,128)S(1)}, f32[1,2,64]{2,1,0:T(2,128)}, u32[]{:S(2)}) copy-start(f32[1,2,64]{2,1,0:T(2,128)} %param.16) | copy-start | bytes 1540
  13.6 24.8 %all-to-all-start.1 = ((bf16[8,120,384]{2,1,0:T(8,128)(2,1)}), bf16[8,120,384]{2,1,0:T(8,128)(2,1)S(1)}, u32[]{:S(2)}, u32[]{:S(2)}) async-start(bf16[8,120,384]{2,1,0:T(8,128)(2,1)} %get-tuple-element.38), calls=%async_computation.1 | async-start | bytes 1474560 | tf_op jit(solution)/shard_map/all_to_all | solution.py:666
  17.2 31.2 %copy-start.1 = (bf16[1,384,768]{2,1,0:T(8,128)(2,1)S(1)}, bf16[1,384,768]{2,1,0:T(8,128)(2,1)}, u32[]{:S(2)}) copy-start(bf16[1,384,768]{2,1,0:T(8,128)(2,1)} %param.15) | copy-start | bytes 1769476
  19.5 18.9 %collective-permute-start = (bf16[3,384,384]{2,1,0:T(8,128)(2,1)}, bf16[3,384,384]{2,1,0:T(8,128)(2,1)S(1)}, u32[]{:S(2)}, u32[]{:S(2)}) collective-permute-start(bf16[3,384,384]{2,1,0:T(8,128)(2,1)} %constant_dynamic-slice_fusion.1), channel_id=1, source_target_pairs={{16,17},{17,16},{18,19},{19,18},{20,21},{21,20},{22,23},{23,22},{2... | collective-permute-start | bytes 2654216 | tf_op jit(solution)/shard_map/ppermute | solution.py:658
  48.9 7.4 %collective-permute-start.1 = (bf16[96,384]{1,0:T(8,128)(2,1)S(1)}, bf16[96,384]{1,0:T(8,128)(2,1)S(1)}, u32[]{:S(2)}, u32[]{:S(2)}) collective-permute-start(bf16[96,384]{1,0:T(8,128)(2,1)S(1)} %shard_map.109.made), channel_id=1, source_target_pairs={{0,25},{1,24},{2,27},{3,26},{4,29},{5,28},{6,31},{7,30},{8,17},{9,... | collective-permute-start | bytes 221192 | tf_op jit(solution)/shard_map/ppermute | solution.py:658
  50.2 6.8 %collective-permute-start.2 = (bf16[96,384]{1,0:T(8,128)(2,1)S(1)}, bf16[96,384]{1,0:T(8,128)(2,1)S(1)}, u32[]{:S(2)}, u32[]{:S(2)}) collective-permute-start(bf16[96,384]{1,0:T(8,128)(2,1)S(1)} %shard_map.109.made), channel_id=1, source_target_pairs={{0,17},{1,16},{2,19},{3,18},{4,21},{5,20},{6,23},{7,22},{8,25},{9,... | collective-permute-start | bytes 221192 | tf_op jit(solution)/shard_map/ppermute | solution.py:658
  51.5 7.8 %collective-permute-start.3 = (bf16[96,384]{1,0:T(8,128)(2,1)S(1)}, bf16[96,384]{1,0:T(8,128)(2,1)S(1)}, u32[]{:S(2)}, u32[]{:S(2)}) collective-permute-start(bf16[96,384]{1,0:T(8,128)(2,1)S(1)} %shard_map.109.made), channel_id=1, source_target_pairs={{0,24},{1,25},{2,26},{3,27},{4,28},{5,29},{6,30},{7,31},{8,16},{9,... | collective-permute-start | bytes 221192 | tf_op jit(solution)/shard_map/ppermute | solution.py:658
  52.8 6.5 %collective-permute-start.4 = (bf16[96,384]{1,0:T(8,128)(2,1)S(1)}, bf16[96,384]{1,0:T(8,128)(2,1)S(1)}, u32[]{:S(2)}, u32[]{:S(2)}) collective-permute-start(bf16[96,384]{1,0:T(8,128)(2,1)S(1)} %shard_map.109.made), channel_id=1, source_target_pairs={{0,16},{1,17},{2,18},{3,19},{4,20},{5,21},{6,22},{7,23},{8,24},{9,... | collective-permute-start | bytes 221192 | tf_op jit(solution)/shard_map/ppermute | solution.py:658
  55.3 9.7 %copy-start.3 = (bf16[128,384]{1,0:T(8,128)(2,1)S(1)}, bf16[128,384]{1,0:T(8,128)(2,1)}, u32[]{:S(2)}) copy-start(bf16[128,384]{1,0:T(8,128)(2,1)} %get-tuple-element.46.first_cache) | copy-start | bytes 294916
  61.5 11.4 %all-to-all-start.3 = ((bf16[4,136,384]{2,1,0:T(8,128)(2,1)}), bf16[4,136,384]{2,1,0:T(8,128)(2,1)S(1)}, u32[]{:S(2)}, u32[]{:S(2)}) async-start(bf16[4,136,384]{2,1,0:T(8,128)(2,1)} %shard_map.110), calls=%async_computation.3 | async-start | bytes 835584 | tf_op jit(solution)/shard_map/all_to_all | solution.py:666
  65.0 1.4 %collective-permute-start.6 = (bf16[128,384]{1,0:T(8,128)(2,1)S(1)}, bf16[128,384]{1,0:T(8,128)(2,1)S(1)}, u32[]{:S(2)}, u32[]{:S(2)}) collective-permute-start(bf16[128,384]{1,0:T(8,128)(2,1)S(1)} %copy-done.3), channel_id=1, source_target_pairs={{0,1},{1,0},{2,3},{3,2},{4,5},{5,4},{6,7},{7,6},{8,9},{9,8},{10,11... | collective-permute-start | bytes 294920 | tf_op jit(solution)/shard_map/ppermute | solution.py:658
  65.7 0.7 collective-permute-start.5
  76.1 9.6 %all-to-all-start.4 = ((bf16[8,24,384]{2,1,0:T(8,128)(2,1)}), bf16[8,24,384]{2,1,0:T(8,128)(2,1)S(1)}, u32[]{:S(2)}, u32[]{:S(2)}) async-start(bf16[8,24,384]{2,1,0:T(8,128)(2,1)} %get-tuple-element.51), calls=%async_computation.4 | async-start | bytes 294912 | tf_op jit(solution)/shard_map/all_to_all | solution.py:666
  79.5 5.6 %collective-permute-start.7 = (bf16[128,384]{1,0:T(8,128)(2,1)}, bf16[128,384]{1,0:T(8,128)(2,1)S(1)}, u32[]{:S(2)}, u32[]{:S(2)}) collective-permute-start(bf16[128,384]{1,0:T(8,128)(2,1)} %get-tuple-element.52), channel_id=1, source_target_pairs={{16,17},{17,16},{18,19},{19,18},{20,21},{21,20},{22,23},{23,22},{2... | collective-permute-start | bytes 294920 | tf_op jit(solution)/shard_map/ppermute | solution.py:658
  87.5 12.5 %all-to-all-start.5 = ((bf16[16,16,384]{2,1,0:T(8,128)(2,1)}), bf16[16,16,384]{2,1,0:T(8,128)(2,1)S(1)}, u32[]{:S(2)}, u32[]{:S(2)}) async-start(bf16[16,16,384]{2,1,0:T(8,128)(2,1)} %get-tuple-element.55), calls=%async_computation.5 | async-start | bytes 393216 | tf_op jit(solution)/shard_map/all_to_all | solution.py:689
  92.4 6.8 %collective-permute-start.8 = (bf16[2,128,384]{2,1,0:T(8,128)(2,1)}, bf16[2,128,384]{2,1,0:T(8,128)(2,1)S(1)}, u32[]{:S(2)}, u32[]{:S(2)}) collective-permute-start(bf16[2,128,384]{2,1,0:T(8,128)(2,1)} %get-tuple-element.57), channel_id=1, source_target_pairs={{0,2},{1,3},{2,0},{3,1},{4,6},{5,7},{6,4},{7,5},{8,10},{9,11},{10,... | collective-permute-start | bytes 589832 | tf_op jit(solution)/shard_map/ppermute | solution.py:862

commit v3 on v2

--- a/solution.py
+++ b/solution.py
@@ -271,29 +271,35 @@
     live, width, groups, turns = dims.live, dims.group_width, dims.groups, dims.turns
     share = live // turns
     fold = share // 2
-    sides = query.shape[1] // (groups * width)
+    sides = key.shape[1] // (groups * width)
     copies = []
+    places = [
+        (g, h, (h * groups + g % groups) * sides + g // groups)
+        for g in range(sides * groups)
+        for h in range(turns)
+    ]
     for g in range(sides * groups):
         cut = slice(g * width, (g + 1) * width)
         pair = jnp.concatenate([key[:live, cut], value[:live, cut]], axis=1).astype(BF16)
+        for other, h, at in places:
+            if other == g:
+                staged[at, :live, :] = pair
+    query = query()
+    for g, h, at in places:
+        cut = slice(g * width, (g + 1) * width)
+        part = query[h * share : (h + 1) * share, cut]
+        rows = [jnp.concatenate([part[:fold], part[fold:]], axis=1)]
         if extra:
             last = query[live : live + 4, cut]
-            rest = [
+            rows += [
                 jnp.concatenate([key[live : live + 4, cut], value[live : live + 4, cut]], axis=1),
                 jnp.concatenate([last, jnp.zeros_like(last)], axis=1),
             ]
-        else:
-            rest = []
-        for h in range(turns):
-            part = query[h * share : (h + 1) * share, cut]
-            rows = [jnp.concatenate([part[:fold], part[fold:]], axis=1)] + rest
-            at = (h * groups + g % groups) * sides + g // groups
-            staged[at, :live, :] = pair
-            rows = jnp.concatenate(rows, axis=0)
-            staged[at, live : live + rows.shape[0], :] = rows.astype(BF16)
-            if extra:
-                staged[at, live + fold + 8 :, :] = stats
-            copies.append(begin(staged.at[at], out.at[at], sems.at[at]))
+        rows = jnp.concatenate(rows, axis=0)
+        staged[at, live : live + rows.shape[0], :] = rows.astype(BF16)
+        if extra:
+            staged[at, live + fold + 8 :, :] = stats
+        copies.append(begin(staged.at[at], out.at[at], sems.at[at]))
     finish(copies)
 
 
@@ -303,21 +309,21 @@
     return jnp.where(second, right, left), jnp.where(second, left, right)
 
 
-def load(dims, side, weights, out, sems):
+def load(dims, side, first, weights, out, sems):
     columns = out.shape[2]
     start = pl.multiple_of(lax.axis_index("tok") % dims.pairs * columns, 128) if side else 0
     finish(
         [
-            begin(weights.at[i, :, pl.ds(start, columns)], out.at[i], sems.at[i])
+            begin(weights.at[first + i, :, pl.ds(start, columns)], out.at[i], sems.at[i])
             for i in range(out.shape[0])
         ]
     )
 
 
 def first_partials(
-    dims, sizes, mod, weights, values, arrived, kept_states, out, held, sem, staged, sems
+    dims, sizes, mod, weights, queries, arrived, kept_states, out, held, sem, staged, sems
 ):
-    copy = begin(values.at[2], held, sem)
+    copy = begin(queries.at[0], held, sem)
     patch, slot = slots_by_device((1, dims.total), 1, dims.cap_dev, dims.patches)
     position = positions(sizes, patch, slot, dims.patches)
     pick = (iota((dims.live, dims.total), 0) == position).astype(F32).astype(BF16)
@@ -330,9 +336,12 @@
     modded = ((states - mean) * inverse * (1.0 + scale) + shift).astype(BF16)
     kept_states[...] = states.astype(BF16)
     mixed = [jnp.dot(modded, weights[i], preferred_element_type=F32) for i in range(2)]
-    copy.wait()
-    mixed.append(jnp.dot(modded, held[...], preferred_element_type=F32))
-    put_partials(dims, out, staged, sems, *mixed, False, None)
+
+    def query():
+        copy.wait()
+        return jnp.dot(modded, held[...], preferred_element_type=F32)
+
+    put_partials(dims, out, staged, sems, query, *mixed, False, None)
 
 
 def head_means(values, blocks, terms):
@@ -507,7 +516,7 @@
         + jnp.dot(left[:, dims.depth :], swapped[i], preferred_element_type=F32)
         for i in range(3)
     ]
-    put_partials(dims, out, staged, sems, *mixed, True, stats)
+    put_partials(dims, out, staged, sems, lambda: mixed[0], *mixed[1:], True, stats)
 
 
 def last_rows(
@@ -695,8 +704,8 @@
     attended_shape = (
         Leaves(count, fold, 2 * group_width),
         Leaves(total, 2 * group_width),
-        Stays(total, 2 * group_width),
-    )
+    )
+    kept_rows = (total, 2 * group_width)
     attended_scratch = [
         pltpu.VMEM((fold, 2 * group_width), BF16),
         pltpu.SemaphoreType.DMA((count + 1,)),
@@ -724,7 +733,7 @@
     )
     sizes = jnp.concatenate([lengths, text_count])
     loaded_first = stage(
-        working(0, load, False),
+        working(0, load, False, 1),
         Stays(2, depth, local_width),
         0,
         weights_now,
@@ -757,7 +766,7 @@
     blocks, weights_now = after(blocks, weights)
     arrived = over_tok(blocks, 0)
     loaded_last = stage(
-        working(1, load, True),
+        working(1, load, True, 0),
         Stays(3, depth, half_width),
         0,
         weights_now,
@@ -769,7 +778,7 @@
     swapped_last = send(leaving, 1, 1, dt=1)
     arrived, swapped_last = after(arrived, swapped_last)
 
-    attended, cache_first, _ = stage(
+    attended, cache_first = stage(
         working(0, attention, 0),
         attended_shape,
         1,
@@ -777,7 +786,7 @@
         gains,
         stale,
         arrived,
-        scratch=attended_scratch,
+        scratch=[pltpu.VMEM(kept_rows, BF16)] + attended_scratch,
     )
     arrived = over_tok(attended, 0)
     made = stage(
@@ -819,7 +828,7 @@
 
     attended, cache_last, kept_last = stage(
         working(1, attention, 1),
-        attended_shape,
+        attended_shape + (Stays(*kept_rows),),
         1,
         sizes,
         gains,

time: 102 us -> 101 us (level)
  no operation moved by 1% of the time
where the time goes in v3:
time: 101 us; the launch traced here: 100 us
  waiting for transfers between devices  37.8 us (37%)
  starting transfers between devices  34.9 us (35%)
  Pallas kernels  13 us (13%)
  blocking collectives  8.99 us (9%)
  local copies, waits for them, and re-layouts  3.38 us (3%)
  between operations  2.26 us (2%)
    ppermute x8, waiting for transfers between devices, send(): return lax.ppermute(block, ('section', 'fsdp', 'tok'), ends)  21.5 us
    all_to_all x4, starting transfers between devices, grouped(): lax.all_to_all(blocks, ('section', 'fsdp', 'tok'), 0, 0, axis_index_group...  15.7 us
    pallas_call x10, Pallas kernels, stage(): pl.pallas_call(body, out_shape=outs, in_specs=[pl.BlockSpec(memory_space=...  13 us
    ppermute x8, starting transfers between devices, send(): return lax.ppermute(block, ('section', 'fsdp', 'tok'), ends)  13 us
    all_to_all x4, waiting for transfers between devices, grouped(): lax.all_to_all(blocks, ('section', 'fsdp', 'tok'), 0, 0, axis_index_group...  9.91 us
    all_to_all x1, blocking collectives, grouped(): lax.all_to_all(blocks, ('section', 'fsdp', 'tok'), 0, 0, axis_index_group...  8.99 us
    ppermute x1, waiting for transfers between devices, by_kernels(): other = lax.ppermute(pair, 'tok', [(t, t ^ pairs) for t in range(count)])  5.47 us
    all_to_all x1, starting transfers between devices, all_devices(): return lax.all_to_all(blocks, ('fsdp', 'tok'), 0, 0, tiled=False)  4.81 us
  transfers between devices with their start and end apart: 14, of which 10 were waited for; matrix products, arithmetic and copies ran while one was open for 3% of the time, Pallas kernels for 1%

profile of v3, /device:TPU:1, one launch (start us, length us, event | category | flops | bytes accessed | tf_op | source)
XLA Modules:
  0.0 100.4 jit_solution(10495876676169976572)
XLA Ops:
  0.7 1.9 %shard_map.104 = bf16[8,16,512]{2,1,0:T(8,128)(2,1)} custom-call(bf16[4,4,3072]{2,1,0:T(4,128)(2,1)} %hidden.1), custom_call_target="tpu_custom_call" | custom-call | tf_op jit(solution)/shard_map/pallas_call | solution.py:620
  2.6 5.3 %all-to-all-start = ((bf16[8,16,512]{2,1,0:T(8,128)(2,1)}), bf16[8,16,512]{2,1,0:T(8,128)(2,1)S(1)}, u32[]{:S(2)}, u32[]{:S(2)}) async-start(bf16[8,16,512]{2,1,0:T(8,128)(2,1)} %shard_map.104), calls=%async_computation | async-start | bytes 262144 | tf_op jit(solution)/shard_map/all_to_all | solution.py:675
  9.2 1.0 constant_dynamic-slice_fusion.2
  10.3 2.7 %all-to-all-done.refs_4_ = bf16[8,16,512]{2,1,0:T(8,128)(2,1)S(1)} async-done(((bf16[8,16,512]{2,1,0:T(8,128)(2,1)}), bf16[8,16,512]{2,1,0:T(8,128)(2,1)S(1)}, u32[]{:S(2)}, u32[]{:S(2)}) %all-to-all-start) | async-done | bytes 131104 | tf_op jit(solution)/shard_map/all_to_all | solution.py:675
  13.6 3.6 %all-to-all-start.1 = ((bf16[8,120,384]{2,1,0:T(8,128)(2,1)}), bf16[8,120,384]{2,1,0:T(8,128)(2,1)S(1)}, u32[]{:S(2)}, u32[]{:S(2)}) async-start(bf16[8,120,384]{2,1,0:T(8,128)(2,1)} %get-tuple-element.38), calls=%async_computation.1 | async-start | bytes 1474560 | tf_op jit(solution)/shard_map/all_to_all | solution.py:675
  17.2 2.3 %constant_dynamic-slice_fusion.1 = bf16[3,384,384]{2,1,0:T(8,128)(2,1)} fusion(bf16[3,384,768]{2,1,0:T(8,128)(2,1)} %bitcast.25, s32[]{:T(128)S(6)} %select_n.31), kind=kLoop, calls=%fused_computation.2 | loop fusion | bytes 1769476 | tf_op jit(solution)/shard_map/dynamic_slice | solution.py:777
  19.5 3.2 %collective-permute-start = (bf16[3,384,384]{2,1,0:T(8,128)(2,1)}, bf16[3,384,384]{2,1,0:T(8,128)(2,1)S(1)}, u32[]{:S(2)}, u32[]{:S(2)}) collective-permute-start(bf16[3,384,384]{2,1,0:T(8,128)(2,1)} %constant_dynamic-slice_fusion.1), channel_id=1, source_target_pairs={{16,17},{17,16},{18,19},{19,18},{20,21},{21,20},{22,23},{23,22},{2... | collective-permute-start | bytes 2654216 | tf_op jit(solution)/shard_map/ppermute | solution.py:667
  22.9 15.5 %collective-permute-done.refs_3_ = bf16[3,384,384]{2,1,0:T(8,128)(2,1)S(1)} collective-permute-done((bf16[3,384,384]{2,1,0:T(8,128)(2,1)}, bf16[3,384,384]{2,1,0:T(8,128)(2,1)S(1)}, u32[]{:S(2)}, u32[]{:S(2)}) %collective-permute-start) | collective-permute-done | bytes 884768 | tf_op jit(solution)/shard_map/ppermute | solution.py:667
  39.1 9.0 %all_to_all.30.refs_4_ = bf16[8,24,384]{2,1,0:T(8,128)(2,1)S(1)} all-to-all(bf16[8,24,384]{2,1,0:T(8,128)(2,1)} %get-tuple-element.42), channel_id=1, replica_groups={{0,1,2,3,4,5,6,7},{8,9,10,11,12,13,14,15},{16,17,18,19,24,25,26,27},{20..., dimensions={0} | all-to-all | bytes 294912 | tf_op jit(solution)/shard_map/all_to_all | solution.py:675
  48.6 1.3 %collective-permute-start.1 = (bf16[96,384]{1,0:T(8,128)(2,1)S(1)}, bf16[96,384]{1,0:T(8,128)(2,1)S(1)}, u32[]{:S(2)}, u32[]{:S(2)}) collective-permute-start(bf16[96,384]{1,0:T(8,128)(2,1)S(1)} %shard_map.109.made), channel_id=1, source_target_pairs={{0,25},{1,24},{2,27},{3,26},{4,29},{5,28},{6,31},{7,30},{8,17},{9,... | collective-permute-start | bytes 221192 | tf_op jit(solution)/shard_map/ppermute | solution.py:667
  49.9 1.3 %collective-permute-start.2 = (bf16[96,384]{1,0:T(8,128)(2,1)S(1)}, bf16[96,384]{1,0:T(8,128)(2,1)S(1)}, u32[]{:S(2)}, u32[]{:S(2)}) collective-permute-start(bf16[96,384]{1,0:T(8,128)(2,1)S(1)} %shard_map.109.made), channel_id=1, source_target_pairs={{0,17},{1,16},{2,19},{3,18},{4,21},{5,20},{6,23},{7,22},{8,25},{9,... | collective-permute-start | bytes 221192 | tf_op jit(solution)/shard_map/ppermute | solution.py:667
  51.2 1.3 %collective-permute-start.3 = (bf16[96,384]{1,0:T(8,128)(2,1)S(1)}, bf16[96,384]{1,0:T(8,128)(2,1)S(1)}, u32[]{:S(2)}, u32[]{:S(2)}) collective-permute-start(bf16[96,384]{1,0:T(8,128)(2,1)S(1)} %shard_map.109.made), channel_id=1, source_target_pairs={{0,24},{1,25},{2,26},{3,27},{4,28},{5,29},{6,30},{7,31},{8,16},{9,... | collective-permute-start | bytes 221192 | tf_op jit(solution)/shard_map/ppermute | solution.py:667
  52.5 1.3 %collective-permute-start.4 = (bf16[96,384]{1,0:T(8,128)(2,1)S(1)}, bf16[96,384]{1,0:T(8,128)(2,1)S(1)}, u32[]{:S(2)}, u32[]{:S(2)}) collective-permute-start(bf16[96,384]{1,0:T(8,128)(2,1)S(1)} %shard_map.109.made), channel_id=1, source_target_pairs={{0,16},{1,17},{2,18},{3,19},{4,20},{5,21},{6,22},{7,23},{8,24},{9,... | collective-permute-start | bytes 221192 | tf_op jit(solution)/shard_map/ppermute | solution.py:667
  53.8 1.2 %shard_map.107.refs_2_ = bf16[3,384,384]{2,1,0:T(8,128)(2,1)S(1)} custom-call(bf16[3,384,768]{2,1,0:T(8,128)(2,1)} %bitcast.26), custom_call_target="tpu_custom_call" | custom-call | bytes 3538944 | tf_op jit(solution)/shard_map/pallas_call | solution.py:620
  55.0 0.7 collective-permute-done.1.refs_4_
  55.7 0.7 collective-permute-done.2.refs_5_
  56.4 2.2 %collective-permute-done.3.refs_6_.across = bf16[96,384]{1,0:T(8,128)(2,1)S(1)} collective-permute-done((bf16[96,384]{1,0:T(8,128)(2,1)S(1)}, bf16[96,384]{1,0:T(8,128)(2,1)S(1)}, u32[]{:S(2)}, u32[]{:S(2)}) %collective-permute-start.3) | collective-permute-done | bytes 73760 | tf_op jit(solution)/shard_map/ppermute | solution.py:667
  58.7 2.2 %shard_map.110 = bf16[4,136,384]{2,1,0:T(8,128)(2,1)} custom-call(s32[5]{0:T(128)S(1)} %pad_add_fusion.refs_0_.sizes, bf16[6,768]{1,0:T(8,128)(2,1)S(1)} %bitcast.19, bf16[3,384,384]{2,1,0:T(8,128)(2,1)S(1)} %shard_map.107.refs_2_, bf16[3,384,384]{2,1,0:T(8,128)(2,1)S(1)} %collective-permute-done.refs_3_, ...), custom_call_target="tpu_custom_call" | custom-call | tf_op jit(solution)/shard_map/pallas_call | solution.py:620
  60.9 3.5 %all-to-all-start.3 = ((bf16[4,136,384]{2,1,0:T(8,128)(2,1)}), bf16[4,136,384]{2,1,0:T(8,128)(2,1)S(1)}, u32[]{:S(2)}, u32[]{:S(2)}) async-start(bf16[4,136,384]{2,1,0:T(8,128)(2,1)} %shard_map.110), calls=%async_computation.3 | async-start | bytes 835584 | tf_op jit(solution)/shard_map/all_to_all | solution.py:675
  64.4 0.7 collective-permute-start.6
  65.1 0.7 collective-permute-start.5
  65.7 6.6 %all-to-all-done.3.refs_3_ = bf16[4,136,384]{2,1,0:T(8,128)(2,1)S(1)} async-done(((bf16[4,136,384]{2,1,0:T(8,128)(2,1)}), bf16[4,136,384]{2,1,0:T(8,128)(2,1)S(1)}, u32[]{:S(2)}, u32[]{:S(2)}) %all-to-all-start.3) | async-done | bytes 417824 | tf_op jit(solution)/shard_map/all_to_all | solution.py:675
  72.3 3.1 %shard_map.111 = (bf16[8,24,384]{2,1,0:T(8,128)(2,1)}, bf16[128,384]{1,0:T(8,128)(2,1)}, bf16[128,384]{1,0:T(8,128)(2,1)S(1)}) custom-call(s32[5]{0:T(128)S(1)} %pad_add_fusion.refs_0_.sizes, f32[2,64]{1,0:T(2,128)S(1)} %bitcast.22, bf16[2,128,192]{2,1,0:T(8,128)(2,1)S(1)} %constant_dynamic-slice_fusion.refs_2_, bf16[4,136,384]{2,1,0:T(8,128)(2,1)S(1)} %all-to-all-done.3.refs_3_), custom_call_target="tpu_custom_call" | custom-call | tf_op jit(solution)/shard_map/pallas_call | solution.py:620
  75.4 3.4 %all-to-all-start.4 = ((bf16[8,24,384]{2,1,0:T(8,128)(2,1)}), bf16[8,24,384]{2,1,0:T(8,128)(2,1)S(1)}, u32[]{:S(2)}, u32[]{:S(2)}) async-start(bf16[8,24,384]{2,1,0:T(8,128)(2,1)} %get-tuple-element.51), calls=%async_computation.4 | async-start | bytes 294912 | tf_op jit(solution)/shard_map/all_to_all | solution.py:675
  78.8 3.3 %collective-permute-start.7 = (bf16[128,384]{1,0:T(8,128)(2,1)}, bf16[128,384]{1,0:T(8,128)(2,1)S(1)}, u32[]{:S(2)}, u32[]{:S(2)}) collective-permute-start(bf16[128,384]{1,0:T(8,128)(2,1)} %get-tuple-element.52), channel_id=1, source_target_pairs={{16,17},{17,16},{18,19},{19,18},{20,21},{21,20},{22,23},{23,22},{2... | collective-permute-start | bytes 294920 | tf_op jit(solution)/shard_map/ppermute | solution.py:667
  82.1 2.3 %collective-permute-done.7.last_side = bf16[128,384]{1,0:T(8,128)(2,1)S(1)} collective-permute-done((bf16[128,384]{1,0:T(8,128)(2,1)}, bf16[128,384]{1,0:T(8,128)(2,1)S(1)}, u32[]{:S(2)}, u32[]{:S(2)}) %collective-permute-start.7) | collective-permute-done | bytes 98336 | tf_op jit(solution)/shard_map/ppermute | solution.py:667
  85.1 1.8 %shard_map.112 = (bf16[16,16,384]{2,1,0:T(8,128)(2,1)}, bf16[2,128,384]{2,1,0:T(8,128)(2,1)}, bf16[2,128,384]{2,1,0:T(8,128)(2,1)S(1)}) custom-call(s32[5]{0:T(128)S(1)} %pad_add_fusion.refs_0_.sizes, bf16[6,768]{1,0:T(8,128)(2,1)S(1)} %bitcast.20, bf16[384,768]{1,0:T(8,128)(2,1)S(1)} %bitcast.16, bf16[96,384]{1,0:T(8,128)(2,1)S(1)} %shard_map.109.made, ...), custom_call_target="tpu_custom_call" | custom-call | tf_op jit(solution)/shard_map/pallas_call | solution.py:620
  86.9 4.8 %all-to-all-start.5 = ((bf16[16,16,384]{2,1,0:T(8,128)(2,1)}), bf16[16,16,384]{2,1,0:T(8,128)(2,1)S(1)}, u32[]{:S(2)}, u32[]{:S(2)}) async-start(bf16[16,16,384]{2,1,0:T(8,128)(2,1)} %get-tuple-element.55), calls=%async_computation.5 | async-start | bytes 393216 | tf_op jit(solution)/shard_map/all_to_all | solution.py:698
  91.7 1.4 %collective-permute-start.8 = (bf16[2,128,384]{2,1,0:T(8,128)(2,1)}, bf16[2,128,384]{2,1,0:T(8,128)(2,1)S(1)}, u32[]{:S(2)}, u32[]{:S(2)}) collective-permute-start(bf16[2,128,384]{2,1,0:T(8,128)(2,1)} %get-tuple-element.57), channel_id=1, source_target_pairs={{0,2},{1,3},{2,0},{3,1},{4,6},{5,7},{6,4},{7,5},{8,10},{9,11},{10,... | collective-permute-start | bytes 589832 | tf_op jit(solution)/shard_map/ppermute | solution.py:871
  93.1 5.5 %collective-permute-done.8.other = bf16[2,128,384]{2,1,0:T(8,128)(2,1)S(1)} collective-permute-done((bf16[2,128,384]{2,1,0:T(8,128)(2,1)}, bf16[2,128,384]{2,1,0:T(8,128)(2,1)S(1)}, u32[]{:S(2)}, u32[]{:S(2)}) %collective-permute-start.8) | collective-permute-done | bytes 196640 | tf_op jit(solution)/shard_map/ppermute | solution.py:871
  98.6 0.9 all-to-all-done.5.arrived
  99.5 1.0 shard_map.113
  (22 shorter events, 2.7 us)
Async XLA Ops:
  0.6 22.1 %copy-start = (bf16[1,2,4,32,768]{4,3,2,1,0:T(8,128)(2,1)S(1)}, bf16[1,2,4,32,768]{4,3,2,1,0:T(8,128)(2,1)}, u32[]{:S(2)}) copy-start(bf16[1,2,4,32,768]{4,3,2,1,0:T(8,128)(2,1)} %param.17) | copy-start | bytes 1179652
  0.6 9.6 %copy-start.4 = (s32[4]{0:T(128)S(1)}, s32[4]{0:T(128)}, u32[]{:S(2)}) copy-start(s32[4]{0:T(128)} %param.10) | copy-start | bytes 52
  2.6 10.4 %all-to-all-start = ((bf16[8,16,512]{2,1,0:T(8,128)(2,1)}), bf16[8,16,512]{2,1,0:T(8,128)(2,1)S(1)}, u32[]{:S(2)}, u32[]{:S(2)}) async-start(bf16[8,16,512]{2,1,0:T(8,128)(2,1)} %shard_map.104), calls=%async_computation | async-start | bytes 262144 | tf_op jit(solution)/shard_map/all_to_all | solution.py:675
  13.6 24.8 %copy-start.2 = (f32[1,2,64]{2,1,0:T(2,128)S(1)}, f32[1,2,64]{2,1,0:T(2,128)}, u32[]{:S(2)}) copy-start(f32[1,2,64]{2,1,0:T(2,128)} %param.16) | copy-start | bytes 1540
  13.6 24.8 %all-to-all-start.1 = ((bf16[8,120,384]{2,1,0:T(8,128)(2,1)}), bf16[8,120,384]{2,1,0:T(8,128)(2,1)S(1)}, u32[]{:S(2)}, u32[]{:S(2)}) async-start(bf16[8,120,384]{2,1,0:T(8,128)(2,1)} %get-tuple-element.38), calls=%async_computation.1 | async-start | bytes 1474560 | tf_op jit(solution)/shard_map/all_to_all | solution.py:675
  17.2 30.8 %copy-start.1 = (bf16[1,384,768]{2,1,0:T(8,128)(2,1)S(1)}, bf16[1,384,768]{2,1,0:T(8,128)(2,1)}, u32[]{:S(2)}) copy-start(bf16[1,384,768]{2,1,0:T(8,128)(2,1)} %param.15) | copy-start | bytes 1769476
  19.5 18.9 %collective-permute-start = (bf16[3,384,384]{2,1,0:T(8,128)(2,1)}, bf16[3,384,384]{2,1,0:T(8,128)(2,1)S(1)}, u32[]{:S(2)}, u32[]{:S(2)}) collective-permute-start(bf16[3,384,384]{2,1,0:T(8,128)(2,1)} %constant_dynamic-slice_fusion.1), channel_id=1, source_target_pairs={{16,17},{17,16},{18,19},{19,18},{20,21},{21,20},{22,23},{23,22},{2... | collective-permute-start | bytes 2654216 | tf_op jit(solution)/shard_map/ppermute | solution.py:667
  48.6 7.1 %collective-permute-start.1 = (bf16[96,384]{1,0:T(8,128)(2,1)S(1)}, bf16[96,384]{1,0:T(8,128)(2,1)S(1)}, u32[]{:S(2)}, u32[]{:S(2)}) collective-permute-start(bf16[96,384]{1,0:T(8,128)(2,1)S(1)} %shard_map.109.made), channel_id=1, source_target_pairs={{0,25},{1,24},{2,27},{3,26},{4,29},{5,28},{6,31},{7,30},{8,17},{9,... | collective-permute-start | bytes 221192 | tf_op jit(solution)/shard_map/ppermute | solution.py:667
  49.9 6.5 %collective-permute-start.2 = (bf16[96,384]{1,0:T(8,128)(2,1)S(1)}, bf16[96,384]{1,0:T(8,128)(2,1)S(1)}, u32[]{:S(2)}, u32[]{:S(2)}) collective-permute-start(bf16[96,384]{1,0:T(8,128)(2,1)S(1)} %shard_map.109.made), channel_id=1, source_target_pairs={{0,17},{1,16},{2,19},{3,18},{4,21},{5,20},{6,23},{7,22},{8,25},{9,... | collective-permute-start | bytes 221192 | tf_op jit(solution)/shard_map/ppermute | solution.py:667
  51.2 7.4 %collective-permute-start.3 = (bf16[96,384]{1,0:T(8,128)(2,1)S(1)}, bf16[96,384]{1,0:T(8,128)(2,1)S(1)}, u32[]{:S(2)}, u32[]{:S(2)}) collective-permute-start(bf16[96,384]{1,0:T(8,128)(2,1)S(1)} %shard_map.109.made), channel_id=1, source_target_pairs={{0,24},{1,25},{2,26},{3,27},{4,28},{5,29},{6,30},{7,31},{8,16},{9,... | collective-permute-start | bytes 221192 | tf_op jit(solution)/shard_map/ppermute | solution.py:667
  52.5 6.1 %collective-permute-start.4 = (bf16[96,384]{1,0:T(8,128)(2,1)S(1)}, bf16[96,384]{1,0:T(8,128)(2,1)S(1)}, u32[]{:S(2)}, u32[]{:S(2)}) collective-permute-start(bf16[96,384]{1,0:T(8,128)(2,1)S(1)} %shard_map.109.made), channel_id=1, source_target_pairs={{0,16},{1,17},{2,18},{3,19},{4,20},{5,21},{6,22},{7,23},{8,24},{9,... | collective-permute-start | bytes 221192 | tf_op jit(solution)/shard_map/ppermute | solution.py:667
  55.0 9.4 %copy-start.3 = (bf16[128,384]{1,0:T(8,128)(2,1)S(1)}, bf16[128,384]{1,0:T(8,128)(2,1)}, u32[]{:S(2)}) copy-start(bf16[128,384]{1,0:T(8,128)(2,1)} %get-tuple-element.46.first_cache) | copy-start | bytes 294916
  60.9 11.4 %all-to-all-start.3 = ((bf16[4,136,384]{2,1,0:T(8,128)(2,1)}), bf16[4,136,384]{2,1,0:T(8,128)(2,1)S(1)}, u32[]{:S(2)}, u32[]{:S(2)}) async-start(bf16[4,136,384]{2,1,0:T(8,128)(2,1)} %shard_map.110), calls=%async_computation.3 | async-start | bytes 835584 | tf_op jit(solution)/shard_map/all_to_all | solution.py:675
  64.4 1.4 %collective-permute-start.6 = (bf16[128,384]{1,0:T(8,128)(2,1)S(1)}, bf16[128,384]{1,0:T(8,128)(2,1)S(1)}, u32[]{:S(2)}, u32[]{:S(2)}) collective-permute-start(bf16[128,384]{1,0:T(8,128)(2,1)S(1)} %copy-done.3), channel_id=1, source_target_pairs={{0,1},{1,0},{2,3},{3,2},{4,5},{5,4},{6,7},{7,6},{8,9},{9,8},{10,11... | collective-permute-start | bytes 294920 | tf_op jit(solution)/shard_map/ppermute | solution.py:667
  65.1 0.7 collective-permute-start.5
  75.4 9.6 %all-to-all-start.4 = ((bf16[8,24,384]{2,1,0:T(8,128)(2,1)}), bf16[8,24,384]{2,1,0:T(8,128)(2,1)S(1)}, u32[]{:S(2)}, u32[]{:S(2)}) async-start(bf16[8,24,384]{2,1,0:T(8,128)(2,1)} %get-tuple-element.51), calls=%async_computation.4 | async-start | bytes 294912 | tf_op jit(solution)/shard_map/all_to_all | solution.py:675
  78.8 5.6 %collective-permute-start.7 = (bf16[128,384]{1,0:T(8,128)(2,1)}, bf16[128,384]{1,0:T(8,128)(2,1)S(1)}, u32[]{:S(2)}, u32[]{:S(2)}) collective-permute-start(bf16[128,384]{1,0:T(8,128)(2,1)} %get-tuple-element.52), channel_id=1, source_target_pairs={{16,17},{17,16},{18,19},{19,18},{20,21},{21,20},{22,23},{23,22},{2... | collective-permute-start | bytes 294920 | tf_op jit(solution)/shard_map/ppermute | solution.py:667
  86.9 12.6 %all-to-all-start.5 = ((bf16[16,16,384]{2,1,0:T(8,128)(2,1)}), bf16[16,16,384]{2,1,0:T(8,128)(2,1)S(1)}, u32[]{:S(2)}, u32[]{:S(2)}) async-start(bf16[16,16,384]{2,1,0:T(8,128)(2,1)} %get-tuple-element.55), calls=%async_computation.5 | async-start | bytes 393216 | tf_op jit(solution)/shard_map/all_to_all | solution.py:698
  91.7 6.8 %collective-permute-start.8 = (bf16[2,128,384]{2,1,0:T(8,128)(2,1)}, bf16[2,128,384]{2,1,0:T(8,128)(2,1)S(1)}, u32[]{:S(2)}, u32[]{:S(2)}) collective-permute-start(bf16[2,128,384]{2,1,0:T(8,128)(2,1)} %get-tuple-element.57), channel_id=1, source_target_pairs={{0,2},{1,3},{2,0},{3,1},{4,6},{5,7},{6,4},{7,5},{8,10},{9,11},{10,... | collective-permute-start | bytes 589832 | tf_op jit(solution)/shard_map/ppermute | solution.py:871

commit v4 on v3

--- a/solution.py
+++ b/solution.py
@@ -520,7 +520,7 @@
 
 
 def last_rows(
-    dims, sizes, mod, near, made, back, given, across, first_cache, last_cache, first_side,
+    dims, sizes, mod, near, made, given, across, first_cache, last_cache, first_side,
     last_side, arrived, out, pair, pieces, staged, sems, fetched, sent
 ):
     def spread(states):
@@ -544,7 +544,7 @@
         pieces[1] = first_side[...]
         copy.wait()
         copy = begin(pieces, pair, sent)
-        states = from_first(dims, both(made, back)).astype(BF16)
+        states = made[...]
         spread(states)
         copy.wait()
 
@@ -820,11 +820,10 @@
             pltpu.SemaphoreType.DMA((lines,)),
         ],
     )
-    blocks, made, cache_first = after(blocks, made, cache_first)
+    blocks, cache_first = after(blocks, cache_first)
     arrived = over_lines(blocks, 1)
-    back = send(made, 0, 0, df=1)
     side_first = send(cache_first, 0, 0, dt=1)
-    arrived, back, side_first = after(arrived, back, side_first)
+    arrived, side_first = after(arrived, side_first)
 
     attended, cache_last, kept_last = stage(
         working(1, attention, 1),
@@ -851,7 +850,6 @@
         mod,
         near,
         made,
-        back,
         given,
         across,
         cache_first,
@@ -859,7 +857,7 @@
         side_first,
         side_last,
         arrived,
-        left=(7,),
+        left=(6,),
         scratch=[
             pltpu.VMEM((count, rows, depth), BF16),
             pltpu.SemaphoreType.DMA((halves,)),

time: 101 us -> 102 us (level)
    ppermute x8 -> x7, starting transfers between devices: 13 us -> 12.3 us  [send(): return lax.ppermute(block, ('section', 'fsdp', 'tok'), ends)]
    ppermute x8 -> x7, waiting for transfers between devices: 21.5 us -> 21.9 us  [send(): return lax.ppermute(block, ('section', 'fsdp', 'tok'), ends)]
  transfers between devices with their start and end apart: 14 -> 13, of which waited for: 10 -> 10; matrix products, arithmetic and copies ran while one was open for 3% -> 3% of each run, Pallas kernels for 1% -> 1%
where the time goes in v4:
time: 102 us; the launch traced here: 101 us
  waiting for transfers between devices  38.1 us (37%)
  starting transfers between devices  35.3 us (35%)
  Pallas kernels  13 us (13%)
  blocking collectives  8.99 us (9%)
  local copies, waits for them, and re-layouts  3.39 us (3%)
  between operations  2.24 us (2%)
    ppermute x7, waiting for transfers between devices, send(): return lax.ppermute(block, ('section', 'fsdp', 'tok'), ends)  21.9 us
    all_to_all x4, starting transfers between devices, grouped(): lax.all_to_all(blocks, ('section', 'fsdp', 'tok'), 0, 0, axis_index_group...  16.3 us
    pallas_call x10, Pallas kernels, stage(): pl.pallas_call(body, out_shape=outs, in_specs=[pl.BlockSpec(memory_space=...  13 us
    ppermute x7, starting transfers between devices, send(): return lax.ppermute(block, ('section', 'fsdp', 'tok'), ends)  12.3 us
    all_to_all x4, waiting for transfers between devices, grouped(): lax.all_to_all(blocks, ('section', 'fsdp', 'tok'), 0, 0, axis_index_group...  10.6 us
    all_to_all x1, blocking collectives, grouped(): lax.all_to_all(blocks, ('section', 'fsdp', 'tok'), 0, 0, axis_index_group...  8.99 us
    all_to_all x1, starting transfers between devices, all_devices(): return lax.all_to_all(blocks, ('fsdp', 'tok'), 0, 0, tiled=False)  5.33 us
    ppermute x1, waiting for transfers between devices, by_kernels(): other = lax.ppermute(pair, 'tok', [(t, t ^ pairs) for t in range(count)])  4.84 us
  transfers between devices with their start and end apart: 13, of which 10 were waited for; matrix products, arithmetic and copies ran while one was open for 3% of the time, Pallas kernels for 1%

profile of v4, /device:TPU:1, one launch (start us, length us, event | category | flops | bytes accessed | tf_op | source)
XLA Modules:
  0.0 101.1 jit_solution(8952340446907468874)
XLA Ops:
  0.7 1.9 %shard_map.104 = bf16[8,16,512]{2,1,0:T(8,128)(2,1)} custom-call(bf16[4,4,3072]{2,1,0:T(4,128)(2,1)} %hidden.1), custom_call_target="tpu_custom_call" | custom-call | tf_op jit(solution)/shard_map/pallas_call | solution.py:620
  2.6 5.3 %all-to-all-start = ((bf16[8,16,512]{2,1,0:T(8,128)(2,1)}), bf16[8,16,512]{2,1,0:T(8,128)(2,1)S(1)}, u32[]{:S(2)}, u32[]{:S(2)}) async-start(bf16[8,16,512]{2,1,0:T(8,128)(2,1)} %shard_map.104), calls=%async_computation | async-start | bytes 262144 | tf_op jit(solution)/shard_map/all_to_all | solution.py:675
  9.2 1.0 constant_dynamic-slice_fusion.2
  10.3 2.7 %all-to-all-done.refs_4_ = bf16[8,16,512]{2,1,0:T(8,128)(2,1)S(1)} async-done(((bf16[8,16,512]{2,1,0:T(8,128)(2,1)}), bf16[8,16,512]{2,1,0:T(8,128)(2,1)S(1)}, u32[]{:S(2)}, u32[]{:S(2)}) %all-to-all-start) | async-done | bytes 131104 | tf_op jit(solution)/shard_map/all_to_all | solution.py:675
  13.6 3.6 %all-to-all-start.1 = ((bf16[8,120,384]{2,1,0:T(8,128)(2,1)}), bf16[8,120,384]{2,1,0:T(8,128)(2,1)S(1)}, u32[]{:S(2)}, u32[]{:S(2)}) async-start(bf16[8,120,384]{2,1,0:T(8,128)(2,1)} %get-tuple-element.36), calls=%async_computation.1 | async-start | bytes 1474560 | tf_op jit(solution)/shard_map/all_to_all | solution.py:675
  17.2 2.3 %constant_dynamic-slice_fusion = bf16[3,384,384]{2,1,0:T(8,128)(2,1)} fusion(bf16[3,384,768]{2,1,0:T(8,128)(2,1)} %bitcast.25, s32[]{:T(128)S(6)} %select_n.33), kind=kLoop, calls=%fused_computation.1 | loop fusion | bytes 1769476 | tf_op jit(solution)/shard_map/dynamic_slice | solution.py:777
  19.5 3.2 %collective-permute-start = (bf16[3,384,384]{2,1,0:T(8,128)(2,1)}, bf16[3,384,384]{2,1,0:T(8,128)(2,1)S(1)}, u32[]{:S(2)}, u32[]{:S(2)}) collective-permute-start(bf16[3,384,384]{2,1,0:T(8,128)(2,1)} %constant_dynamic-slice_fusion), channel_id=1, source_target_pairs={{16,17},{17,16},{18,19},{19,18},{20,21},{21,20},{22,23},{23,22},{2... | collective-permute-start | bytes 2654216 | tf_op jit(solution)/shard_map/ppermute | solution.py:667
  22.9 15.5 %collective-permute-done.refs_3_ = bf16[3,384,384]{2,1,0:T(8,128)(2,1)S(1)} collective-permute-done((bf16[3,384,384]{2,1,0:T(8,128)(2,1)}, bf16[3,384,384]{2,1,0:T(8,128)(2,1)S(1)}, u32[]{:S(2)}, u32[]{:S(2)}) %collective-permute-start) | collective-permute-done | bytes 884768 | tf_op jit(solution)/shard_map/ppermute | solution.py:667
  39.1 9.0 %all_to_all.30.refs_4_ = bf16[8,24,384]{2,1,0:T(8,128)(2,1)S(1)} all-to-all(bf16[8,24,384]{2,1,0:T(8,128)(2,1)} %get-tuple-element.39), channel_id=1, replica_groups={{0,1,2,3,4,5,6,7},{8,9,10,11,12,13,14,15},{16,17,18,19,24,25,26,27},{20..., dimensions={0} | all-to-all | bytes 294912 | tf_op jit(solution)/shard_map/all_to_all | solution.py:675
  48.6 1.3 %collective-permute-start.1 = (bf16[96,384]{1,0:T(8,128)(2,1)S(1)}, bf16[96,384]{1,0:T(8,128)(2,1)S(1)}, u32[]{:S(2)}, u32[]{:S(2)}) collective-permute-start(bf16[96,384]{1,0:T(8,128)(2,1)S(1)} %shard_map.108.made), channel_id=1, source_target_pairs={{0,16},{1,17},{2,18},{3,19},{4,20},{5,21},{6,22},{7,23},{8,24},{9,... | collective-permute-start | bytes 221192 | tf_op jit(solution)/shard_map/ppermute | solution.py:667
  49.9 1.3 %collective-permute-start.2 = (bf16[96,384]{1,0:T(8,128)(2,1)S(1)}, bf16[96,384]{1,0:T(8,128)(2,1)S(1)}, u32[]{:S(2)}, u32[]{:S(2)}) collective-permute-start(bf16[96,384]{1,0:T(8,128)(2,1)S(1)} %shard_map.108.made), channel_id=1, source_target_pairs={{0,24},{1,25},{2,26},{3,27},{4,28},{5,29},{6,30},{7,31},{8,16},{9,... | collective-permute-start | bytes 221192 | tf_op jit(solution)/shard_map/ppermute | solution.py:667
  51.2 1.3 %collective-permute-start.3 = (bf16[96,384]{1,0:T(8,128)(2,1)S(1)}, bf16[96,384]{1,0:T(8,128)(2,1)S(1)}, u32[]{:S(2)}, u32[]{:S(2)}) collective-permute-start(bf16[96,384]{1,0:T(8,128)(2,1)S(1)} %shard_map.108.made), channel_id=1, source_target_pairs={{0,25},{1,24},{2,27},{3,26},{4,29},{5,28},{6,31},{7,30},{8,17},{9,... | collective-permute-start | bytes 221192 | tf_op jit(solution)/shard_map/ppermute | solution.py:667
  52.5 1.3 %collective-permute-start.4 = (bf16[96,384]{1,0:T(8,128)(2,1)S(1)}, bf16[96,384]{1,0:T(8,128)(2,1)S(1)}, u32[]{:S(2)}, u32[]{:S(2)}) collective-permute-start(bf16[96,384]{1,0:T(8,128)(2,1)S(1)} %shard_map.108.made), channel_id=1, source_target_pairs={{0,17},{1,16},{2,19},{3,18},{4,21},{5,20},{6,23},{7,22},{8,25},{9,... | collective-permute-start | bytes 221192 | tf_op jit(solution)/shard_map/ppermute | solution.py:667
  53.8 1.2 %shard_map.109.refs_2_ = bf16[3,384,384]{2,1,0:T(8,128)(2,1)S(1)} custom-call(bf16[3,384,768]{2,1,0:T(8,128)(2,1)} %bitcast.26), custom_call_target="tpu_custom_call" | custom-call | bytes 3538944 | tf_op jit(solution)/shard_map/pallas_call | solution.py:620
  55.0 2.3 %collective-permute-done.2.refs_6_.across = bf16[96,384]{1,0:T(8,128)(2,1)S(1)} collective-permute-done((bf16[96,384]{1,0:T(8,128)(2,1)S(1)}, bf16[96,384]{1,0:T(8,128)(2,1)S(1)}, u32[]{:S(2)}, u32[]{:S(2)}) %collective-permute-start.2) | collective-permute-done | bytes 73760 | tf_op jit(solution)/shard_map/ppermute | solution.py:667
  57.4 0.9 collective-permute-done.3.refs_4_
  58.3 0.7 collective-permute-done.4.refs_5_
  59.0 2.2 %shard_map.110 = bf16[4,136,384]{2,1,0:T(8,128)(2,1)} custom-call(s32[5]{0:T(128)S(1)} %pad_add_fusion.refs_0_.sizes, bf16[6,768]{1,0:T(8,128)(2,1)S(1)} %bitcast.19, bf16[3,384,384]{2,1,0:T(8,128)(2,1)S(1)} %shard_map.109.refs_2_, bf16[3,384,384]{2,1,0:T(8,128)(2,1)S(1)} %collective-permute-done.refs_3_, ...), custom_call_target="tpu_custom_call" | custom-call | tf_op jit(solution)/shard_map/pallas_call | solution.py:620
  61.2 4.1 %all-to-all-start.3 = ((bf16[4,136,384]{2,1,0:T(8,128)(2,1)}), bf16[4,136,384]{2,1,0:T(8,128)(2,1)S(1)}, u32[]{:S(2)}, u32[]{:S(2)}) async-start(bf16[4,136,384]{2,1,0:T(8,128)(2,1)} %shard_map.110), calls=%async_computation.3 | async-start | bytes 835584 | tf_op jit(solution)/shard_map/all_to_all | solution.py:675
  65.3 0.7 collective-permute-start.5
  66.0 7.3 %all-to-all-done.3.refs_3_ = bf16[4,136,384]{2,1,0:T(8,128)(2,1)S(1)} async-done(((bf16[4,136,384]{2,1,0:T(8,128)(2,1)}), bf16[4,136,384]{2,1,0:T(8,128)(2,1)S(1)}, u32[]{:S(2)}, u32[]{:S(2)}) %all-to-all-start.3) | async-done | bytes 417824 | tf_op jit(solution)/shard_map/all_to_all | solution.py:675
  73.3 3.1 %shard_map.111 = (bf16[8,24,384]{2,1,0:T(8,128)(2,1)}, bf16[128,384]{1,0:T(8,128)(2,1)}, bf16[128,384]{1,0:T(8,128)(2,1)S(1)}) custom-call(s32[5]{0:T(128)S(1)} %pad_add_fusion.refs_0_.sizes, f32[2,64]{1,0:T(2,128)S(1)} %bitcast.22, bf16[2,128,192]{2,1,0:T(8,128)(2,1)S(1)} %constant_dynamic-slice_fusion.1.refs_2_, ...), custom_call_target="tpu_custom_call" | custom-call | tf_op jit(solution)/shard_map/pallas_call | solution.py:620
  76.4 3.4 %all-to-all-start.4 = ((bf16[8,24,384]{2,1,0:T(8,128)(2,1)}), bf16[8,24,384]{2,1,0:T(8,128)(2,1)S(1)}, u32[]{:S(2)}, u32[]{:S(2)}) async-start(bf16[8,24,384]{2,1,0:T(8,128)(2,1)} %get-tuple-element.47), calls=%async_computation.4 | async-start | bytes 294912 | tf_op jit(solution)/shard_map/all_to_all | solution.py:675
  79.8 3.3 %collective-permute-start.6 = (bf16[128,384]{1,0:T(8,128)(2,1)}, bf16[128,384]{1,0:T(8,128)(2,1)S(1)}, u32[]{:S(2)}, u32[]{:S(2)}) collective-permute-start(bf16[128,384]{1,0:T(8,128)(2,1)} %get-tuple-element.48), channel_id=1, source_target_pairs={{16,17},{17,16},{18,19},{19,18},{20,21},{21,20},{22,23},{23,22},{2... | collective-permute-start | bytes 294920 | tf_op jit(solution)/shard_map/ppermute | solution.py:667
  83.1 2.3 %collective-permute-done.6.last_side = bf16[128,384]{1,0:T(8,128)(2,1)S(1)} collective-permute-done((bf16[128,384]{1,0:T(8,128)(2,1)}, bf16[128,384]{1,0:T(8,128)(2,1)S(1)}, u32[]{:S(2)}, u32[]{:S(2)}) %collective-permute-start.6) | collective-permute-done | bytes 98336 | tf_op jit(solution)/shard_map/ppermute | solution.py:667
  85.4 0.6 all-to-all-done.4.arrived
  86.0 1.8 %shard_map.112 = (bf16[16,16,384]{2,1,0:T(8,128)(2,1)}, bf16[2,128,384]{2,1,0:T(8,128)(2,1)}, bf16[2,128,384]{2,1,0:T(8,128)(2,1)S(1)}) custom-call(s32[5]{0:T(128)S(1)} %pad_add_fusion.refs_0_.sizes, bf16[6,768]{1,0:T(8,128)(2,1)S(1)} %bitcast.20, bf16[384,768]{1,0:T(8,128)(2,1)S(1)} %bitcast.16, bf16[96,384]{1,0:T(8,128)(2,1)S(1)} %shard_map.108.made, ...), custom_call_target="tpu_custom_call" | custom-call | tf_op jit(solution)/shard_map/pallas_call | solution.py:620
  87.9 5.3 %all-to-all-start.5 = ((bf16[16,16,384]{2,1,0:T(8,128)(2,1)}), bf16[16,16,384]{2,1,0:T(8,128)(2,1)S(1)}, u32[]{:S(2)}, u32[]{:S(2)}) async-start(bf16[16,16,384]{2,1,0:T(8,128)(2,1)} %get-tuple-element.51), calls=%async_computation.5 | async-start | bytes 393216 | tf_op jit(solution)/shard_map/all_to_all | solution.py:698
  93.2 1.4 %collective-permute-start.7 = (bf16[2,128,384]{2,1,0:T(8,128)(2,1)}, bf16[2,128,384]{2,1,0:T(8,128)(2,1)S(1)}, u32[]{:S(2)}, u32[]{:S(2)}) collective-permute-start(bf16[2,128,384]{2,1,0:T(8,128)(2,1)} %get-tuple-element.53), channel_id=1, source_target_pairs={{0,2},{1,3},{2,0},{3,1},{4,6},{5,7},{6,4},{7,5},{8,10},{9,11},{10,... | collective-permute-start | bytes 589832 | tf_op jit(solution)/shard_map/ppermute | solution.py:869
  94.6 4.8 %collective-permute-done.7.other = bf16[2,128,384]{2,1,0:T(8,128)(2,1)S(1)} collective-permute-done((bf16[2,128,384]{2,1,0:T(8,128)(2,1)}, bf16[2,128,384]{2,1,0:T(8,128)(2,1)S(1)}, u32[]{:S(2)}, u32[]{:S(2)}) %collective-permute-start.7) | collective-permute-done | bytes 196640 | tf_op jit(solution)/shard_map/ppermute | solution.py:869
  99.4 0.7 all-to-all-done.5.arrived
  100.1 1.0 shard_map.113
  (20 shorter events, 2.1 us)
Async XLA Ops:
  0.6 22.1 %copy-start = (bf16[1,2,4,32,768]{4,3,2,1,0:T(8,128)(2,1)S(1)}, bf16[1,2,4,32,768]{4,3,2,1,0:T(8,128)(2,1)}, u32[]{:S(2)}) copy-start(bf16[1,2,4,32,768]{4,3,2,1,0:T(8,128)(2,1)} %param.17) | copy-start | bytes 1179652
  0.6 9.6 %copy-start.4 = (s32[4]{0:T(128)S(1)}, s32[4]{0:T(128)}, u32[]{:S(2)}) copy-start(s32[4]{0:T(128)} %param.10) | copy-start | bytes 52
  2.6 10.4 %all-to-all-start = ((bf16[8,16,512]{2,1,0:T(8,128)(2,1)}), bf16[8,16,512]{2,1,0:T(8,128)(2,1)S(1)}, u32[]{:S(2)}, u32[]{:S(2)}) async-start(bf16[8,16,512]{2,1,0:T(8,128)(2,1)} %shard_map.104), calls=%async_computation | async-start | bytes 262144 | tf_op jit(solution)/shard_map/all_to_all | solution.py:675
  13.6 24.8 %copy-start.2 = (f32[1,2,64]{2,1,0:T(2,128)S(1)}, f32[1,2,64]{2,1,0:T(2,128)}, u32[]{:S(2)}) copy-start(f32[1,2,64]{2,1,0:T(2,128)} %param.16) | copy-start | bytes 1540
  13.6 24.8 %all-to-all-start.1 = ((bf16[8,120,384]{2,1,0:T(8,128)(2,1)}), bf16[8,120,384]{2,1,0:T(8,128)(2,1)S(1)}, u32[]{:S(2)}, u32[]{:S(2)}) async-start(bf16[8,120,384]{2,1,0:T(8,128)(2,1)} %get-tuple-element.36), calls=%async_computation.1 | async-start | bytes 1474560 | tf_op jit(solution)/shard_map/all_to_all | solution.py:675
  17.2 30.8 %copy-start.1 = (bf16[1,384,768]{2,1,0:T(8,128)(2,1)S(1)}, bf16[1,384,768]{2,1,0:T(8,128)(2,1)}, u32[]{:S(2)}) copy-start(bf16[1,384,768]{2,1,0:T(8,128)(2,1)} %param.15) | copy-start | bytes 1769476
  19.5 18.9 %collective-permute-start = (bf16[3,384,384]{2,1,0:T(8,128)(2,1)}, bf16[3,384,384]{2,1,0:T(8,128)(2,1)S(1)}, u32[]{:S(2)}, u32[]{:S(2)}) collective-permute-start(bf16[3,384,384]{2,1,0:T(8,128)(2,1)} %constant_dynamic-slice_fusion), channel_id=1, source_target_pairs={{16,17},{17,16},{18,19},{19,18},{20,21},{21,20},{22,23},{23,22},{2... | collective-permute-start | bytes 2654216 | tf_op jit(solution)/shard_map/ppermute | solution.py:667
  48.6 6.4 %collective-permute-start.1 = (bf16[96,384]{1,0:T(8,128)(2,1)S(1)}, bf16[96,384]{1,0:T(8,128)(2,1)S(1)}, u32[]{:S(2)}, u32[]{:S(2)}) collective-permute-start(bf16[96,384]{1,0:T(8,128)(2,1)S(1)} %shard_map.108.made), channel_id=1, source_target_pairs={{0,16},{1,17},{2,18},{3,19},{4,20},{5,21},{6,22},{7,23},{8,24},{9,... | collective-permute-start | bytes 221192 | tf_op jit(solution)/shard_map/ppermute | solution.py:667
  49.9 7.4 %collective-permute-start.2 = (bf16[96,384]{1,0:T(8,128)(2,1)S(1)}, bf16[96,384]{1,0:T(8,128)(2,1)S(1)}, u32[]{:S(2)}, u32[]{:S(2)}) collective-permute-start(bf16[96,384]{1,0:T(8,128)(2,1)S(1)} %shard_map.108.made), channel_id=1, source_target_pairs={{0,24},{1,25},{2,26},{3,27},{4,28},{5,29},{6,30},{7,31},{8,16},{9,... | collective-permute-start | bytes 221192 | tf_op jit(solution)/shard_map/ppermute | solution.py:667
  51.2 7.1 %collective-permute-start.3 = (bf16[96,384]{1,0:T(8,128)(2,1)S(1)}, bf16[96,384]{1,0:T(8,128)(2,1)S(1)}, u32[]{:S(2)}, u32[]{:S(2)}) collective-permute-start(bf16[96,384]{1,0:T(8,128)(2,1)S(1)} %shard_map.108.made), channel_id=1, source_target_pairs={{0,25},{1,24},{2,27},{3,26},{4,29},{5,28},{6,31},{7,30},{8,17},{9,... | collective-permute-start | bytes 221192 | tf_op jit(solution)/shard_map/ppermute | solution.py:667
  52.5 6.5 %collective-permute-start.4 = (bf16[96,384]{1,0:T(8,128)(2,1)S(1)}, bf16[96,384]{1,0:T(8,128)(2,1)S(1)}, u32[]{:S(2)}, u32[]{:S(2)}) collective-permute-start(bf16[96,384]{1,0:T(8,128)(2,1)S(1)} %shard_map.108.made), channel_id=1, source_target_pairs={{0,17},{1,16},{2,19},{3,18},{4,21},{5,20},{6,23},{7,22},{8,25},{9,... | collective-permute-start | bytes 221192 | tf_op jit(solution)/shard_map/ppermute | solution.py:667
  55.0 10.3 %copy-start.3 = (bf16[128,384]{1,0:T(8,128)(2,1)S(1)}, bf16[128,384]{1,0:T(8,128)(2,1)}, u32[]{:S(2)}) copy-start(bf16[128,384]{1,0:T(8,128)(2,1)} %get-tuple-element.42.first_cache) | copy-start | bytes 294916
  61.2 12.1 %all-to-all-start.3 = ((bf16[4,136,384]{2,1,0:T(8,128)(2,1)}), bf16[4,136,384]{2,1,0:T(8,128)(2,1)S(1)}, u32[]{:S(2)}, u32[]{:S(2)}) async-start(bf16[4,136,384]{2,1,0:T(8,128)(2,1)} %shard_map.110), calls=%async_computation.3 | async-start | bytes 835584 | tf_op jit(solution)/shard_map/all_to_all | solution.py:675
  65.3 0.7 collective-permute-start.5
  76.4 9.6 %all-to-all-start.4 = ((bf16[8,24,384]{2,1,0:T(8,128)(2,1)}), bf16[8,24,384]{2,1,0:T(8,128)(2,1)S(1)}, u32[]{:S(2)}, u32[]{:S(2)}) async-start(bf16[8,24,384]{2,1,0:T(8,128)(2,1)} %get-tuple-element.47), calls=%async_computation.4 | async-start | bytes 294912 | tf_op jit(solution)/shard_map/all_to_all | solution.py:675
  79.8 5.6 %collective-permute-start.6 = (bf16[128,384]{1,0:T(8,128)(2,1)}, bf16[128,384]{1,0:T(8,128)(2,1)S(1)}, u32[]{:S(2)}, u32[]{:S(2)}) collective-permute-start(bf16[128,384]{1,0:T(8,128)(2,1)} %get-tuple-element.48), channel_id=1, source_target_pairs={{16,17},{17,16},{18,19},{19,18},{20,21},{21,20},{22,23},{23,22},{2... | collective-permute-start | bytes 294920 | tf_op jit(solution)/shard_map/ppermute | solution.py:667
  87.9 12.3 %all-to-all-start.5 = ((bf16[16,16,384]{2,1,0:T(8,128)(2,1)}), bf16[16,16,384]{2,1,0:T(8,128)(2,1)S(1)}, u32[]{:S(2)}, u32[]{:S(2)}) async-start(bf16[16,16,384]{2,1,0:T(8,128)(2,1)} %get-tuple-element.51), calls=%async_computation.5 | async-start | bytes 393216 | tf_op jit(solution)/shard_map/all_to_all | solution.py:698
  93.2 6.2 %collective-permute-start.7 = (bf16[2,128,384]{2,1,0:T(8,128)(2,1)}, bf16[2,128,384]{2,1,0:T(8,128)(2,1)S(1)}, u32[]{:S(2)}, u32[]{:S(2)}) collective-permute-start(bf16[2,128,384]{2,1,0:T(8,128)(2,1)} %get-tuple-element.53), channel_id=1, source_target_pairs={{0,2},{1,3},{2,0},{3,1},{4,6},{5,7},{6,4},{7,5},{8,10},{9,11},{10,... | collective-permute-start | bytes 589832 | tf_op jit(solution)/shard_map/ppermute | solution.py:869

commit v5 on v4

--- a/solution.py
+++ b/solution.py
@@ -520,8 +520,8 @@
 
 
 def last_rows(
-    dims, sizes, mod, near, made, given, across, first_cache, last_cache, first_side,
-    last_side, arrived, out, pair, pieces, staged, sems, fetched, sent
+    dims, sizes, mod, near, made, first_cache, last_cache, first_side, last_side, given, across,
+    arrived, out, pair, pieces, staged, sems, fetched, sent
 ):
     def spread(states):
         patch, slot = slots_by_device((dims.total, 1), 0, dims.cap_dev, dims.patches)
@@ -850,14 +850,14 @@
         mod,
         near,
         made,
-        given,
-        across,
         cache_first,
         kept_last,
         side_first,
         side_last,
+        given,
+        across,
         arrived,
-        left=(6,),
+        left=(4,),
         scratch=[
             pltpu.VMEM((count, rows, depth), BF16),
             pltpu.SemaphoreType.DMA((halves,)),

time: 102 us -> 101 us (level)
  starting transfers between devices: 35.3 us -> 34.2 us
where the time goes in v5:
time: 101 us; the launch traced here: 99.6 us
  waiting for transfers between devices  37.7 us (37%)
  starting transfers between devices  34.2 us (34%)
  Pallas kernels  13 us (13%)
  blocking collectives  8.99 us (9%)
  local copies, waits for them, and re-layouts  3.39 us (3%)
  between operations  2.25 us (2%)
    ppermute x7, waiting for transfers between devices, send(): return lax.ppermute(block, ('section', 'fsdp', 'tok'), ends)  21.5 us
    all_to_all x4, starting transfers between devices, grouped(): lax.all_to_all(blocks, ('section', 'fsdp', 'tok'), 0, 0, axis_index_group...  15.7 us
    pallas_call x10, Pallas kernels, stage(): pl.pallas_call(body, out_shape=outs, in_specs=[pl.BlockSpec(memory_space=...  13 us
    ppermute x7, starting transfers between devices, send(): return lax.ppermute(block, ('section', 'fsdp', 'tok'), ends)  12.3 us
    all_to_all x4, waiting for transfers between devices, grouped(): lax.all_to_all(blocks, ('section', 'fsdp', 'tok'), 0, 0, axis_index_group...  10.6 us
    all_to_all x1, blocking collectives, grouped(): lax.all_to_all(blocks, ('section', 'fsdp', 'tok'), 0, 0, axis_index_group...  8.99 us
    ppermute x1, waiting for transfers between devices, by_kernels(): other = lax.ppermute(pair, 'tok', [(t, t ^ pairs) for t in range(count)])  4.84 us
    all_to_all x1, starting transfers between devices, all_devices(): return lax.all_to_all(blocks, ('fsdp', 'tok'), 0, 0, tiled=False)  4.81 us
  transfers between devices with their start and end apart: 13, of which 10 were waited for; matrix products, arithmetic and copies ran while one was open for 3% of the time, Pallas kernels for 1%

profile of v5, /device:TPU:1, one launch (start us, length us, event | category | flops | bytes accessed | tf_op | source)
XLA Modules:
  0.0 99.6 jit_solution(13766193214444142803)
XLA Ops:
  0.7 1.9 %shard_map.104 = bf16[8,16,512]{2,1,0:T(8,128)(2,1)} custom-call(bf16[4,4,3072]{2,1,0:T(4,128)(2,1)} %hidden.1), custom_call_target="tpu_custom_call" | custom-call | tf_op jit(solution)/shard_map/pallas_call | solution.py:620
  2.6 5.3 %all-to-all-start = ((bf16[8,16,512]{2,1,0:T(8,128)(2,1)}), bf16[8,16,512]{2,1,0:T(8,128)(2,1)S(1)}, u32[]{:S(2)}, u32[]{:S(2)}) async-start(bf16[8,16,512]{2,1,0:T(8,128)(2,1)} %shard_map.104), calls=%async_computation | async-start | bytes 262144 | tf_op jit(solution)/shard_map/all_to_all | solution.py:675
  9.2 1.0 constant_dynamic-slice_fusion.2
  10.3 2.7 %all-to-all-done.refs_4_ = bf16[8,16,512]{2,1,0:T(8,128)(2,1)S(1)} async-done(((bf16[8,16,512]{2,1,0:T(8,128)(2,1)}), bf16[8,16,512]{2,1,0:T(8,128)(2,1)S(1)}, u32[]{:S(2)}, u32[]{:S(2)}) %all-to-all-start) | async-done | bytes 131104 | tf_op jit(solution)/shard_map/all_to_all | solution.py:675
  13.6 3.6 %all-to-all-start.1 = ((bf16[8,120,384]{2,1,0:T(8,128)(2,1)}), bf16[8,120,384]{2,1,0:T(8,128)(2,1)S(1)}, u32[]{:S(2)}, u32[]{:S(2)}) async-start(bf16[8,120,384]{2,1,0:T(8,128)(2,1)} %get-tuple-element.36), calls=%async_computation.1 | async-start | bytes 1474560 | tf_op jit(solution)/shard_map/all_to_all | solution.py:675
  17.2 2.3 %constant_dynamic-slice_fusion = bf16[3,384,384]{2,1,0:T(8,128)(2,1)} fusion(bf16[3,384,768]{2,1,0:T(8,128)(2,1)} %bitcast.25, s32[]{:T(128)S(6)} %select_n.33), kind=kLoop, calls=%fused_computation.1 | loop fusion | bytes 1769476 | tf_op jit(solution)/shard_map/dynamic_slice | solution.py:777
  19.5 3.2 %collective-permute-start = (bf16[3,384,384]{2,1,0:T(8,128)(2,1)}, bf16[3,384,384]{2,1,0:T(8,128)(2,1)S(1)}, u32[]{:S(2)}, u32[]{:S(2)}) collective-permute-start(bf16[3,384,384]{2,1,0:T(8,128)(2,1)} %constant_dynamic-slice_fusion), channel_id=1, source_target_pairs={{16,17},{17,16},{18,19},{19,18},{20,21},{21,20},{22,23},{23,22},{2... | collective-permute-start | bytes 2654216 | tf_op jit(solution)/shard_map/ppermute | solution.py:667
  22.9 15.5 %collective-permute-done.refs_3_ = bf16[3,384,384]{2,1,0:T(8,128)(2,1)S(1)} collective-permute-done((bf16[3,384,384]{2,1,0:T(8,128)(2,1)}, bf16[3,384,384]{2,1,0:T(8,128)(2,1)S(1)}, u32[]{:S(2)}, u32[]{:S(2)}) %collective-permute-start) | collective-permute-done | bytes 884768 | tf_op jit(solution)/shard_map/ppermute | solution.py:667
  39.1 9.0 %all_to_all.30.refs_4_ = bf16[8,24,384]{2,1,0:T(8,128)(2,1)S(1)} all-to-all(bf16[8,24,384]{2,1,0:T(8,128)(2,1)} %get-tuple-element.39), channel_id=1, replica_groups={{0,1,2,3,4,5,6,7},{8,9,10,11,12,13,14,15},{16,17,18,19,24,25,26,27},{20..., dimensions={0} | all-to-all | bytes 294912 | tf_op jit(solution)/shard_map/all_to_all | solution.py:675
  48.6 1.3 %collective-permute-start.1 = (bf16[96,384]{1,0:T(8,128)(2,1)S(1)}, bf16[96,384]{1,0:T(8,128)(2,1)S(1)}, u32[]{:S(2)}, u32[]{:S(2)}) collective-permute-start(bf16[96,384]{1,0:T(8,128)(2,1)S(1)} %shard_map.108.made), channel_id=1, source_target_pairs={{0,25},{1,24},{2,27},{3,26},{4,29},{5,28},{6,31},{7,30},{8,17},{9,... | collective-permute-start | bytes 221192 | tf_op jit(solution)/shard_map/ppermute | solution.py:667
  49.9 1.3 %collective-permute-start.2 = (bf16[96,384]{1,0:T(8,128)(2,1)S(1)}, bf16[96,384]{1,0:T(8,128)(2,1)S(1)}, u32[]{:S(2)}, u32[]{:S(2)}) collective-permute-start(bf16[96,384]{1,0:T(8,128)(2,1)S(1)} %shard_map.108.made), channel_id=1, source_target_pairs={{0,17},{1,16},{2,19},{3,18},{4,21},{5,20},{6,23},{7,22},{8,25},{9,... | collective-permute-start | bytes 221192 | tf_op jit(solution)/shard_map/ppermute | solution.py:667
  51.2 1.3 %collective-permute-start.3 = (bf16[96,384]{1,0:T(8,128)(2,1)S(1)}, bf16[96,384]{1,0:T(8,128)(2,1)S(1)}, u32[]{:S(2)}, u32[]{:S(2)}) collective-permute-start(bf16[96,384]{1,0:T(8,128)(2,1)S(1)} %shard_map.108.made), channel_id=1, source_target_pairs={{0,24},{1,25},{2,26},{3,27},{4,28},{5,29},{6,30},{7,31},{8,16},{9,... | collective-permute-start | bytes 221192 | tf_op jit(solution)/shard_map/ppermute | solution.py:667
  52.5 1.3 %collective-permute-start.4 = (bf16[96,384]{1,0:T(8,128)(2,1)S(1)}, bf16[96,384]{1,0:T(8,128)(2,1)S(1)}, u32[]{:S(2)}, u32[]{:S(2)}) collective-permute-start(bf16[96,384]{1,0:T(8,128)(2,1)S(1)} %shard_map.108.made), channel_id=1, source_target_pairs={{0,16},{1,17},{2,18},{3,19},{4,20},{5,21},{6,22},{7,23},{8,24},{9,... | collective-permute-start | bytes 221192 | tf_op jit(solution)/shard_map/ppermute | solution.py:667
  53.8 1.2 %shard_map.109.refs_2_ = bf16[3,384,384]{2,1,0:T(8,128)(2,1)S(1)} custom-call(bf16[3,384,768]{2,1,0:T(8,128)(2,1)} %bitcast.26), custom_call_target="tpu_custom_call" | custom-call | bytes 3538944 | tf_op jit(solution)/shard_map/pallas_call | solution.py:620
  55.0 0.7 collective-permute-done.1.refs_4_
  55.7 0.7 collective-permute-done.2.refs_5_
  56.4 2.2 %collective-permute-done.3.refs_6_.across = bf16[96,384]{1,0:T(8,128)(2,1)S(1)} collective-permute-done((bf16[96,384]{1,0:T(8,128)(2,1)S(1)}, bf16[96,384]{1,0:T(8,128)(2,1)S(1)}, u32[]{:S(2)}, u32[]{:S(2)}) %collective-permute-start.3) | collective-permute-done | bytes 73760 | tf_op jit(solution)/shard_map/ppermute | solution.py:667
  58.7 2.2 %shard_map.110 = bf16[4,136,384]{2,1,0:T(8,128)(2,1)} custom-call(s32[5]{0:T(128)S(1)} %pad_add_fusion.refs_0_.sizes, bf16[6,768]{1,0:T(8,128)(2,1)S(1)} %bitcast.19, bf16[3,384,384]{2,1,0:T(8,128)(2,1)S(1)} %shard_map.109.refs_2_, bf16[3,384,384]{2,1,0:T(8,128)(2,1)S(1)} %collective-permute-done.refs_3_, ...), custom_call_target="tpu_custom_call" | custom-call | tf_op jit(solution)/shard_map/pallas_call | solution.py:620
  60.9 3.5 %all-to-all-start.3 = ((bf16[4,136,384]{2,1,0:T(8,128)(2,1)}), bf16[4,136,384]{2,1,0:T(8,128)(2,1)S(1)}, u32[]{:S(2)}, u32[]{:S(2)}) async-start(bf16[4,136,384]{2,1,0:T(8,128)(2,1)} %shard_map.110), calls=%async_computation.3 | async-start | bytes 835584 | tf_op jit(solution)/shard_map/all_to_all | solution.py:675
  64.4 0.7 collective-permute-start.5
  65.1 7.3 %all-to-all-done.3.refs_3_ = bf16[4,136,384]{2,1,0:T(8,128)(2,1)S(1)} async-done(((bf16[4,136,384]{2,1,0:T(8,128)(2,1)}), bf16[4,136,384]{2,1,0:T(8,128)(2,1)S(1)}, u32[]{:S(2)}, u32[]{:S(2)}) %all-to-all-start.3) | async-done | bytes 417824 | tf_op jit(solution)/shard_map/all_to_all | solution.py:675
  72.3 3.1 %shard_map.111 = (bf16[8,24,384]{2,1,0:T(8,128)(2,1)}, bf16[128,384]{1,0:T(8,128)(2,1)}, bf16[128,384]{1,0:T(8,128)(2,1)S(1)}) custom-call(s32[5]{0:T(128)S(1)} %pad_add_fusion.refs_0_.sizes, f32[2,64]{1,0:T(2,128)S(1)} %bitcast.22, bf16[2,128,192]{2,1,0:T(8,128)(2,1)S(1)} %constant_dynamic-slice_fusion.1.refs_2_, ...), custom_call_target="tpu_custom_call" | custom-call | tf_op jit(solution)/shard_map/pallas_call | solution.py:620
  75.4 3.4 %all-to-all-start.4 = ((bf16[8,24,384]{2,1,0:T(8,128)(2,1)}), bf16[8,24,384]{2,1,0:T(8,128)(2,1)S(1)}, u32[]{:S(2)}, u32[]{:S(2)}) async-start(bf16[8,24,384]{2,1,0:T(8,128)(2,1)} %get-tuple-element.47), calls=%async_computation.4 | async-start | bytes 294912 | tf_op jit(solution)/shard_map/all_to_all | solution.py:675
  78.8 3.3 %collective-permute-start.6 = (bf16[128,384]{1,0:T(8,128)(2,1)}, bf16[128,384]{1,0:T(8,128)(2,1)S(1)}, u32[]{:S(2)}, u32[]{:S(2)}) collective-permute-start(bf16[128,384]{1,0:T(8,128)(2,1)} %get-tuple-element.48), channel_id=1, source_target_pairs={{16,17},{17,16},{18,19},{19,18},{20,21},{21,20},{22,23},{23,22},{2... | collective-permute-start | bytes 294920 | tf_op jit(solution)/shard_map/ppermute | solution.py:667
  82.1 2.3 %collective-permute-done.6.last_side = bf16[128,384]{1,0:T(8,128)(2,1)S(1)} collective-permute-done((bf16[128,384]{1,0:T(8,128)(2,1)}, bf16[128,384]{1,0:T(8,128)(2,1)S(1)}, u32[]{:S(2)}, u32[]{:S(2)}) %collective-permute-start.6) | collective-permute-done | bytes 98336 | tf_op jit(solution)/shard_map/ppermute | solution.py:667
  84.4 0.6 all-to-all-done.4.arrived
  85.1 1.8 %shard_map.112 = (bf16[16,16,384]{2,1,0:T(8,128)(2,1)}, bf16[2,128,384]{2,1,0:T(8,128)(2,1)}, bf16[2,128,384]{2,1,0:T(8,128)(2,1)S(1)}) custom-call(s32[5]{0:T(128)S(1)} %pad_add_fusion.refs_0_.sizes, bf16[6,768]{1,0:T(8,128)(2,1)S(1)} %bitcast.20, bf16[384,768]{1,0:T(8,128)(2,1)S(1)} %bitcast.16, bf16[96,384]{1,0:T(8,128)(2,1)S(1)} %shard_map.108.made, ...), custom_call_target="tpu_custom_call" | custom-call | tf_op jit(solution)/shard_map/pallas_call | solution.py:620
  86.9 4.8 %all-to-all-start.5 = ((bf16[16,16,384]{2,1,0:T(8,128)(2,1)}), bf16[16,16,384]{2,1,0:T(8,128)(2,1)S(1)}, u32[]{:S(2)}, u32[]{:S(2)}) async-start(bf16[16,16,384]{2,1,0:T(8,128)(2,1)} %get-tuple-element.51), calls=%async_computation.5 | async-start | bytes 393216 | tf_op jit(solution)/shard_map/all_to_all | solution.py:698
  91.7 1.4 %collective-permute-start.7 = (bf16[2,128,384]{2,1,0:T(8,128)(2,1)}, bf16[2,128,384]{2,1,0:T(8,128)(2,1)S(1)}, u32[]{:S(2)}, u32[]{:S(2)}) collective-permute-start(bf16[2,128,384]{2,1,0:T(8,128)(2,1)} %get-tuple-element.53), channel_id=1, source_target_pairs={{0,2},{1,3},{2,0},{3,1},{4,6},{5,7},{6,4},{7,5},{8,10},{9,11},{10,... | collective-permute-start | bytes 589832 | tf_op jit(solution)/shard_map/ppermute | solution.py:869
  93.1 4.8 %collective-permute-done.7.other = bf16[2,128,384]{2,1,0:T(8,128)(2,1)S(1)} collective-permute-done((bf16[2,128,384]{2,1,0:T(8,128)(2,1)}, bf16[2,128,384]{2,1,0:T(8,128)(2,1)S(1)}, u32[]{:S(2)}, u32[]{:S(2)}) %collective-permute-start.7) | collective-permute-done | bytes 196640 | tf_op jit(solution)/shard_map/ppermute | solution.py:869
  97.9 0.7 all-to-all-done.5.arrived
  98.6 1.0 shard_map.113
  (20 shorter events, 2.1 us)
Async XLA Ops:
  0.6 22.1 %copy-start = (bf16[1,2,4,32,768]{4,3,2,1,0:T(8,128)(2,1)S(1)}, bf16[1,2,4,32,768]{4,3,2,1,0:T(8,128)(2,1)}, u32[]{:S(2)}) copy-start(bf16[1,2,4,32,768]{4,3,2,1,0:T(8,128)(2,1)} %param.17) | copy-start | bytes 1179652
  0.6 9.6 %copy-start.4 = (s32[4]{0:T(128)S(1)}, s32[4]{0:T(128)}, u32[]{:S(2)}) copy-start(s32[4]{0:T(128)} %param.10) | copy-start | bytes 52
  2.6 10.4 %all-to-all-start = ((bf16[8,16,512]{2,1,0:T(8,128)(2,1)}), bf16[8,16,512]{2,1,0:T(8,128)(2,1)S(1)}, u32[]{:S(2)}, u32[]{:S(2)}) async-start(bf16[8,16,512]{2,1,0:T(8,128)(2,1)} %shard_map.104), calls=%async_computation | async-start | bytes 262144 | tf_op jit(solution)/shard_map/all_to_all | solution.py:675
  13.6 24.8 %copy-start.2 = (f32[1,2,64]{2,1,0:T(2,128)S(1)}, f32[1,2,64]{2,1,0:T(2,128)}, u32[]{:S(2)}) copy-start(f32[1,2,64]{2,1,0:T(2,128)} %param.16) | copy-start | bytes 1540
  13.6 24.8 %all-to-all-start.1 = ((bf16[8,120,384]{2,1,0:T(8,128)(2,1)}), bf16[8,120,384]{2,1,0:T(8,128)(2,1)S(1)}, u32[]{:S(2)}, u32[]{:S(2)}) async-start(bf16[8,120,384]{2,1,0:T(8,128)(2,1)} %get-tuple-element.36), calls=%async_computation.1 | async-start | bytes 1474560 | tf_op jit(solution)/shard_map/all_to_all | solution.py:675
  17.2 30.8 %copy-start.1 = (bf16[1,384,768]{2,1,0:T(8,128)(2,1)S(1)}, bf16[1,384,768]{2,1,0:T(8,128)(2,1)}, u32[]{:S(2)}) copy-start(bf16[1,384,768]{2,1,0:T(8,128)(2,1)} %param.15) | copy-start | bytes 1769476
  19.5 18.9 %collective-permute-start = (bf16[3,384,384]{2,1,0:T(8,128)(2,1)}, bf16[3,384,384]{2,1,0:T(8,128)(2,1)S(1)}, u32[]{:S(2)}, u32[]{:S(2)}) collective-permute-start(bf16[3,384,384]{2,1,0:T(8,128)(2,1)} %constant_dynamic-slice_fusion), channel_id=1, source_target_pairs={{16,17},{17,16},{18,19},{19,18},{20,21},{21,20},{22,23},{23,22},{2... | collective-permute-start | bytes 2654216 | tf_op jit(solution)/shard_map/ppermute | solution.py:667
  48.6 7.1 %collective-permute-start.1 = (bf16[96,384]{1,0:T(8,128)(2,1)S(1)}, bf16[96,384]{1,0:T(8,128)(2,1)S(1)}, u32[]{:S(2)}, u32[]{:S(2)}) collective-permute-start(bf16[96,384]{1,0:T(8,128)(2,1)S(1)} %shard_map.108.made), channel_id=1, source_target_pairs={{0,25},{1,24},{2,27},{3,26},{4,29},{5,28},{6,31},{7,30},{8,17},{9,... | collective-permute-start | bytes 221192 | tf_op jit(solution)/shard_map/ppermute | solution.py:667
  49.9 6.5 %collective-permute-start.2 = (bf16[96,384]{1,0:T(8,128)(2,1)S(1)}, bf16[96,384]{1,0:T(8,128)(2,1)S(1)}, u32[]{:S(2)}, u32[]{:S(2)}) collective-permute-start(bf16[96,384]{1,0:T(8,128)(2,1)S(1)} %shard_map.108.made), channel_id=1, source_target_pairs={{0,17},{1,16},{2,19},{3,18},{4,21},{5,20},{6,23},{7,22},{8,25},{9,... | collective-permute-start | bytes 221192 | tf_op jit(solution)/shard_map/ppermute | solution.py:667
  51.2 7.4 %collective-permute-start.3 = (bf16[96,384]{1,0:T(8,128)(2,1)S(1)}, bf16[96,384]{1,0:T(8,128)(2,1)S(1)}, u32[]{:S(2)}, u32[]{:S(2)}) collective-permute-start(bf16[96,384]{1,0:T(8,128)(2,1)S(1)} %shard_map.108.made), channel_id=1, source_target_pairs={{0,24},{1,25},{2,26},{3,27},{4,28},{5,29},{6,30},{7,31},{8,16},{9,... | collective-permute-start | bytes 221192 | tf_op jit(solution)/shard_map/ppermute | solution.py:667
  52.5 6.1 %collective-permute-start.4 = (bf16[96,384]{1,0:T(8,128)(2,1)S(1)}, bf16[96,384]{1,0:T(8,128)(2,1)S(1)}, u32[]{:S(2)}, u32[]{:S(2)}) collective-permute-start(bf16[96,384]{1,0:T(8,128)(2,1)S(1)} %shard_map.108.made), channel_id=1, source_target_pairs={{0,16},{1,17},{2,18},{3,19},{4,20},{5,21},{6,22},{7,23},{8,24},{9,... | collective-permute-start | bytes 221192 | tf_op jit(solution)/shard_map/ppermute | solution.py:667
  55.0 9.4 %copy-start.3 = (bf16[128,384]{1,0:T(8,128)(2,1)S(1)}, bf16[128,384]{1,0:T(8,128)(2,1)}, u32[]{:S(2)}) copy-start(bf16[128,384]{1,0:T(8,128)(2,1)} %get-tuple-element.42.first_cache) | copy-start | bytes 294916
  60.9 11.4 %all-to-all-start.3 = ((bf16[4,136,384]{2,1,0:T(8,128)(2,1)}), bf16[4,136,384]{2,1,0:T(8,128)(2,1)S(1)}, u32[]{:S(2)}, u32[]{:S(2)}) async-start(bf16[4,136,384]{2,1,0:T(8,128)(2,1)} %shard_map.110), calls=%async_computation.3 | async-start | bytes 835584 | tf_op jit(solution)/shard_map/all_to_all | solution.py:675
  64.4 0.7 collective-permute-start.5
  75.4 9.6 %all-to-all-start.4 = ((bf16[8,24,384]{2,1,0:T(8,128)(2,1)}), bf16[8,24,384]{2,1,0:T(8,128)(2,1)S(1)}, u32[]{:S(2)}, u32[]{:S(2)}) async-start(bf16[8,24,384]{2,1,0:T(8,128)(2,1)} %get-tuple-element.47), calls=%async_computation.4 | async-start | bytes 294912 | tf_op jit(solution)/shard_map/all_to_all | solution.py:675
  78.8 5.6 %collective-permute-start.6 = (bf16[128,384]{1,0:T(8,128)(2,1)}, bf16[128,384]{1,0:T(8,128)(2,1)S(1)}, u32[]{:S(2)}, u32[]{:S(2)}) collective-permute-start(bf16[128,384]{1,0:T(8,128)(2,1)} %get-tuple-element.48), channel_id=1, source_target_pairs={{16,17},{17,16},{18,19},{19,18},{20,21},{21,20},{22,23},{23,22},{2... | collective-permute-start | bytes 294920 | tf_op jit(solution)/shard_map/ppermute | solution.py:667
  86.9 11.7 %all-to-all-start.5 = ((bf16[16,16,384]{2,1,0:T(8,128)(2,1)}), bf16[16,16,384]{2,1,0:T(8,128)(2,1)S(1)}, u32[]{:S(2)}, u32[]{:S(2)}) async-start(bf16[16,16,384]{2,1,0:T(8,128)(2,1)} %get-tuple-element.51), calls=%async_computation.5 | async-start | bytes 393216 | tf_op jit(solution)/shard_map/all_to_all | solution.py:698
  91.7 6.2 %collective-permute-start.7 = (bf16[2,128,384]{2,1,0:T(8,128)(2,1)}, bf16[2,128,384]{2,1,0:T(8,128)(2,1)S(1)}, u32[]{:S(2)}, u32[]{:S(2)}) collective-permute-start(bf16[2,128,384]{2,1,0:T(8,128)(2,1)} %get-tuple-element.53), channel_id=1, source_target_pairs={{0,2},{1,3},{2,0},{3,1},{4,6},{5,7},{6,4},{7,5},{8,10},{9,11},{10,... | collective-permute-start | bytes 589832 | tf_op jit(solution)/shard_map/ppermute | solution.py:869
